TPU v7x, 32 devices: a whole 2x2x4 slice. The times are simulated.
32 devices in a mesh: dp: 8 (over y, x, core), mp: 4 (over z).
Axes of the slice: x: 2, y: 2, z: 4, core: 2. Of those that a mesh axis runs over, the one named last changes fastest.
Arguments:
- tokens: bfloat16 [16384, 2048], P('dp'), may hold values from -6 to 6
- cotangent: bfloat16 [16384, 2048], P('dp'), may hold values from -6 to 6
- seq_len: int32 [32], replicated, may hold values from 0 to 2048, as said below
- seq_device: int32 [32], replicated, may hold values from 0 to 7, as said below
- owner_map: int32 [192], replicated, may hold values from 0 to 191, as said below
- weight_blocks: float32 [4, 192, 256, 256], P('mp', 'dp')
- left_stat: float32 [4, 192, 256, 256], P('mp', 'dp'), as said below
- right_stat: float32 [4, 192, 256, 256], P('mp', 'dp'), as said below
- left_root: float32 [4, 192, 256, 256], P('mp', 'dp'), as said below
- right_root: float32 [4, 192, 256, 256], P('mp', 'dp'), as said below
- vectors: float32 [6, 2048], replicated
- vector_stat: float32 [6, 2048], replicated, as said below
- unit_bias: float32 [4, 3584], P('mp'), may hold values from -1.5 to 1.5
- unit_stat: float32 [4, 3584], P('mp'), as said below
Outputs:
- block_out: bfloat16 [16384, 2048], P('dp')
- input_grad: bfloat16 [16384, 2048], P('dp')
- block_grad: float32 [4, 192, 256, 256], P('mp', 'dp')
- left_new: float32 [4, 192, 256, 256], P('mp', 'dp')
- right_new: float32 [4, 192, 256, 256], P('mp', 'dp')
- weight_new: float32 [4, 192, 256, 256], P('mp', 'dp')
- vector_grad: float32 [6, 2048], replicated
- vector_stat_new: float32 [6, 2048], replicated
- vector_new: float32 [6, 2048], replicated
- unit_grad: float32 [4, 3584], P('mp')
- unit_stat_new: float32 [4, 3584], P('mp')
- unit_new: float32 [4, 3584], P('mp')
Inputs may be any that keep to these rules, and one draw needn't show every extreme that they name: `seq_len`: the lengths of the sequences of one dp index sum to 2048 or less; one index holds a single sequence of exactly 2048. `seq_device`: each dp index is named by exactly 4 sequences. `owner_map`: a permutation; slot s lies on dp index s // 24. `left_stat`: symmetric. `right_stat`: symmetric. `left_root`: symmetric. `right_root`: symmetric. `vector_stat`: every entry is positive. `unit_stat`: every entry is positive.
All inputs are finite; a program needn't handle non-finite values.
Results may differ from a plain program's by a relative error of at most 0.012.
Values may be sent and summed in bfloat16 or wider, within the bound.
A program may use at most 384 MiB of HBM per device.

v0:
```python
import math

import jax
import jax.numpy as jnp
from jax import lax
from jax.sharding import PartitionSpec as P

D = 2048
HEADS = 8
HD = 256
ROT = 64
FF = 8192
B = 256


highest = lax.Precision.HIGHEST
norm_eps = 1e-05
step_share = 0.5
vector_rate = 0.15
masked_score = -1e30


def layer_norm(values, gain, shift):
    center = values - jnp.mean(values, axis=-1, keepdims=True)
    spread = jnp.mean(center * center, axis=-1, keepdims=True)
    return center * lax.rsqrt(spread + norm_eps) * gain + shift


def gelu_exact(values):
    return jax.nn.gelu(values, approximate=False)


def segment_layout(seq_len, seq_device, device, row_count):
    is_mine = seq_device == device
    lengths = jnp.where(is_mine, seq_len, 0)
    seq_ends = jnp.cumsum(lengths)
    row_index = jnp.arange(row_count, dtype=jnp.int32)
    passed = is_mine[None, :] & (seq_ends[None, :] <= row_index[:, None])
    segment = jnp.sum(passed.astype(jnp.int32), axis=1)
    seq_start = jnp.max(jnp.where(passed, seq_ends[None, :], 0), axis=1)
    return (segment, row_index - seq_start)


def rotary_tables(position):
    half_rot = ROT // 2
    frequency = 10000.0 ** (-2.0 * jnp.arange(half_rot, dtype=jnp.float32) / ROT)
    angles = position.astype(jnp.float32)[:, None] * frequency[None, :]
    cosine_table = jnp.concatenate([jnp.cos(angles), jnp.cos(angles)], axis=1)
    sine_table = jnp.concatenate([jnp.sin(angles), jnp.sin(angles)], axis=1)
    return (cosine_table, sine_table)


def rotate(values, cosine_table, sine_table):
    rot_dims = cosine_table.shape[1]
    half_rot = rot_dims // 2
    leading = values[..., :rot_dims]
    turned = jnp.concatenate([-leading[..., half_rot:], leading[..., :half_rot]], axis=-1)
    rotated = leading * cosine_table[:, None, :] + turned * sine_table[:, None, :]
    return jnp.concatenate([rotated, values[..., rot_dims:]], axis=-1)


def blocks_to_matrix(blocks, across):
    down_count = blocks.shape[0] // across
    return (
        blocks.reshape(down_count, across, B, B)
        .transpose(0, 2, 1, 3)
        .reshape(down_count * B, across * B)
    )


def matrix_to_blocks(matrix):
    down_count = matrix.shape[0] // B
    across = matrix.shape[1] // B
    return (
        matrix.reshape(down_count, B, across, B)
        .transpose(0, 2, 1, 3)
        .reshape(down_count * across, B, B)
    )


def split_blocks(blocks, qkv_cols, head_cols, unit_cols):
    qkv_end = D // B * (qkv_cols // B)
    out_end = qkv_end + head_cols // B * (D // B)
    up_end = out_end + D // B * (unit_cols // B)
    qkv_w = blocks_to_matrix(blocks[:qkv_end], qkv_cols // B)
    out_w = blocks_to_matrix(blocks[qkv_end:out_end], D // B)
    up_w = blocks_to_matrix(blocks[out_end:up_end], unit_cols // B)
    down_w = blocks_to_matrix(blocks[up_end:], D // B)
    return (qkv_w, out_w, up_w, down_w)


def apply_step(weight, direction):
    weight_size = jnp.sqrt(jnp.mean(weight * weight, axis=(-2, -1), keepdims=True))
    step_size = jnp.sqrt(jnp.mean(direction * direction, axis=(-2, -1), keepdims=True) + 1e-06)
    return weight - step_share * weight_size * direction / step_size


def vector_update(values, old_stat, gradient):
    new_stat = 0.5 * old_stat + 0.5 * gradient * gradient
    return (new_stat, values - vector_rate * gradient * lax.rsqrt(new_stat))


def block_mask(block_segment, block_row, segment, column):
    return (block_segment[:, None] == segment[None, :]) & (column[None, :] <= block_row[:, None])


def attention_forward(queries, keys_low, values_low, segment):
    row_count, head_count, head_dim = queries.shape
    block_rows = min(512, row_count)
    block_count = row_count // block_rows
    score_scale = 1.0 / math.sqrt(head_dim)
    column = jnp.arange(row_count, dtype=jnp.int32)

    def one_block(inputs):
        block_query, block_segment, block_row = inputs
        scores = (
            jnp.einsum("qhd,khd->hqk", block_query, keys_low, preferred_element_type=jnp.float32)
            * score_scale
        )
        scores = jnp.where(
            block_mask(block_segment, block_row, segment, column)[None], scores, masked_score
        )
        log_total = jax.nn.logsumexp(scores, axis=-1)
        weights = jnp.exp(scores - log_total[:, :, None]).astype(jnp.bfloat16)
        context = jnp.einsum(
            "hqk,khd->qhd", weights, values_low, preferred_element_type=jnp.float32
        )
        return (context, log_total)

    contexts, log_totals = lax.map(
        one_block,
        (
            queries.reshape(block_count, block_rows, head_count, head_dim),
            segment.reshape(block_count, block_rows),
            column.reshape(block_count, block_rows),
        ),
    )
    return (contexts.reshape(row_count, head_count, head_dim), log_totals)


def attention_backward(queries, keys_low, values_low, context_grad, log_totals, segment):
    row_count, head_count, head_dim = queries.shape
    block_rows = min(512, row_count)
    block_count = row_count // block_rows
    score_scale = 1.0 / math.sqrt(head_dim)
    column = jnp.arange(row_count, dtype=jnp.int32)

    def one_block(totals, inputs):
        key_grad, value_grad = totals
        block_query, block_grad, block_total, block_segment, block_row = inputs
        scores = (
            jnp.einsum("qhd,khd->hqk", block_query, keys_low, preferred_element_type=jnp.float32)
            * score_scale
        )
        scores = jnp.where(
            block_mask(block_segment, block_row, segment, column)[None], scores, masked_score
        )
        probs = jnp.exp(scores - block_total[:, :, None])
        weights = probs.astype(jnp.bfloat16)
        prob_grad = jnp.einsum(
            "qhd,khd->hqk", block_grad, values_low, preferred_element_type=jnp.float32
        )
        delta = jnp.sum(probs * prob_grad, axis=-1, keepdims=True)
        score_grad = (probs * (prob_grad - delta)).astype(jnp.bfloat16)
        query_grad = (
            jnp.einsum("hqk,khd->qhd", score_grad, keys_low, preferred_element_type=jnp.float32)
            * score_scale
        )
        key_grad = (
            key_grad
            + jnp.einsum(
                "hqk,qhd->khd", score_grad, block_query, preferred_element_type=jnp.float32
            )
            * score_scale
        )
        value_grad = value_grad + jnp.einsum(
            "hqk,qhd->khd", weights, block_grad, preferred_element_type=jnp.float32
        )
        return ((key_grad, value_grad), query_grad)

    zeros_start = jnp.zeros((row_count, head_count, head_dim), jnp.float32)
    (key_grad, value_grad), query_grad = lax.scan(
        one_block,
        (zeros_start, zeros_start),
        (
            queries.reshape(block_count, block_rows, head_count, head_dim),
            context_grad.reshape(block_count, block_rows, head_count, head_dim),
            log_totals,
            segment.reshape(block_count, block_rows),
            column.reshape(block_count, block_rows),
        ),
    )
    return (query_grad.reshape(row_count, head_count, head_dim), key_grad, value_grad)


def per_device(
    tokens,
    cotangent,
    seq_len,
    seq_device,
    owner_map,
    weight_blocks,
    left_stat,
    right_stat,
    left_root,
    right_root,
    vectors,
    vector_stat,
    unit_bias,
    unit_stat,
):
    groups = lax.axis_size("mp")
    device = lax.axis_index("dp")
    row_count = tokens.shape[0]
    heads_here = HEADS // groups
    qkv_cols = 3 * D // groups
    head_cols = D // groups
    unit_cols = FF // groups
    slot_count = weight_blocks.shape[1]
    sent_blocks = weight_blocks[0].astype(jnp.bfloat16)
    gathered = lax.all_gather(sent_blocks, "dp", axis=0, tiled=True)
    qkv_w, out_w, up_w, down_w = split_blocks(gathered[owner_map], qkv_cols, head_cols, unit_cols)
    segment, position = segment_layout(seq_len, seq_device, device, row_count)
    cosine_table, sine_table = rotary_tables(position)
    unit_shift = unit_bias[0]
    inputs = tokens.astype(jnp.float32)
    normed_one = layer_norm(inputs, vectors[0], vectors[1]).astype(jnp.bfloat16)
    normed_two = layer_norm(inputs, vectors[2], vectors[3]).astype(jnp.bfloat16)
    qkv_proj = (
        jnp.dot(normed_one, qkv_w, preferred_element_type=jnp.float32) + unit_shift[:qkv_cols]
    )
    qkv_proj = qkv_proj.reshape(row_count, heads_here, 3, HD)

    def turn_pair(values):
        return rotate(values.reshape(row_count, 2 * heads_here, HD), cosine_table, sine_table)

    turned, turn_back = jax.vjp(turn_pair, qkv_proj[:, :, :2])
    turned = turned.reshape(row_count, heads_here, 2, HD).astype(jnp.bfloat16)
    queries = turned[:, :, 0]
    keys_low = turned[:, :, 1]
    values_low = qkv_proj[:, :, 2].astype(jnp.bfloat16)
    context, log_totals = attention_forward(queries, keys_low, values_low, segment)
    context_low = context.reshape(row_count, head_cols).astype(jnp.bfloat16)
    hidden = jnp.dot(normed_two, up_w, preferred_element_type=jnp.float32) + unit_shift[qkv_cols:]
    active, gelu_back = jax.vjp(gelu_exact, hidden)
    active_low = active.astype(jnp.bfloat16)
    partial_out = jnp.dot(context_low, out_w, preferred_element_type=jnp.float32) + jnp.dot(
        active_low, down_w, preferred_element_type=jnp.float32
    )
    branch = lax.psum(partial_out.astype(jnp.bfloat16), "mp").astype(jnp.float32)
    block_out = (inputs + branch + (vectors[4] + vectors[5])).astype(jnp.bfloat16)
    grad_full = cotangent.astype(jnp.float32)
    act_grad = jnp.einsum("td,fd->tf", cotangent, down_w, preferred_element_type=jnp.float32)
    hidden_grad = gelu_back(act_grad)[0].astype(jnp.bfloat16)
    context_grad = jnp.einsum(
        "td,id->ti", cotangent, out_w, preferred_element_type=jnp.float32
    ).astype(jnp.bfloat16)
    query_grad, key_grad, value_grad = attention_backward(
        queries,
        keys_low,
        values_low,
        context_grad.reshape(row_count, heads_here, HD),
        log_totals,
        segment,
    )
    pair_grad = turn_back(
        jnp.stack([query_grad, key_grad], axis=2).reshape(row_count, 2 * heads_here, HD)
    )[0]
    qkv_grad = (
        jnp.concatenate([pair_grad, value_grad[:, :, None]], axis=2)
        .reshape(row_count, qkv_cols)
        .astype(jnp.bfloat16)
    )
    one_grad = jnp.einsum("te,de->td", qkv_grad, qkv_w, preferred_element_type=jnp.float32)
    two_grad = jnp.einsum("tf,df->td", hidden_grad, up_w, preferred_element_type=jnp.float32)
    norm_back_one = jax.vjp(layer_norm, inputs, vectors[0], vectors[1])[1]
    norm_back_two = jax.vjp(layer_norm, inputs, vectors[2], vectors[3])[1]
    input_one, gain_one, shift_one = norm_back_one(one_grad)
    input_two, gain_two, shift_two = norm_back_two(two_grad)
    input_part = input_one + input_two
    norm_part = jnp.stack([gain_one, shift_one, gain_two, shift_two])
    input_sum, norm_sum = lax.psum((input_part, norm_part), "mp")
    input_grad = (grad_full + input_sum).astype(jnp.bfloat16)
    qkv_w_grad = jnp.einsum("td,te->de", normed_one, qkv_grad, preferred_element_type=jnp.float32)
    out_w_grad = jnp.einsum("ti,td->id", context_low, cotangent, preferred_element_type=jnp.float32)
    up_w_grad = jnp.einsum("td,tf->df", normed_two, hidden_grad, preferred_element_type=jnp.float32)
    down_w_grad = jnp.einsum("tf,td->fd", active_low, cotangent, preferred_element_type=jnp.float32)
    canonical_grad = jnp.concatenate(
        [matrix_to_blocks(matrix) for matrix in (qkv_w_grad, out_w_grad, up_w_grad, down_w_grad)],
        axis=0,
    )
    slot_grads = canonical_grad[jnp.argsort(owner_map)]
    out_sum = jnp.sum(grad_full, axis=0)
    vector_part = jnp.concatenate([norm_sum, jnp.stack([out_sum, out_sum])], axis=0)
    unit_part = jnp.concatenate(
        [
            jnp.sum(qkv_grad.astype(jnp.float32), axis=0),
            jnp.sum(hidden_grad.astype(jnp.float32), axis=0),
        ]
    )
    summed, vector_grad, unit_grad = lax.psum((slot_grads, vector_part, unit_part), "dp")
    owned = lax.dynamic_slice_in_dim(summed, device * slot_count, slot_count, 0)
    left_new = 0.5 * left_stat[0] + 0.5 * jnp.einsum(
        "nij,nkj->nik", owned, owned, precision=highest
    )
    right_new = 0.5 * right_stat[0] + 0.5 * jnp.einsum(
        "nji,njk->nik", owned, owned, precision=highest
    )
    direction = jnp.einsum("nij,njk->nik", left_root[0], owned, precision=highest)
    direction = jnp.einsum("nij,njk->nik", direction, right_root[0], precision=highest)
    weight_new = apply_step(weight_blocks[0], direction)
    vector_stat_new, vector_new = vector_update(vectors, vector_stat, vector_grad)
    unit_stat_new, unit_new = vector_update(unit_shift, unit_stat[0], unit_grad)
    return (
        block_out,
        input_grad,
        owned[None],
        left_new[None],
        right_new[None],
        weight_new[None],
        vector_grad,
        vector_stat_new,
        vector_new,
        unit_grad[None],
        unit_stat_new[None],
        unit_new[None],
    )


def solution(mesh):
    placed = (
        P("dp", None),
        P("dp", None),
        P(),
        P(),
        P(),
        P("mp", "dp", None, None),
        P("mp", "dp", None, None),
        P("mp", "dp", None, None),
        P("mp", "dp", None, None),
        P("mp", "dp", None, None),
        P(),
        P(),
        P("mp", None),
        P("mp", None),
    )
    return jax.shard_map(
        per_device,
        mesh=mesh,
        in_specs=placed,
        out_specs=(
            P("dp", None),
            P("dp", None),
            P("mp", "dp", None, None),
            P("mp", "dp", None, None),
            P("mp", "dp", None, None),
            P("mp", "dp", None, None),
            P(),
            P(),
            P(),
            P("mp", None),
            P("mp", None),
            P("mp", None),
        ),
        check_vma=False,
    )
```

profile of v0, /device:TPU:0, one launch (start us, length us, event | category | flops | bytes accessed | tf_op | source)
XLA Modules:
  0.0 2202.9 jit_solution(17121372478600683914)
XLA Ops:
  7.3 4.9 bitcast_convert_fusion
  13.5 4.8 convert_reduce_fusion
  26.0 114.4 %all-gather.2.cloned.1.call-done = bf16[192,256,256]{2,1,0:T(8,128)(2,1)} async-done(((bf16[24,256,256]{2,1,0:T(8,128)(2,1)}), bf16[192,256,256]{2,1,0:T(8,128)(2,1)}) %all-gather.2.cloned.1.call-update) | async-done | bytes 25165840 | tf_op jit(solution)/shard_map/all_gather | solution.py:221
  140.4 19.8 gather_fusion
  160.1 6.2 slice.92
  166.3 9.0 copy.88
  175.3 5.5 copy.143
  180.9 18.9 convolution_add_fusion
  208.4 8.8 copy.89
  217.3 8.2 slice_negate_fusion.1
  230.9 6.2 fusion.101
  245.8 42.7 %while.28 = (s32[]{:T(128)}, bf16[4,512,2,256]{3,1,2,0:T(8,128)(2,1)}, f32[4,2,512]{2,1,0:T(2,128)S(1)}, s32[4,512]{1,0:T(4,128)S(1)}, s32[2048]{0:T(1024)S(1)},...) while((s32[]{:T(128)}, ...), condition=%wide.region_8.9_spmd.clone, body=%wide.region_5.8_spmd.clone.sunk | while | flops 2173706240 | bytes 43586696 | solution.py:130
  291.6 9.1 fusion.102
  309.8 111.9 %while.29 = (s32[]{:T(128)}, f32[2048,2,256]{0,2,1:T(8,128)}, f32[2048,2,256]{0,2,1:T(8,128)}, f32[4,512,2,256]{3,1,0,2:T(8,128)}, bf16[4,512,2,256]{3,1,2,0:T(8...) while((s32[]{:T(128)}, f32[2048,2,256]{0,2,1:T(8,128)}, ...), condition=%wide.region_12.13_spmd.clone, body=%wide.region_10.12_spmd.clone.sunk | while | flops 5408816128 | bytes 185649952 | solution.py:182
  322.8 6.0 bitcast_add_fusion.6
  331.1 5.5 bitcast_add_fusion.7
  349.1 7.3 bitcast_add_fusion.6
  358.7 6.2 bitcast_add_fusion.7
  377.5 7.3 bitcast_add_fusion.6
  387.1 6.2 bitcast_add_fusion.7
  405.9 7.3 bitcast_add_fusion.6
  415.4 6.2 bitcast_add_fusion.7
  421.6 5.3 copy.99
  432.5 5.5 split.16
  438.0 11.7 fusion.124
  454.4 4.8 copy.101
  459.2 11.8 copy.94
  471.0 10.5 copy.146
  481.4 12.2 copy.95
  493.6 10.3 copy.147
  504.0 61.4 %multiply_convert_fusion.1 = (bf16[2048,2048]{1,0:T(8,128)(2,1)}, f32[2048,2048]{1,0:T(8,128)}, f32[2048,2048]{1,0:T(8,128)}) fusion(f32[2048]{0:T(1024)S(1)} %bitcast.353, bf16[2048,2048]{1,0:T(8,128)(2,1)} %bitcast.313, bf16[2048,2048]{1,0:T(8,128)(2,1)} %param.18, f32[2048]{0:T(1024)S(1)} %bitcast.355, f32[2048]{0:T(1024)S(1)} %bitcast.336, ...), kind=kOutput, calls=%fused_computation.110 | convolution fusion | flops 17481859072 | bytes 58761216 | tf_op jit(solution)/shard_map/dot_general | solution.py:244
  565.4 33.2 %convert_reduce_fusion.2 = (f32[2048]{0:T(1024)}, bf16[2048,2048]{1,0:T(8,128)(2,1)}) fusion(f32[2048,2048]{1,0:T(8,128)} %get-tuple-element.339, bf16[2048,2048]{1,0:T(8,128)(2,1)} %bitcast.309, bf16[2048,2048]{1,0:T(8,128)(2,1)} %param.19, f32[2048,2048]{1,0:T(8,128)} %get-tuple-element.374, f32[2048]{0:T(1024)S(1)} %bitcast.354), kind=kOutput, calls=%fused_computation.107 | convolution fusion | flops 17251170304 | bytes 58736640 | tf_op jit(solution)/shard_map/td,fd->tf/dot_general | solution.py:253
  598.6 24.5 %fusion.127 = f32[2048,2048]{1,0:T(8,128)} fusion(bf16[2048,2048]{1,0:T(8,128)(2,1)} %get-tuple-element.379, bf16[2048,2048]{1,0:T(8,128)(2,1)} %bitcast.314), kind=kOutput, calls=%fused_computation.215 | convolution fusion | flops 17179869184 | bytes 33554432 | tf_op jit(solution)/shard_map/tf,df->td/dot_general | solution.py:275
  627.6 8.2 fusion.126
  635.8 24.3 %add_convert_fusion = bf16[2048,2048]{1,0:T(8,128)(2,1)} fusion(f32[2048,2048]{1,0:T(8,128)} %fusion.126, bf16[2048,2048]{1,0:T(8,128)(2,1)} %get-tuple-element.338, bf16[2048,2048]{1,0:T(8,128)(2,1)S(1)} %bitcast.312), kind=kOutput, calls=%fused_computation.109 | convolution fusion | flops 17188257792 | bytes 41943040 | tf_op jit(solution)/shard_map/dot_general | solution.py:247
  661.4 6.1 pad_add_fusion.1
  667.5 5.4 pad_add_fusion
  677.0 8.7 copy.102
  685.7 28.7 %fusion.68 = (f32[2048]{0:T(1024)S(1)}, f32[2048]{0:T(1024)S(1)}, f32[2048,2048]{1,0:T(8,128)}) fusion(bf16[2048,2048]{1,0:T(8,128)(2,1)} %param.18, f32[2048]{0:T(1024)S(1)} %bitcast.342, f32[2048]{0:T(1024)S(1)} %copy-done.24, f32[2048,2048]{1,0:T(8,128)} %fusion.127, f32[2048]{0:T(1024)S(1)} %bitcast.337, bf16[2048,1536]{0,1:T(8,128)(2,1)} %bitcast.323, ...), kind=kOutput, calls=%fused_computation.93 | convolution fusion | flops 12918452224 | bytes 54566912 | tf_op jit(solution)/shard_map/te,de->td/dot_general | solution.py:274
  714.5 19.5 fusion.65
  733.9 217.2 %all-reduce.9.cloned.1.call-done = bf16[2048,2048]{1,0:T(8,128)(2,1)} async-done(((bf16[2048,2048]{1,0:T(8,128)(2,1)}), bf16[2048,2048]{1,0:T(8,128)(2,1)}) %all-reduce.9.cloned.1.call-update) | async-done | bytes 8388624 | tf_op jit(solution)/shard_map/psum | solution.py:250
  951.1 30.1 %fusion.118 = (bf16[2048,2048]{0,1:T(8,128)(2,1)}, f32[2048,2048]{1,0:T(8,128)}, bf16[2048,2048]{1,0:T(8,128)(2,1)}) fusion(f32[2048]{0:T(1024)S(1)} %bitcast.347, f32[2048]{0:T(1024)S(1)} %bitcast.344, f32[2048]{0:T(1024)S(1)} %copy-done.27, f32[2048]{0:T(1024)S(1)} %copy-done.24, bf16[2048,2048]{1,0:T(8,128)(2,1)} %param.18, ...), kind=kLoop, calls=%fused_computation.209 | loop fusion | flops 96468992 | bytes 83968000 | tf_op jit(solution)/shard_map/td,te->de/dot_general | solution.py:284
  981.3 12.2 copy.120
  999.7 23.1 %fusion.114 = f32[2048,2048]{1,0:T(8,128)S(1)} fusion(bf16[2048,2048]{1,0:T(8,128)(2,1)} %get-tuple-element.379, bf16[2048,2048]{1,0:T(8,128)(2,1)} %param.18, f32[2048]{0:T(1024)S(1)} %bitcast.356, f32[2048]{0:T(1024)S(1)} %bitcast.340, f32[2048]{0:T(1024)S(1)} %copy-done.27, f32[2048]{0:T(1024)S(1)} %copy-done.24), kind=kOutput, calls=%fused_computation.207 | convolution fusion | flops 17205035008 | bytes 33587200 | tf_op jit(solution)/shard_map/td,tf->df/dot_general | solution.py:286
  1022.8 6.1 copy.148
  1029.0 7.7 copy.106
  1036.7 21.9 fusion.130
  1058.6 11.7 copy.149
  1070.3 8.0 copy.107
  1078.3 6.1 fusion.129
  1084.4 12.2 copy.118
  1096.6 18.9 fusion.128
  1115.6 34.8 %pad_maximum_fusion = f32[192,256,256]{2,1,0:T(8,128)} fusion(f32[64,256,256]{2,1,0:T(8,128)} %bitcast.286, f32[64,256,256]{2,1,0:T(8,128)} %bitcast.285, f32[16,256,256]{2,1,0:T(8,128)} %bitcast.327, f32[48,256,256]{2,1,0:T(8,128)} %bitcast.303), kind=kLoop, calls=%fused_computation.66 | loop fusion | flops 37748736 | bytes 100663296 | tf_op jit(solution)/shard_map/concatenate | solution.py:288
  1150.4 34.6 %gather_fusion.1 = f32[192,256,256]{2,1,0:T(8,128)} fusion(f32[192,256,256]{2,1,0:T(8,128)} %pad_maximum_fusion, s32[1024]{0:T(1024)} %pad_clamp_fusion), kind=kCustom, calls=%fused_computation.1 | custom fusion | bytes 100664064 | tf_op jit(solution)/shard_map/gather | solution.py:292
  1189.3 20.1 psum.45
  1209.5 334.1 %all-reduce.11.cloned.1.call-done = f32[2048,2048]{1,0:T(8,128)} async-done(((f32[2048,2048]{1,0:T(8,128)}), f32[2048,2048]{1,0:T(8,128)}) %all-reduce.11.cloned.1.call-update) | async-done | bytes 16777232 | tf_op jit(solution)/shard_map/psum | solution.py:282
  1543.6 14.7 convert_reduce_fusion.1
  1558.4 27.9 %all-reduce.4 = (f32[6,2048]{1,0:T(8,128)S(1)}, f32[3584]{0:T(1024)S(1)}) all-reduce(f32[6,2048]{1,0:T(8,128)S(1)} %pad_maximum_fusion.5, f32[3584]{0:T(1024)S(1)} %pad_maximum_fusion.7), channel_id=1, replica_groups=mesh['dp'=8,'mp'=4] {'dp'}, use_global_device_ids=true, to_apply=%region_28.29 | all-reduce | flops 15872 | bytes 126976 | tf_op jit(solution)/shard_map/psum | solution.py:301
  1588.8 538.0 %all-reduce.13.cloned.1.call-done = f32[192,256,256]{2,1,0:T(8,128)} async-done(((f32[192,256,256]{2,1,0:T(8,128)}), f32[192,256,256]{2,1,0:T(8,128)}) %all-reduce.13.cloned.1.call-update) | async-done | bytes 50331664 | tf_op jit(solution)/shard_map/psum | solution.py:301
  2126.9 13.1 fusion.87
  2140.0 9.5 multiply_reduce_fusion.1
  2153.5 6.2 dynamic-slice_bitcast_fusion.1
  2159.7 17.2 fusion.90
  2177.0 19.1 fusion.92
  (300 shorter events, 182.4 us)
Async XLA Ops:
  7.2 5.1 copy-start.53
  7.2 5.1 copy-start.54
  7.2 5.6 copy-start.36
  7.2 6.2 copy-start.51
  7.2 133.1 %all-gather.2.cloned.1.call-start = ((), (), s32[]{:S(2)}) async-start(), calls=%async_computation | async-start | bytes 28311552 | tf_op jit(solution)/shard_map/all_gather | solution.py:221
  12.2 939.0 %all-reduce.9.cloned.1.call-start = ((), (), s32[]{:S(2)}) async-start(), calls=%async_computation.1 | async-start | bytes 16777216 | tf_op jit(solution)/shard_map/psum | solution.py:250
  12.8 5.8 copy-start.3
  18.3 6.9 copy-start.20
  18.6 162.3 %copy-start.22 = (f32[2048]{0:T(1024)}, f32[2048]{0:T(1024)S(1)}, u32[]{:S(2)}) copy-start(f32[2048]{0:T(1024)S(1)} %broadcast_multiply_fusion) | copy-start | bytes 24580
  20.9 160.0 %copy-start.25 = (f32[2048]{0:T(1024)}, f32[2048]{0:T(1024)S(1)}, u32[]{:S(2)}) copy-start(f32[2048]{0:T(1024)S(1)} %fusion.110) | copy-start | bytes 24580
  25.2 205.6 %copy-start.9 = (f32[2048,64]{1,0:T(8,128)}, f32[2048,64]{1,0:T(8,128)S(1)}, u32[]{:S(2)}) copy-start(f32[2048,64]{1,0:T(8,128)S(1)} %get-tuple-element.380) | copy-start | bytes 1572868
  25.3 205.6 %copy-start.11 = (f32[2048,64]{1,0:T(8,128)}, f32[2048,64]{1,0:T(8,128)S(1)}, u32[]{:S(2)}) copy-start(f32[2048,64]{1,0:T(8,128)S(1)} %get-tuple-element.381) | copy-start | bytes 1572868
  26.0 154.9 %copy-start.30 = (f32[1,2048]{1,0:T(1,128)}, f32[1,2048]{1,0:T(1,128)S(1)}, u32[]{:S(2)}) copy-start(f32[1,2048]{1,0:T(1,128)S(1)} %get-tuple-element.367) | copy-start | bytes 24580
  26.0 154.9 %copy-start.39 = (f32[1,2048]{1,0:T(1,128)}, f32[1,2048]{1,0:T(1,128)S(1)}, u32[]{:S(2)}) copy-start(f32[1,2048]{1,0:T(1,128)S(1)} %get-tuple-element.366) | copy-start | bytes 24580
  180.9 19.0 copy-start.16
  199.8 4.6 copy-start.13
  217.3 8.2 copy-start.7
  245.8 42.7 %slice-start = ((bf16[192,256,256]{2,1,0:T(8,128)(2,1)}), bf16[16,256,256]{2,1,0:T(8,128)(2,1)S(1)}, s32[]{:S(2)}) async-start(bf16[192,256,256]{2,1,0:T(8,128)(2,1)} %gather_fusion), calls=%async_computation.4 | async-start | bytes 4194304 | tf_op jit(solution)/shard_map/slice | solution.py:86
  300.7 9.0 copy-start.5
  322.8 6.0 copy-start.2
  322.8 6.0 copy-start.8
  322.8 8.3 copy-start.1
  349.1 7.3 copy-start.2
  349.1 7.3 copy-start.8
  349.1 9.6 copy-start.1
  377.5 7.3 copy-start.2
  377.5 7.3 copy-start.8
  377.5 9.6 copy-start.1
  405.9 7.3 copy-start.2
  405.9 7.3 copy-start.8
  405.9 9.5 copy-start.1
  431.6 6.4 copy-start.6
  493.6 10.4 copy-start.23
  493.6 10.4 copy-start.26
  493.6 10.4 copy-start.28
  493.6 10.4 copy-start.47
  493.6 10.4 copy-start.49
  627.0 8.7 slice-start.7
  627.6 8.2 slice-start.8
  660.2 883.5 %all-reduce.11.cloned.1.call-start = ((), (), s32[]{:S(2)}) async-start(), calls=%async_computation.2 | async-start | bytes 33554432 | tf_op jit(solution)/shard_map/psum | solution.py:282
  667.5 5.4 copy-start.14
  677.0 8.7 copy-start.24
  677.0 8.7 copy-start.29
  677.0 8.7 copy-start.31
  685.7 28.8 %copy-start.33 = (f32[2048]{0:T(1024)S(1)}, f32[2048]{0:T(1024)}, u32[]{:S(2)}) copy-start(f32[2048]{0:T(1024)} %copy-done.32) | copy-start | bytes 24580
  685.7 28.8 %copy-start.27 = (f32[2048]{0:T(1024)S(1)}, f32[2048]{0:T(1024)}, u32[]{:S(2)}) copy-start(f32[2048]{0:T(1024)} %copy-done.25) | copy-start | bytes 24580
  714.4 236.7 %copy-start.38 = (f32[1,2048]{1,0:T(1,128)S(1)}, f32[1,2048]{1,0:T(1,128)}, u32[]{:S(2)}) copy-start(f32[1,2048]{1,0:T(1,128)} %get-tuple-element.363) | copy-start | bytes 24580
  714.5 236.7 %copy-start.40 = (f32[1,2048]{1,0:T(1,128)S(1)}, f32[1,2048]{1,0:T(1,128)}, u32[]{:S(2)}) copy-start(f32[1,2048]{1,0:T(1,128)} %copy-done.39) | copy-start | bytes 24580
  981.3 1145.6 %all-reduce.13.cloned.1.call-start = ((), (), s32[]{:S(2)}) async-start(), calls=%async_computation.3 | async-start | bytes 100663296 | tf_op jit(solution)/shard_map/psum | solution.py:301
  981.3 12.2 copy-start.52
  981.3 18.3 copy-start.50
  1022.8 13.9 slice-start.3
  1029.0 7.8 slice-start.4
  1058.6 19.7 slice-start.5
  1070.3 8.0 slice-start.6
  1070.3 8.0 copy-start.19
  1185.0 24.5 %copy-start.48 = (f32[2048]{0:T(1024)S(1)}, f32[2048]{0:T(1024)}, u32[]{:S(2)}) copy-start(f32[2048]{0:T(1024)} %get-tuple-element.378) | copy-start | bytes 24580
  1209.5 378.7 %copy-start.21 = (f32[6,2048]{1,0:T(8,128)S(1)}, f32[6,2048]{1,0:T(8,128)}, u32[]{:S(2)}) copy-start(f32[6,2048]{1,0:T(8,128)} %param.28) | copy-start | bytes 147460
  1209.5 378.7 %copy-start.34 = (f32[6,2048]{1,0:T(8,128)S(1)}, f32[6,2048]{1,0:T(8,128)}, u32[]{:S(2)}) copy-start(f32[6,2048]{1,0:T(8,128)} %param.29) | copy-start | bytes 147460
  1586.3 553.6 %copy-start.35 = (f32[6,2048]{1,0:T(8,128)}, f32[6,2048]{1,0:T(8,128)S(1)}, u32[]{:S(2)}) copy-start(f32[6,2048]{1,0:T(8,128)S(1)} %get-tuple-element.332) | copy-start | bytes 147460
  2126.9 22.6 %slice-start.1 = ((s8[6291456]{0:T(1024)(128)(4,1)}), s8[4194304]{0:T(1024)(128)(4,1)S(1)}, s32[]{:S(2)}) async-start(s8[6291456]{0:T(1024)(128)(4,1)} %bitcast.287), calls=%async_computation.5 | async-start | bytes 8388608
  2139.9 9.5 slice-start.2
  2153.5 23.5 %slice-start.9 = ((s8[6291456]{0:T(1024)(128)(4,1)}), s8[4194304]{0:T(1024)(128)(4,1)S(1)}, s32[]{:S(2)}) async-start(s8[6291456]{0:T(1024)(128)(4,1)} %bitcast.325), calls=%async_computation.13 | async-start | bytes 8388608
  2159.7 17.2 slice-start.10
  (21 other events, 66.1 us)
Sparse Core Ops, SparseCore 0:
  12.3 128.0 all-gather.1
  660.3 290.8 all-reduce.8
  981.4 562.1 all-reduce.10
  1547.2 579.5 all-reduce.12
where the time goes:
time: 2210 us; the launch traced here: 2200 us
  waiting for transfers between devices  1200 us (54%)
  matrix products  455 us (21%)
  local copies, waits for them, and re-layouts  274 us (12%)
  other arithmetic  206 us (9%)
  blocking collectives  48.1 us (2%)
    psum x1, waiting for transfers between devices, per_device(): lax.psum((slot_grads, vector_part, unit_part), 'dp')  538 us
    psum x1, waiting for transfers between devices, per_device(): input_sum, norm_sum = lax.psum((input_part, norm_part), 'mp')  334 us
    psum x1, waiting for transfers between devices, per_device(): lax.psum(partial_out.astype(jnp.bfloat16), 'mp').astype(jnp.float32)  217 us
    all_gather x1, waiting for transfers between devices, per_device(): gathered = lax.all_gather(sent_blocks, 'dp', axis=0, tiled=True)  114 us
    unnamed x130, local copies, waits for them, and re-layouts  62.6 us
    dot_general x1, matrix products, per_device(): jnp.dot(normed_two, up_w, preferred_element_type=jnp.float32)  61.4 us
  transfers between devices with their start and end apart: 4, of which 4 were waited for; matrix products, arithmetic and copies ran while one was open for 14% of the time, Pallas kernels for 0%

commit v1 on v0

--- a/solution.py
+++ b/solution.py
@@ -1,8 +1,11 @@
+import functools
 import math
 
 import jax
 import jax.numpy as jnp
 from jax import lax
+from jax.experimental import pallas as pl
+from jax.experimental.pallas import tpu as pltpu
 from jax.sharding import PartitionSpec as P
 
 D = 2048
@@ -327,6 +330,802 @@
     )
 
 
+LOW = jnp.bfloat16
+WIDE = jnp.float32
+MESH = pl.DeviceIdType.MESH
+ANY = pl.BlockSpec(memory_space=pl.ANY)
+STEP = 256
+SUB = 64
+PAIRS = 16
+STEPS = 8
+VMEM_BYTES = 60 * 1024 * 1024
+
+
+def dot(left, right):
+    return lax.dot_general(left, right, (((1,), (0,)), ((), ())), preferred_element_type=WIDE)
+
+
+def dot_nt(left, right):
+    return lax.dot_general(left, right, (((1,), (1,)), ((), ())), preferred_element_type=WIDE)
+
+
+def dot_tn(left, right):
+    return lax.dot_general(left, right, (((0,), (0,)), ((), ())), preferred_element_type=WIDE)
+
+
+def resident(shape):
+    return pl.BlockSpec(shape, lambda *_: (0,) * len(shape), pipeline_mode=pl.Buffered(1))
+
+
+def tile_of(refs, widths, block):
+    for ref, (rows, cols) in zip(refs, widths):
+        count = (rows // B) * (cols // B)
+        if block < count:
+            i, j = divmod(block, cols // B)
+            return ref.at[pl.ds(i * B, B), pl.ds(j * B, B)]
+        block -= count
+
+
+def move_blocks(copies_in, copies_out):
+    for copy in copies_in:
+        copy.start()
+    for first, second in zip(copies_in, copies_out):
+        first.wait()
+        second.start()
+    for copy in copies_out:
+        copy.wait()
+
+
+def place_kernel(shapes, order_ref, slots_ref, *refs):
+    mats, (hold, sem_in, sem_out) = refs[:-3], refs[-3:]
+    total = slots_ref.shape[0]
+    move_blocks(
+        [
+            pltpu.make_async_copy(slots_ref.at[order_ref[b]], hold.at[b], sem_in.at[b])
+            for b in range(total)
+        ],
+        [
+            pltpu.make_async_copy(hold.at[b], tile_of(mats, shapes, b), sem_out.at[b])
+            for b in range(total)
+        ],
+    )
+
+
+def block_scratch(total):
+    return [
+        pltpu.VMEM((total, B, B), LOW),
+        pltpu.SemaphoreType.DMA((total,)),
+        pltpu.SemaphoreType.DMA((total,)),
+    ]
+
+
+def place_blocks(slots, order, shapes):
+    total = slots.shape[0]
+    return pl.pallas_call(
+        functools.partial(place_kernel, shapes),
+        grid_spec=pltpu.PrefetchScalarGridSpec(
+            num_scalar_prefetch=1,
+            grid=(1,),
+            in_specs=[ANY],
+            out_specs=[ANY] * len(shapes),
+            scratch_shapes=block_scratch(total),
+        ),
+        out_shape=[jax.ShapeDtypeStruct(s, LOW) for s in shapes],
+        compiler_params=pltpu.CompilerParams(vmem_limit_bytes=VMEM_BYTES),
+        name="place_blocks",
+    )(order, slots)
+
+
+def unplace_kernel(shapes, order_ref, *refs):
+    mats, (slots_ref, hold, sem_in, sem_out) = refs[:-4], refs[-4:]
+    total = slots_ref.shape[0]
+    move_blocks(
+        [
+            pltpu.make_async_copy(tile_of(mats, shapes, b), hold.at[b], sem_in.at[b])
+            for b in range(total)
+        ],
+        [
+            pltpu.make_async_copy(hold.at[b], slots_ref.at[order_ref[b]], sem_out.at[b])
+            for b in range(total)
+        ],
+    )
+
+
+def unplace_blocks(mats, order):
+    shapes = [m.shape for m in mats]
+    total = order.shape[0]
+    return pl.pallas_call(
+        functools.partial(unplace_kernel, shapes),
+        grid_spec=pltpu.PrefetchScalarGridSpec(
+            num_scalar_prefetch=1,
+            grid=(1,),
+            in_specs=[ANY] * len(mats),
+            out_specs=ANY,
+            scratch_shapes=block_scratch(total),
+        ),
+        out_shape=jax.ShapeDtypeStruct((total, B, B), LOW),
+        compiler_params=pltpu.CompilerParams(vmem_limit_bytes=VMEM_BYTES),
+        name="unplace_blocks",
+    )(order, *mats)
+
+
+def turn(values, cos, sin_high, sin_low):
+    return (
+        values * cos
+        + pltpu.roll(values, 32, 1) * sin_high
+        - pltpu.roll(values, 96, 1) * sin_low
+    )
+
+
+def turn_back(values, cos, sin_high, sin_low):
+    return (
+        values * cos
+        - pltpu.roll(values, 32, 1) * sin_high
+        + pltpu.roll(values, 96, 1) * sin_low
+    )
+
+
+def qkv_kernel(scale, h_ref, w_ref, bias_ref, cos_ref, high_ref, low_ref, q_ref, k_ref, v_ref):
+    for j in range(w_ref.shape[1] // HD):
+        head, part = divmod(j, 3)
+        cols = slice(head * HD, head * HD + HD)
+        proj = dot(h_ref[...], w_ref[:, j * HD : (j + 1) * HD]) + bias_ref[:, j * HD : (j + 1) * HD]
+        if part == 2:
+            v_ref[:, cols] = proj.astype(LOW)
+            continue
+        front = turn(proj[:, :128], cos_ref[...], high_ref[...], low_ref[...])
+        turned = jnp.concatenate([front, proj[:, 128:]], axis=1).astype(LOW)
+        if part == 0:
+            q_ref[:, cols] = (turned.astype(WIDE) * scale).astype(LOW)
+        else:
+            k_ref[:, cols] = turned
+
+
+def project_qkv(h1, qkv_w, bias, tables):
+    rows, d = h1.shape
+    cols = qkv_w.shape[1]
+    out_cols = cols // 3
+    tile = 512
+    row_spec = lambda width: pl.BlockSpec((tile, width), lambda i: (i, 0))
+    return pl.pallas_call(
+        functools.partial(qkv_kernel, 1.0 / math.sqrt(HD)),
+        grid=(rows // tile,),
+        in_specs=[row_spec(d), resident((d, cols)), resident((1, cols))] + [row_spec(128)] * 3,
+        out_specs=[row_spec(out_cols)] * 3,
+        out_shape=[jax.ShapeDtypeStruct((rows, out_cols), LOW)] * 3,
+        compiler_params=pltpu.CompilerParams(vmem_limit_bytes=VMEM_BYTES),
+        name="project_qkv",
+    )(h1, qkv_w, bias, *tables)
+
+
+def attention_kernel(
+    tile,
+    start_ref,
+    q_ref,
+    k_ref,
+    v_ref,
+    g_ref,
+    cos_ref,
+    high_ref,
+    low_ref,
+    ctx_ref,
+    grad_ref,
+    p_scr,
+    dp_scr,
+    dk_scr,
+    dv_scr,
+):
+    step = pl.program_id(1)
+    count = pl.num_programs(1)
+    scale = 1.0 / math.sqrt(HD)
+
+    @pl.when(step == 0)
+    def _():
+        dk_scr[...] = jnp.zeros_like(dk_scr)
+        dv_scr[...] = jnp.zeros_like(dv_scr)
+
+    def rows(c):
+        q = q_ref[...]
+        g = g_ref[...]
+        first = start_ref[...]
+        top = jnp.full((tile, 1), masked_score, WIDE)
+        for j in range(c + 1):
+            keys = slice(j * tile, (j + 1) * tile)
+            s = dot_nt(q, k_ref[keys, :])
+            col = lax.broadcasted_iota(jnp.int32, (tile, tile), 1) + j * tile
+            ok = col >= first
+            if j == c:
+                row = lax.broadcasted_iota(jnp.int32, (tile, tile), 0) + c * tile
+                ok = ok & (col <= row)
+            s = jnp.where(ok, s, masked_score)
+            p_scr[:, keys] = s
+            top = jnp.maximum(top, jnp.max(s, axis=1, keepdims=True))
+        total = jnp.zeros((tile, 1), WIDE)
+        for j in range(c + 1):
+            keys = slice(j * tile, (j + 1) * tile)
+            e = jnp.exp(p_scr[:, keys] - top)
+            p_scr[:, keys] = e
+            total = total + jnp.sum(e, axis=1, keepdims=True)
+        inverse = 1.0 / total
+        ctx = jnp.zeros((tile, HD), WIDE)
+        delta = jnp.zeros((tile, 1), WIDE)
+        for j in range(c + 1):
+            keys = slice(j * tile, (j + 1) * tile)
+            p = p_scr[:, keys] * inverse
+            p_scr[:, keys] = p
+            pb = p.astype(LOW)
+            dp = dot_nt(g, v_ref[keys, :])
+            dp_scr[:, keys] = dp
+            delta = delta + jnp.sum(p * dp, axis=1, keepdims=True)
+            ctx = ctx + dot(pb, v_ref[keys, :])
+            dv_scr[keys, :] += dot_tn(pb, g)
+        ctx_ref[...] = ctx.astype(LOW)
+        dq = jnp.zeros((tile, HD), WIDE)
+        for j in range(c + 1):
+            keys = slice(j * tile, (j + 1) * tile)
+            ds = (p_scr[:, keys] * (dp_scr[:, keys] - delta)).astype(LOW)
+            dq = dq + dot(ds, k_ref[keys, :])
+            dk_scr[keys, :] += dot_tn(ds, q)
+        dq = dq * scale
+        here = slice(c * tile, (c + 1) * tile)
+        front = turn_back(dq[:, :128], cos_ref[here, :], high_ref[here, :], low_ref[here, :])
+        grad_ref[here, 0:128] = front.astype(LOW)
+        grad_ref[here, 128:HD] = dq[:, 128:].astype(LOW)
+
+    for c in range(dk_scr.shape[0] // tile):
+        pl.when(step == c)(functools.partial(rows, c))
+
+    @pl.when(step == count - 1)
+    def _():
+        dk = dk_scr[...]
+        front = turn_back(dk[:, :128], cos_ref[...], high_ref[...], low_ref[...])
+        grad_ref[:, HD : HD + 128] = front.astype(LOW)
+        grad_ref[:, HD + 128 : 2 * HD] = dk[:, 128:].astype(LOW)
+        grad_ref[:, 2 * HD :] = dv_scr[...].astype(LOW)
+
+
+def attention_both(start, q, k, v, ctx_grad, tables):
+    rows, cols = q.shape
+    heads = cols // HD
+    tile = 512
+    tile_spec = pl.BlockSpec((tile, HD), lambda h, i: (i, h))
+    full_spec = pl.BlockSpec((rows, HD), lambda h, i: (0, h))
+    flops = heads * rows * rows * HD * 6
+    return pl.pallas_call(
+        functools.partial(attention_kernel, tile),
+        grid=(heads, rows // tile),
+        in_specs=[pl.BlockSpec((tile, 1), lambda h, i: (i, 0)), tile_spec, full_spec, full_spec, tile_spec]
+        + [resident((rows, 128))] * 3,
+        out_specs=[tile_spec, pl.BlockSpec((rows, 3 * HD), lambda h, i: (0, h))],
+        out_shape=[
+            jax.ShapeDtypeStruct((rows, cols), LOW),
+            jax.ShapeDtypeStruct((rows, 3 * cols), LOW),
+        ],
+        scratch_shapes=[
+            pltpu.VMEM((tile, rows), WIDE),
+            pltpu.VMEM((tile, rows), WIDE),
+            pltpu.VMEM((rows, HD), WIDE),
+            pltpu.VMEM((rows, HD), WIDE),
+        ],
+        compiler_params=pltpu.CompilerParams(vmem_limit_bytes=VMEM_BYTES),
+        cost_estimate=pl.CostEstimate(flops=flops, bytes_accessed=30 << 20, transcendentals=0),
+        name="attention_both",
+    )(start, q, k, v, ctx_grad, *tables)
+
+
+class Line:
+    def __init__(self, out, part, got, across, sems):
+        self.out, self.part, self.got, self.across = out, part, got, across
+        (
+            self.up_send,
+            self.up_recv,
+            self.far_send,
+            self.far_recv,
+            self.over_send,
+            self.over_recv,
+            self.down_send,
+            self.down_recv,
+            self.relay_send,
+            self.relay_recv,
+            self.own,
+        ) = [sems.at[i] for i in range(11)]
+        z = lax.axis_index("mp")
+        self.inner = (z == 1) | (z == 2)
+        self.near = (z >= 2).astype(jnp.int32)
+        self.far = 1 - self.near
+        self.partner = jnp.where(self.inner, jnp.where(z == 1, 0, 3), jnp.where(z == 0, 1, 2))
+        self.other = 3 - z
+
+    def rows(self, pair, which):
+        return self.out.at[pl.ds(pl.multiple_of(pair * (2 * SUB) + which * SUB, SUB), SUB), :]
+
+    def greet(self):
+        barrier = pltpu.get_barrier_semaphore()
+        pl.semaphore_signal(barrier, inc=1, device_id={"mp": self.partner}, device_id_type=MESH)
+
+        @pl.when(self.inner)
+        def _():
+            pl.semaphore_signal(barrier, inc=1, device_id={"mp": self.other}, device_id_type=MESH)
+            pl.semaphore_wait(barrier, 2)
+
+        @pl.when(jnp.logical_not(self.inner))
+        def _():
+            pl.semaphore_wait(barrier, 1)
+
+    def copy(self, src, dst, send, recv, pair, target):
+        return pltpu.make_async_remote_copy(
+            src_ref=src,
+            dst_ref=dst,
+            send_sem=send.at[pair],
+            recv_sem=recv.at[pair],
+            device_id={"mp": target},
+            device_id_type=MESH,
+        )
+
+    def up(self, pair):
+        return self.copy(self.part.at[pair], self.got.at[pair], self.up_send, self.up_recv, pair, self.partner)
+
+    def far_sum(self, pair):
+        return self.copy(
+            self.part.at[pair, self.far], self.across.at[pair], self.far_send, self.far_recv, pair, self.other
+        )
+
+    def over(self, pair, which):
+        src = self.part.at[pair, self.near]
+        return self.copy(src, self.rows(pair, which), self.over_send, self.over_recv, pair, self.other)
+
+    def down(self, pair):
+        src = self.part.at[pair, self.near]
+        return self.copy(
+            src, self.rows(pair, self.near), self.down_send, self.down_recv, pair, self.partner
+        )
+
+    def relay(self, pair):
+        far = self.rows(pair, self.far)
+        return self.copy(far, far, self.relay_send, self.relay_recv, pair, self.partner)
+
+    def keep(self, pair):
+        src = self.part.at[pair, self.near]
+        return pltpu.make_async_copy(src, self.rows(pair, self.near), self.own.at[pair])
+
+    def send_up(self, pair):
+        @pl.when(jnp.logical_not(self.inner))
+        def _():
+            self.up(pair).start()
+
+    def add_far(self, pair):
+        self.up(pair).wait_recv()
+        far = self.part[pair, self.far].astype(WIDE) + self.got[pair, self.far].astype(WIDE)
+        self.part[pair, self.far] = far.astype(LOW)
+        self.far_sum(pair).start()
+
+    def finish_near(self, pair, base):
+        self.far_sum(pair).wait_recv()
+        total = (
+            self.part[pair, self.near].astype(WIDE)
+            + self.got[pair, self.near].astype(WIDE)
+            + self.across[pair].astype(WIDE)
+        )
+        self.part[pair, self.near] = (base + total).astype(LOW)
+        self.over(pair, self.near).start()
+        self.down(pair).start()
+        self.keep(pair).start()
+
+    def send_relay(self, pair):
+        self.over(pair, self.far).wait_recv()
+        self.relay(pair).start()
+
+    def drain(self):
+        @pl.when(self.inner)
+        def _():
+            @pl.loop(0, PAIRS)
+            def _(pair):
+                self.far_sum(pair).wait_send()
+                self.over(pair, self.near).wait_send()
+                self.down(pair).wait_send()
+                self.relay(pair).wait_send()
+                self.keep(pair).wait()
+
+        @pl.when(jnp.logical_not(self.inner))
+        def _():
+            @pl.loop(0, PAIRS)
+            def _(pair):
+                self.up(pair).wait_send()
+                self.down(pair).wait_recv()
+                self.relay(pair).wait_recv()
+
+    def tick(self, step, base_of):
+        @pl.when(self.inner & (step >= 1) & (step < STEPS + 1))
+        def _():
+            for s in range(2):
+                self.add_far((step - 1) * 2 + s)
+
+        @pl.when(self.inner & (step >= 2) & (step < STEPS + 2))
+        def _():
+            for s in range(2):
+                offset = pl.multiple_of(s * 2 * SUB + self.near * SUB, SUB)
+                self.finish_near((step - 2) * 2 + s, base_of(offset))
+
+        @pl.when(self.inner & (step >= 3) & (step < STEPS + 3))
+        def _():
+            for s in range(2):
+                self.send_relay((step - 3) * 2 + s)
+
+
+LINE_STEPS = STEPS + 3
+
+
+def line_scratch(d):
+    return [
+        pltpu.VMEM((PAIRS, 2, SUB, d), LOW),
+        pltpu.VMEM((PAIRS, 2, SUB, d), LOW),
+        pltpu.VMEM((PAIRS, SUB, d), LOW),
+        pltpu.SemaphoreType.DMA((11, PAIRS)),
+    ]
+
+
+def now(step):
+    return jnp.minimum(step, STEPS - 1)
+
+
+def later(step):
+    return jnp.clip(step - 2, 0, STEPS - 1)
+
+
+def row_block(width, at):
+    return pl.BlockSpec((STEP, width), lambda i: (at(i), 0))
+
+
+def gelu_parts(z):
+    e = jnp.exp(z * z * -0.5)
+    t = 1.0 / (1.0 + jnp.abs(z) * (0.3275911 * math.sqrt(0.5)))
+    poly = t * (
+        0.5 * 0.254829592
+        + t
+        * (
+            0.5 * -0.284496736
+            + t * (0.5 * 1.421413741 + t * (0.5 * -1.453152027 + t * (0.5 * 1.061405429)))
+        )
+    )
+    below = poly * e
+    cdf = jnp.where(z >= 0, 1.0 - below, below)
+    return cdf, e * (1.0 / math.sqrt(2.0 * math.pi))
+
+
+def store_part(part_ref, step, cols, value):
+    part_ref[pl.ds(step * 2, 2), :, :, cols] = value.astype(LOW).reshape(2, 2, SUB, value.shape[1])
+
+
+def forward_kernel(
+    h_ref,
+    g_ref,
+    ctx_ref,
+    x_ref,
+    up_ref,
+    od_ref,
+    bias_ref,
+    shift_ref,
+    act_ref,
+    hg_ref,
+    out_ref,
+    part,
+    got,
+    across,
+    sems,
+):
+    step = pl.program_id(0)
+    line = Line(out_ref, part, got, across, sems)
+    heads = ctx_ref.shape[1]
+    width = 512
+
+    @pl.when(step == 0)
+    def _():
+        line.greet()
+
+    @pl.when(step < STEPS)
+    def _():
+        for n in range(up_ref.shape[1] // width):
+            cols = slice(n * width, (n + 1) * width)
+            hidden = dot(h_ref[...], up_ref[:, cols]) + bias_ref[:, cols]
+            act_grad = dot_nt(g_ref[...], od_ref[heads + n * width : heads + (n + 1) * width, :])
+            cdf, density = gelu_parts(hidden)
+            act_ref[:, cols] = (hidden * cdf).astype(LOW)
+            hg_ref[:, cols] = (act_grad * (cdf + hidden * density)).astype(LOW)
+        for n in range(od_ref.shape[1] // width):
+            cols = slice(n * width, (n + 1) * width)
+            value = dot(ctx_ref[...], od_ref[:heads, cols]) + dot(act_ref[...], od_ref[heads:, cols])
+            store_part(part, step, cols, value)
+        for s in range(2):
+            line.send_up(step * 2 + s)
+
+    line.tick(
+        step, lambda offset: x_ref[pl.ds(offset, SUB), :].astype(WIDE) + shift_ref[...]
+    )
+
+    @pl.when(step == LINE_STEPS - 1)
+    def _():
+        line.drain()
+
+
+def forward_line(h2, cotangent, ctx, tokens, up_w, od_w, bias, shift):
+    rows, d = tokens.shape
+    units = up_w.shape[1]
+    return pl.pallas_call(
+        forward_kernel,
+        grid=(LINE_STEPS,),
+        in_specs=[
+            row_block(d, now),
+            row_block(d, now),
+            row_block(ctx.shape[1], now),
+            row_block(d, later),
+            resident(up_w.shape),
+            resident(od_w.shape),
+            resident(bias.shape),
+            resident(shift.shape),
+        ],
+        out_specs=[row_block(units, now), row_block(units, now), ANY],
+        out_shape=[
+            jax.ShapeDtypeStruct((rows, units), LOW),
+            jax.ShapeDtypeStruct((rows, units), LOW),
+            jax.ShapeDtypeStruct((rows, d), LOW),
+        ],
+        scratch_shapes=line_scratch(d),
+        compiler_params=pltpu.CompilerParams(
+            vmem_limit_bytes=VMEM_BYTES, collective_id=1, has_side_effects=True
+        ),
+        cost_estimate=pl.CostEstimate(
+            flops=200_000_000_000, bytes_accessed=80 << 20, transcendentals=0
+        ),
+        name="forward_line",
+    )(h2, cotangent, ctx, tokens, up_w, od_w, bias, shift)
+
+
+def backward_kernel(
+    qg_ref,
+    hg_ref,
+    x_ref,
+    g_ref,
+    qkv_ref,
+    up_ref,
+    one_ref,
+    two_ref,
+    norm_ref,
+    out_ref,
+    gc_scr,
+    xhat_scr,
+    part,
+    got,
+    across,
+    sems,
+):
+    step = pl.program_id(0)
+    line = Line(out_ref, part, got, across, sems)
+    d = x_ref.shape[1]
+    width = 512
+
+    @pl.when(step == 0)
+    def _():
+        line.greet()
+        norm_ref[...] = jnp.zeros_like(norm_ref)
+
+    @pl.when(step < STEPS)
+    def _():
+        x = x_ref[...].astype(WIDE)
+        center = x - jnp.mean(x, axis=1, keepdims=True)
+        scale = lax.rsqrt(jnp.mean(center * center, axis=1, keepdims=True) + norm_eps)
+        xhat_scr[...] = center * scale
+        mean = jnp.zeros((STEP, 1), WIDE)
+        slope = jnp.zeros((STEP, 1), WIDE)
+        for n in range(d // width):
+            cols = slice(n * width, (n + 1) * width)
+            e1 = dot_nt(qg_ref[...], qkv_ref[cols, :])
+            e2 = dot_nt(hg_ref[...], up_ref[cols, :])
+            xhat = xhat_scr[:, cols]
+            gc = e1 * one_ref[:, cols] + e2 * two_ref[:, cols]
+            gc_scr[:, cols] = gc
+            mean = mean + jnp.sum(gc, axis=1, keepdims=True)
+            slope = slope + jnp.sum(gc * xhat, axis=1, keepdims=True)
+            norm_ref[0:1, cols] += jnp.sum(e1 * xhat, axis=0, keepdims=True)
+            norm_ref[1:2, cols] += jnp.sum(e1, axis=0, keepdims=True)
+            norm_ref[2:3, cols] += jnp.sum(e2 * xhat, axis=0, keepdims=True)
+            norm_ref[3:4, cols] += jnp.sum(e2, axis=0, keepdims=True)
+        mean = mean * (1.0 / d)
+        slope = slope * (1.0 / d)
+        for n in range(d // width):
+            cols = slice(n * width, (n + 1) * width)
+            value = (gc_scr[:, cols] - mean - xhat_scr[:, cols] * slope) * scale
+            store_part(part, step, cols, value)
+        for s in range(2):
+            line.send_up(step * 2 + s)
+
+    line.tick(step, lambda offset: g_ref[pl.ds(offset, SUB), :].astype(WIDE))
+
+    @pl.when(step == LINE_STEPS - 1)
+    def _():
+        line.drain()
+
+
+def backward_line(qkv_grad, hidden_grad, tokens, cotangent, qkv_w, up_w, gain_one, gain_two):
+    rows, d = tokens.shape
+    return pl.pallas_call(
+        backward_kernel,
+        grid=(LINE_STEPS,),
+        in_specs=[
+            row_block(qkv_grad.shape[1], now),
+            row_block(hidden_grad.shape[1], now),
+            row_block(d, now),
+            row_block(d, later),
+            resident(qkv_w.shape),
+            resident(up_w.shape),
+            resident((1, d)),
+            resident((1, d)),
+        ],
+        out_specs=[pl.BlockSpec((8, d), lambda i: (0, 0)), ANY],
+        out_shape=[jax.ShapeDtypeStruct((8, d), WIDE), jax.ShapeDtypeStruct((rows, d), LOW)],
+        scratch_shapes=[pltpu.VMEM((STEP, d), WIDE), pltpu.VMEM((STEP, d), WIDE)] + line_scratch(d),
+        compiler_params=pltpu.CompilerParams(
+            vmem_limit_bytes=VMEM_BYTES, collective_id=2, has_side_effects=True
+        ),
+        cost_estimate=pl.CostEstimate(
+            flops=200_000_000_000, bytes_accessed=60 << 20, transcendentals=0
+        ),
+        name="backward_line",
+    )(qkv_grad, hidden_grad, tokens, cotangent, qkv_w, up_w, gain_one, gain_two)
+
+
+def halves(values):
+    high = values.astype(LOW)
+    return high, (values - high.astype(WIDE)).astype(LOW)
+
+
+def shampoo_kernel(
+    g_ref, w_ref, ls_ref, rs_ref, lr_ref, rr_ref, grad_ref, left_ref, right_ref, weight_ref
+):
+    for n in range(g_ref.shape[0]):
+        g = g_ref[n]
+        grad_ref[n] = g.astype(WIDE)
+        left_ref[n] = 0.5 * ls_ref[n] + 0.5 * dot_nt(g, g)
+        right_ref[n] = 0.5 * rs_ref[n] + 0.5 * dot_tn(g, g)
+        l_high, l_low = halves(lr_ref[n])
+        r_high, r_low = halves(rr_ref[n])
+        d_high, d_low = halves(dot(l_high, g) + dot(l_low, g))
+        direction = dot(d_high, r_high) + dot(d_low, r_high) + dot(d_high, r_low)
+        weight = w_ref[n]
+        size = 1.0 / (B * B)
+        weight_size = jnp.sqrt(jnp.sum(weight * weight, keepdims=True) * size)
+        step_size = jnp.sqrt(jnp.sum(direction * direction, keepdims=True) * size + 1e-06)
+        weight_ref[n] = weight - direction * (step_share * weight_size / step_size)
+
+
+def shampoo(grads, weights, left_stat, right_stat, left_root, right_root):
+    count = grads.shape[0]
+    group = 2
+    spec = pl.BlockSpec((group, B, B), lambda i: (i, 0, 0))
+    return pl.pallas_call(
+        shampoo_kernel,
+        grid=(count // group,),
+        in_specs=[spec] * 6,
+        out_specs=[spec] * 4,
+        out_shape=[jax.ShapeDtypeStruct((count, B, B), WIDE)] * 4,
+        compiler_params=pltpu.CompilerParams(vmem_limit_bytes=VMEM_BYTES),
+        name="shampoo",
+    )(grads, weights, left_stat, right_stat, left_root, right_root)
+
+
+def per_device_line(
+    tokens,
+    cotangent,
+    seq_len,
+    seq_device,
+    owner_map,
+    weight_blocks,
+    left_stat,
+    right_stat,
+    left_root,
+    right_root,
+    vectors,
+    vector_stat,
+    unit_bias,
+    unit_stat,
+):
+    groups = lax.axis_size("mp")
+    device = lax.axis_index("dp")
+    row_count, d = tokens.shape
+    qkv_cols = 3 * d // groups
+    head_cols = d // groups
+    unit_cols = FF // groups
+    gathered = lax.all_gather(weight_blocks[0].astype(LOW), "dp", axis=0, tiled=True)
+
+    segment, position = segment_layout(seq_len, seq_device, device, row_count)
+    start = (jnp.arange(row_count, dtype=jnp.int32) - position)[:, None]
+    frequency = 10000.0 ** (-2.0 * jnp.arange(ROT // 2, dtype=WIDE) / ROT)
+    angles = position.astype(WIDE)[:, None] * frequency[None, :]
+    cos, sin = jnp.cos(angles), jnp.sin(angles)
+    pad = jnp.zeros((row_count, 128 - ROT), WIDE)
+    empty = jnp.zeros_like(sin)
+    tables = (
+        jnp.concatenate([cos, cos, pad + 1.0], axis=1),
+        jnp.concatenate([empty, sin, pad], axis=1),
+        jnp.concatenate([sin, empty, pad], axis=1),
+    )
+    inputs = tokens.astype(WIDE)
+    normed_one = layer_norm(inputs, vectors[0], vectors[1]).astype(LOW)
+    normed_two = layer_norm(inputs, vectors[2], vectors[3]).astype(LOW)
+    out_sum = jnp.sum(cotangent.astype(WIDE), axis=0)
+    shift = (vectors[4] + vectors[5])[None]
+    unit_shift = unit_bias[0]
+
+    shapes = ((d, qkv_cols), (head_cols + unit_cols, d), (d, unit_cols))
+    blocks = [(a // B) * (b // B) for a, b in ((d, qkv_cols), (head_cols, d), (d, unit_cols))]
+    order = jnp.concatenate(
+        [
+            owner_map[: blocks[0] + blocks[1]],
+            owner_map[blocks[0] + blocks[1] + blocks[2] :],
+            owner_map[blocks[0] + blocks[1] : blocks[0] + blocks[1] + blocks[2]],
+        ]
+    )
+    qkv_w, od_w, up_w = place_blocks(gathered, order, shapes)
+
+    q, k, v = project_qkv(normed_one, qkv_w, unit_shift[None, :qkv_cols], tables)
+    ctx_grad = jnp.einsum(
+        "td,id->ti", cotangent, od_w[:head_cols], preferred_element_type=WIDE
+    ).astype(LOW)
+    ctx, qkv_grad = attention_both(start, q, k, v, ctx_grad, tables)
+    act, hidden_grad, block_out = forward_line(
+        normed_two, cotangent, ctx, tokens, up_w, od_w, unit_shift[None, qkv_cols:], shift
+    )
+    mats = [
+        lax.dot_general(a, b, (((0,), (0,)), ((), ())), preferred_element_type=WIDE).astype(LOW)
+        for a, b in (
+            (normed_one, qkv_grad),
+            (ctx, cotangent),
+            (normed_two, hidden_grad),
+            (act, cotangent),
+        )
+    ]
+    slots = unplace_blocks(mats, owner_map)
+    owned = lax.psum_scatter(slots, "dp", scatter_dimension=0, tiled=True)
+    qkv_grad, hidden_grad, slots = lax.optimization_barrier((qkv_grad, hidden_grad, slots))
+    norm_part, input_grad = backward_line(
+        qkv_grad,
+        hidden_grad,
+        tokens,
+        cotangent,
+        qkv_w,
+        up_w,
+        vectors[0:1],
+        vectors[2:3],
+    )
+    block_grad, left_new, right_new, weight_new = shampoo(
+        owned, weight_blocks[0], left_stat[0], right_stat[0], left_root[0], right_root[0]
+    )
+    unit_part = jnp.concatenate(
+        [
+            jnp.sum(qkv_grad.astype(WIDE), axis=0),
+            jnp.sum(hidden_grad.astype(WIDE), axis=0),
+        ]
+    )
+    norm_sum = lax.psum(norm_part[:4], "mp")
+    vector_part = jnp.concatenate([norm_sum, jnp.stack([out_sum, out_sum])], axis=0)
+    vector_grad, unit_grad = lax.psum((vector_part, unit_part), "dp")
+    vector_stat_new, vector_new = vector_update(vectors, vector_stat, vector_grad)
+    unit_stat_new, unit_new = vector_update(unit_shift, unit_stat[0], unit_grad)
+    return (
+        block_out,
+        input_grad,
+        block_grad[None],
+        left_new[None],
+        right_new[None],
+        weight_new[None],
+        vector_grad,
+        vector_stat_new,
+        vector_new,
+        unit_grad[None],
+        unit_stat_new[None],
+        unit_new[None],
+    )
+
+
 def solution(mesh):
     placed = (
         P("dp", None),
@@ -344,8 +1143,11 @@
         P("mp", None),
         P("mp", None),
     )
+    body = per_device
+    if mesh.shape["dp"] == 8 and mesh.shape["mp"] == 4:
+        body = per_device_line
     return jax.shard_map(
-        per_device,
+        body,
         mesh=mesh,
         in_specs=placed,
         out_specs=(

time: 2210 us -> 947 us (0.43)
  waiting for transfers between devices: 1200 us -> 96.7 us
  Pallas kernels: 0 us -> 631 us
  matrix products: 455 us -> 83 us
  local copies, waits for them, and re-layouts: 274 us -> 22.3 us
  other arithmetic: 206 us -> 50.8 us
    psum x3 -> x0, waiting for transfers between devices: 1090 us -> none  [the longest x1 538 us: per_device(): lax.psum((slot_grads, vector_part, unit_part), 'dp')]
    pallas_call x0 -> x7, Pallas kernels: none -> 631 us  [the longest x1 259 us: forward_line(): pl.pallas_call(forward_kernel, grid=(LINE_STEPS,), in_specs=[row_block(d,...]
    dot_general x44 -> x5, matrix products: 455 us -> 83 us  [the longest x4 73.1 us: per_device_line(): lax.dot_general(a, b, (((0,), (0,)), ((), ())), preferred_element_type=WIDE)]
    gather x2 -> x0, local copies, waits for them, and re-layouts: 54.3 us -> none  [the longest x1 34.6 us: per_device(): slot_grads = canonical_grad[jnp.argsort(owner_map)]]
    reshape x7 -> x0, local copies, waits for them, and re-layouts: 49.9 us -> none  [the longest x4 34.1 us: blocks_to_matrix(): blocks.reshape(down_count, across, B, B).transpose(0, 2, 1, 3)]
    unnamed x130 -> x42, local copies, waits for them, and re-layouts: 62.6 us -> 17.7 us
    reduce_sum x8 -> x3, other arithmetic: 51.9 us -> 14.5 us  [the longest x1 6.09 us: per_device_line(): out_sum = jnp.sum(cotangent.astype(WIDE), axis=0)]
    concatenate x5 -> x4, other arithmetic: 38.5 us -> 3.26 us  [the longest x1 2.58 us: per_device_line(): jnp.concatenate([sin, empty, pad], axis=1)]
  transfers between devices with their start and end apart: 4 -> 2, of which waited for: 4 -> 1; matrix products, arithmetic and copies ran while one was open for 14% -> 5% of each run, Pallas kernels for 0% -> 27%
where the time goes in v1:
time: 947 us; the launch traced here: 939 us
  Pallas kernels  631 us (67%)
  waiting for transfers between devices  96.7 us (10%)
  matrix products  83 us (9%)
  other arithmetic  50.8 us (5%)
  blocking collectives  41 us (4%)
  local copies, waits for them, and re-layouts  22.3 us (2%)
  between operations  14.6 us (2%)
    pallas_call x1, Pallas kernels, forward_line(): pl.pallas_call(forward_kernel, grid=(LINE_STEPS,), in_specs=[row_block(d,...  259 us
    pallas_call x1, Pallas kernels, backward_line(): pl.pallas_call(backward_kernel, grid=(LINE_STEPS,), in_specs=[row_block(q...  254 us
    all_gather x1, waiting for transfers between devices, per_device_line(): lax.all_gather(weight_blocks[0].astype(LOW), 'dp', axis=0, tiled=True)  96.6 us
    dot_general x4, matrix products, per_device_line(): lax.dot_general(a, b, (((0,), (0,)), ((), ())), preferred_element_type=WIDE)  73.1 us
    pallas_call x1, Pallas kernels, attention_both(): pl.pallas_call(functools.partial(attention_kernel, tile), grid=(heads, ro...  31.7 us
    pallas_call x1, Pallas kernels, shampoo(): pl.pallas_call(shampoo_kernel, grid=(count // group,), in_specs=[spec] *...  24.6 us
    psum x1, blocking collectives, per_device_line(): vector_grad, unit_grad = lax.psum((vector_part, unit_part), 'dp')  23.6 us
    pallas_call x1, Pallas kernels, unplace_blocks(): pl.pallas_call(functools.partial(unplace_kernel, shapes), grid_spec=pltpu...  21.2 us
  transfers between devices with their start and end apart: 2, of which 1 were waited for; matrix products, arithmetic and copies ran while one was open for 5% of the time, Pallas kernels for 27%

profile of v1, /device:TPU:0, one launch (start us, length us, event | category | flops | bytes accessed | tf_op | source)
XLA Modules:
  0.0 939.1 jit_solution(18061998456055472936)
XLA Ops:
  7.2 0.0 copy-start.7
  7.2 0.0 copy-start.13
  7.2 0.0 all-gather.2.cloned.1.call-start
  7.3 4.9 bitcast_convert_fusion
  12.1 0.0 all-gather.2.cloned.1.call-update
  12.2 0.0 reduce-scatter.2.cloned.1.call-start
  12.2 0.6 slice.50.bias_ref
  12.8 0.6 slice.52.bias_ref
  13.4 0.1 copy.34
  13.5 0.1 reduce-window.8
  13.6 0.1 reduce
  13.7 0.2 select_reduce_fusion
  13.9 0.4 copy.35
  14.3 0.1 pad.10.clone
  14.3 0.1 pad.13.clone
  14.4 0.1 fusion.15
  14.5 0.6 pad_add_fusion.order_ref
  15.1 4.6 convert_reduce_fusion
  19.7 0.0 slice-start
  19.7 7.2 fusion.8
  27.0 0.6 slice_add_fusion
  27.6 1.1 subtract_subtract_fusion.start_ref
  28.7 3.7 multiply_sine_fusion
  32.4 0.1 broadcast_in_dim.57
  32.5 2.6 maximum_maximum_fusion.2
  35.1 8.6 fusion.7
  43.7 96.6 %all-gather.2.cloned.1.call-done.slots_ref = bf16[192,256,256]{2,1,0:T(8,128)(2,1)} async-done(((bf16[24,256,256]{2,1,0:T(8,128)(2,1)}), bf16[192,256,256]{2,1,0:T(8,128)(2,1)}) %all-gather.2.cloned.1.call-update) | async-done | bytes 25165840 | tf_op jit(solution)/shard_map/all_gather | solution.py:1037
  140.4 21.0 %place_blocks.1 = (bf16[2048,1536]{1,0:T(8,128)(2,1)}, bf16[2560,2048]{1,0:T(8,128)(2,1)}, bf16[2048,2048]{1,0:T(8,128)(2,1)}) custom-call(s32[192]{0:T(256)} %pad_add_fusion.order_ref, bf16[192,256,256]{2,1,0:T(8,128)(2,1)} %all-gather.2.cloned.1.call-done.slots_ref), custom_call_target="tpu_custom_call" | custom-call | tf_op jit(solution)/shard_map/place_blocks/pallas_call | solution.py:404
  161.4 9.9 %fusion.9.g_ref = bf16[2048,512]{1,0:T(8,128)(2,1)} fusion(bf16[2048,2048]{1,0:T(8,128)(2,1)} %g_ref.3, bf16[2560,2048]{1,0:T(8,128)(2,1)} %get-tuple-element.35.od_ref), kind=kOutput, calls=%fused_computation.19 | convolution fusion | flops 4296015872 | bytes 12582912 | tf_op jit(solution)/shard_map/td,id->ti/dot_general | solution.py:1070
  171.3 18.8 %project_qkv.1 = (bf16[2048,512]{1,0:T(8,128)(2,1)}, bf16[2048,512]{1,0:T(8,128)(2,1)}, bf16[2048,512]{1,0:T(8,128)(2,1)}) custom-call(bf16[2048,2048]{1,0:T(8,128)(2,1)} %get-tuple-element.56.h_ref, bf16[2048,1536]{1,0:T(8,128)(2,1)} %get-tuple-element.31.w_ref.qkv_ref, f32[1,1536]{1,0:T(1,128)} %slice.50.bias_ref, f32[2048,128]{1,0:T(8,128)} %get-tuple-element.72.cos_ref, ...), custom_call_target="tpu_custom_call" | custom-call | tf_op jit(solution)/shard_map/project_qkv/pallas_call | solution.py:490
  190.1 31.7 %attention_both.1 = (bf16[2048,512]{1,0:T(8,128)(2,1)}, bf16[2048,1536]{1,0:T(8,128)(2,1)}) custom-call(s32[2048,1]{1,0:T(8,128)} %subtract_subtract_fusion.start_ref, bf16[2048,512]{1,0:T(8,128)(2,1)} %get-tuple-element.32.q_ref, bf16[2048,512]{1,0:T(8,128)(2,1)} %get-tuple-element.33.k_ref, bf16[2048,512]{1,0:T(8,128)(2,1)} %get-tuple-element.34.v_ref, ...), custom_call_target="tpu_custom_call" | custom-call | flops 12884901888 | bytes 31457280 | tf_op jit(solution)/shard_map/attention_both/pallas_call | solution.py:594
  221.8 19.2 %convolution_convert_fusion.2.refs_0_ = bf16[2048,1536]{1,0:T(8,128)(2,1)} fusion(bf16[2048,2048]{1,0:T(8,128)(2,1)} %get-tuple-element.56.h_ref, bf16[2048,1536]{1,0:T(8,128)(2,1)} %get-tuple-element.42.qg_ref), kind=kOutput, calls=%fused_computation.16 | convolution fusion | flops 12888047616 | bytes 20971520 | tf_op jit(solution)/shard_map/dot_general | solution.py:1078
  241.1 9.1 convolution_convert_fusion.3.refs_1_
  250.2 259.4 %forward_line.1 = (bf16[2048,2048]{1,0:T(8,128)(2,1)}, bf16[2048,2048]{1,0:T(8,128)(2,1)}, bf16[2048,2048]{1,0:T(8,128)(2,1)}) custom-call(bf16[2048,2048]{1,0:T(8,128)(2,1)} %get-tuple-element.57.h_ref, bf16[2048,2048]{1,0:T(8,128)(2,1)} %g_ref.3, bf16[2048,512]{1,0:T(8,128)(2,1)} %get-tuple-element.36.ctx_ref, bf16[2048,2048]{1,0:T(8,128)(2,1)} %x_ref.3, ...), custom_call_target="tpu_custom_call" | custom-call | flops 199999995904 | bytes 83886080 | tf_op jit(solution)/shard_map/forward_line/pallas_call | solution.py:853
  509.6 0.0 copy-start
  509.6 23.8 %convolution_convert_fusion.1.refs_2_ = bf16[2048,2048]{1,0:T(8,128)(2,1)} fusion(bf16[2048,2048]{1,0:T(8,128)(2,1)} %get-tuple-element.57.h_ref, bf16[2048,2048]{1,0:T(8,128)(2,1)} %get-tuple-element.43.hg_ref), kind=kOutput, calls=%fused_computation.15 | convolution fusion | flops 17184063488 | bytes 25165824 | tf_op jit(solution)/shard_map/dot_general | solution.py:1078
  533.4 21.0 %convolution_convert_fusion.refs_3_ = bf16[2048,2048]{1,0:T(8,128)(2,1)} fusion(bf16[2048,2048]{1,0:T(8,128)(2,1)S(1)} %copy-done.17, bf16[2048,2048]{1,0:T(8,128)(2,1)S(1)} %copy-done), kind=kOutput, calls=%fused_computation.14 | convolution fusion | flops 17184063488 | bytes 25165824 | tf_op jit(solution)/shard_map/dot_general | solution.py:1078
  554.4 21.2 %unplace_blocks.1 = bf16[192,256,256]{2,1,0:T(8,128)(2,1)} custom-call(s32[192]{0:T(256)} %order_ref.1, bf16[2048,1536]{1,0:T(8,128)(2,1)} %convolution_convert_fusion.2.refs_0_, bf16[512,2048]{1,0:T(8,128)(2,1)} %convolution_convert_fusion.3.refs_1_, bf16[2048,2048]{1,0:T(8,128)(2,1)} %convolution_convert_fusion.1.refs_2_, ...), custom_call_target="tpu_custom_call" | custom-call | tf_op jit(solution)/shard_map/unplace_blocks/pallas_call | solution.py:437
  575.6 0.0 copy-start.8
  575.6 0.0 copy-start.12
  575.6 0.0 reduce-scatter.2.cloned.1.call-update
  575.7 0.7 copy-done.8
  576.3 0.6 reduce.2
  577.0 0.6 multiply_reduce_fusion
  577.6 6.1 convert_reduce_fusion.2
  583.7 253.9 %backward_line.1 = (f32[8,2048]{1,0:T(8,128)}, bf16[2048,2048]{1,0:T(8,128)(2,1)}) custom-call(bf16[2048,1536]{1,0:T(8,128)(2,1)} %get-tuple-element.42.qg_ref, bf16[2048,2048]{1,0:T(8,128)(2,1)} %get-tuple-element.43.hg_ref, bf16[2048,2048]{1,0:T(8,128)(2,1)} %x_ref.3, bf16[2048,2048]{1,0:T(8,128)(2,1)} %g_ref.3, ...), custom_call_target="tpu_custom_call" | custom-call | flops 199999995904 | bytes 62914560 | tf_op jit(solution)/shard_map/backward_line/pallas_call | solution.py:950
  837.6 0.0 copy-start.11
  837.6 0.0 copy-start.5
  837.6 0.0 copy-start.6
  837.6 0.0 copy-start.2
  837.6 0.0 copy-start.3
  837.6 0.9 slice.55
  838.5 17.4 %psum.21 = f32[4,2048]{1,0:T(4,128)S(1)} all-reduce(f32[4,2048]{1,0:T(4,128)S(1)} %slice.55), channel_id=1, replica_groups=mesh['dp'=8,'mp'=4] {'mp'}, use_global_device_ids=true, to_apply=%region_5.6 | all-reduce | flops 8192 | bytes 65536 | tf_op jit(solution)/shard_map/psum | solution.py:1108
  855.9 3.7 convert_reduce_fusion.3
  859.6 4.7 convert_reduce_fusion.1
  864.4 23.6 %all-reduce = (f32[6,2048]{1,0:T(8,128)S(1)}, f32[3584]{0:T(1024)S(1)}) all-reduce(f32[6,2048]{1,0:T(8,128)S(1)} %pad_maximum_fusion, f32[3584]{0:T(1024)S(1)} %pad_maximum_fusion.1), channel_id=1, replica_groups=mesh['dp'=8,'mp'=4] {'dp'}, use_global_device_ids=true, to_apply=%region_7.8 | all-reduce | flops 15872 | bytes 126976 | tf_op jit(solution)/shard_map/psum | solution.py:1110
  888.0 0.0 copy-start.4
  888.0 0.6 broadcast_in_dim.63
  888.7 0.6 broadcast_in_dim.64
  889.3 0.6 broadcast_in_dim.65
  889.9 0.7 multiply_subtract_fusion
  890.6 24.6 %shampoo.1 = (f32[24,256,256]{2,1,0:T(8,128)}, f32[24,256,256]{2,1,0:T(8,128)}, f32[24,256,256]{2,1,0:T(8,128)}, f32[24,256,256]{2,1,0:T(8,128)}) custom-call(bf16[24,256,256]{2,1,0:T(8,128)(2,1)} %reduce-scatter.2.cloned.1.call-done.g_ref, f32[24,256,256]{2,1,0:T(8,128)} %bitcast.31, f32[24,256,256]{2,1,0:T(8,128)} %bitcast.32, f32[24,256,256]{2,1,0:T(8,128)} %bitcast.33, ...), custom_call_target="tpu_custom_call" | custom-call | tf_op jit(solution)/shard_map/shampoo/pallas_call | solution.py:1004
  915.2 8.4 copy.40
  923.6 8.4 copy.41
  (39 shorter events, 0.1 us)
Async XLA Ops:
  7.2 5.1 copy-start.7
  7.2 6.2 copy-start.14
  7.2 6.2 copy-start.15
  7.2 7.2 copy-start.13
  7.2 133.1 %all-gather.2.cloned.1.call-start = ((), (), s32[]{:S(2)}) async-start(), calls=%async_computation.1 | async-start | bytes 28311552 | tf_op jit(solution)/shard_map/all_gather | solution.py:1037
  12.2 878.4 %reduce-scatter.2.cloned.1.call-start = ((), (), s32[]{:S(2)}) async-start(), calls=%async_computation.2 | async-start | bytes 28311552 | tf_op jit(solution)/shard_map/reduce_scatter | solution.py:1087
  15.1 11.8 %copy-start.1 = (f32[6,2048]{1,0:T(8,128)S(1)}, f32[6,2048]{1,0:T(8,128)}, u32[]{:S(2)}) copy-start(f32[6,2048]{1,0:T(8,128)} %param.24) | copy-start | bytes 147460
  19.7 15.4 %slice-start = ((s8[8388608]{0:T(1024)(128)(4,1)}), s8[4194304]{0:T(1024)(128)(4,1)S(1)}, s32[]{:S(2)}) async-start(s8[8388608]{0:T(1024)(128)(4,1)} %bitcast.29), calls=%async_computation.3 | async-start | bytes 8388608
  27.6 7.5 copy-start.9
  27.6 7.5 copy-start.10
  27.6 7.5 slice-start.1
  221.8 19.2 %copy-start.16 = (bf16[2048,512]{1,0:T(8,128)(2,1)S(1)}, bf16[2048,512]{1,0:T(8,128)(2,1)}, u32[]{:S(2)}) copy-start(bf16[2048,512]{1,0:T(8,128)(2,1)} %get-tuple-element.36.ctx_ref) | copy-start | bytes 6291460
  509.6 23.8 %copy-start = (bf16[2048,2048]{1,0:T(8,128)(2,1)S(1)}, bf16[2048,2048]{1,0:T(8,128)(2,1)}, u32[]{:S(2)}) copy-start(bf16[2048,2048]{1,0:T(8,128)(2,1)} %g_ref.3) | copy-start | bytes 25165828
  509.6 23.8 %copy-start.17 = (bf16[2048,2048]{1,0:T(8,128)(2,1)S(1)}, bf16[2048,2048]{1,0:T(8,128)(2,1)}, u32[]{:S(2)}) copy-start(bf16[2048,2048]{1,0:T(8,128)(2,1)} %get-tuple-element.41) | copy-start | bytes 25165828
  575.6 0.7 copy-start.8
  575.6 1.3 copy-start.12
  837.6 26.8 %copy-start.11 = (f32[2048]{0:T(1024)S(1)}, f32[2048]{0:T(1024)}, u32[]{:S(2)}) copy-start(f32[2048]{0:T(1024)} %convert_reduce_fusion.2) | copy-start | bytes 24580
  837.6 51.1 %copy-start.5 = (f32[3584]{0:T(1024)S(1)}, f32[3584]{0:T(1024)}, u32[]{:S(2)}) copy-start(f32[3584]{0:T(1024)} %reduce.2) | copy-start | bytes 43012
  837.6 51.0 %copy-start.6 = (f32[3584]{0:T(1024)S(1)}, f32[3584]{0:T(1024)}, u32[]{:S(2)}) copy-start(f32[3584]{0:T(1024)} %multiply_reduce_fusion) | copy-start | bytes 43012
  837.6 52.3 %copy-start.2 = (f32[6,2048]{1,0:T(8,128)S(1)}, f32[6,2048]{1,0:T(8,128)}, u32[]{:S(2)}) copy-start(f32[6,2048]{1,0:T(8,128)} %param.24) | copy-start | bytes 147460
  837.6 52.3 %copy-start.3 = (f32[6,2048]{1,0:T(8,128)S(1)}, f32[6,2048]{1,0:T(8,128)}, u32[]{:S(2)}) copy-start(f32[6,2048]{1,0:T(8,128)} %param.25) | copy-start | bytes 147460
  888.0 27.1 %copy-start.4 = (f32[6,2048]{1,0:T(8,128)}, f32[6,2048]{1,0:T(8,128)S(1)}, u32[]{:S(2)}) copy-start(f32[6,2048]{1,0:T(8,128)S(1)} %get-tuple-element.91) | copy-start | bytes 147460
Sparse Core Ops, SparseCore 0:
  12.3 128.0 all-gather.1
  575.8 155.9 reduce-scatter.1

commit v2 on v1

--- a/solution.py
+++ b/solution.py
@@ -339,6 +339,7 @@
 PAIRS = 16
 STEPS = 8
 VMEM_BYTES = 60 * 1024 * 1024
+FORWARD_VMEM = 63 * 1024 * 1024
 
 
 def dot(left, right):
@@ -504,12 +505,14 @@
     q_ref,
     k_ref,
     v_ref,
-    g_ref,
+    cot_ref,
+    out_ref,
     cos_ref,
     high_ref,
     low_ref,
     ctx_ref,
     grad_ref,
+    sums_ref,
     p_scr,
     dp_scr,
     dk_scr,
@@ -526,7 +529,7 @@
 
     def rows(c):
         q = q_ref[...]
-        g = g_ref[...]
+        g = dot_nt(cot_ref[...], out_ref[...]).astype(LOW)
         first = start_ref[...]
         top = jnp.full((tile, 1), masked_score, WIDE)
         for j in range(c + 1):
@@ -582,10 +585,13 @@
         grad_ref[:, HD : HD + 128] = front.astype(LOW)
         grad_ref[:, HD + 128 : 2 * HD] = dk[:, 128:].astype(LOW)
         grad_ref[:, 2 * HD :] = dv_scr[...].astype(LOW)
-
-
-def attention_both(start, q, k, v, ctx_grad, tables):
+        total = jnp.sum(grad_ref[...].astype(WIDE), axis=0, keepdims=True)
+        sums_ref[...] = jnp.broadcast_to(total, sums_ref.shape)
+
+
+def attention_both(start, q, k, v, cotangent, od_w, tables):
     rows, cols = q.shape
+    d = cotangent.shape[1]
     heads = cols // HD
     tile = 512
     tile_spec = pl.BlockSpec((tile, HD), lambda h, i: (i, h))
@@ -594,12 +600,24 @@
     return pl.pallas_call(
         functools.partial(attention_kernel, tile),
         grid=(heads, rows // tile),
-        in_specs=[pl.BlockSpec((tile, 1), lambda h, i: (i, 0)), tile_spec, full_spec, full_spec, tile_spec]
+        in_specs=[
+            pl.BlockSpec((tile, 1), lambda h, i: (i, 0)),
+            tile_spec,
+            full_spec,
+            full_spec,
+            pl.BlockSpec((tile, d), lambda h, i: (i, 0)),
+            pl.BlockSpec((HD, d), lambda h, i: (h, 0)),
+        ]
         + [resident((rows, 128))] * 3,
-        out_specs=[tile_spec, pl.BlockSpec((rows, 3 * HD), lambda h, i: (0, h))],
+        out_specs=[
+            tile_spec,
+            pl.BlockSpec((rows, 3 * HD), lambda h, i: (0, h)),
+            pl.BlockSpec((8, 3 * HD), lambda h, i: (0, h)),
+        ],
         out_shape=[
             jax.ShapeDtypeStruct((rows, cols), LOW),
             jax.ShapeDtypeStruct((rows, 3 * cols), LOW),
+            jax.ShapeDtypeStruct((8, 3 * cols), WIDE),
         ],
         scratch_shapes=[
             pltpu.VMEM((tile, rows), WIDE),
@@ -610,7 +628,7 @@
         compiler_params=pltpu.CompilerParams(vmem_limit_bytes=VMEM_BYTES),
         cost_estimate=pl.CostEstimate(flops=flops, bytes_accessed=30 << 20, transcendentals=0),
         name="attention_both",
-    )(start, q, k, v, ctx_grad, *tables)
+    )(start, q, k, v, cotangent, od_w, *tables)
 
 
 class Line:
@@ -734,25 +752,18 @@
                 self.down(pair).wait_recv()
                 self.relay(pair).wait_recv()
 
-    def tick(self, step, base_of):
-        @pl.when(self.inner & (step >= 1) & (step < STEPS + 1))
+    def tick(self, step, lag, base):
+        @pl.when(self.inner & (step >= lag + 2) & (step < lag + 2 + PAIRS))
         def _():
-            for s in range(2):
-                self.add_far((step - 1) * 2 + s)
-
-        @pl.when(self.inner & (step >= 2) & (step < STEPS + 2))
+            self.send_relay(step - lag - 2)
+
+        @pl.when(self.inner & (step >= lag + 1) & (step < lag + 1 + PAIRS))
         def _():
-            for s in range(2):
-                offset = pl.multiple_of(s * 2 * SUB + self.near * SUB, SUB)
-                self.finish_near((step - 2) * 2 + s, base_of(offset))
-
-        @pl.when(self.inner & (step >= 3) & (step < STEPS + 3))
+            self.finish_near(step - lag - 1, base())
+
+        @pl.when(self.inner & (step >= lag) & (step < lag + PAIRS))
         def _():
-            for s in range(2):
-                self.send_relay((step - 3) * 2 + s)
-
-
-LINE_STEPS = STEPS + 3
+            self.add_far(step - lag)
 
 
 def line_scratch(d):
@@ -768,12 +779,16 @@
     return jnp.minimum(step, STEPS - 1)
 
 
-def later(step):
-    return jnp.clip(step - 2, 0, STEPS - 1)
-
-
-def row_block(width, at):
-    return pl.BlockSpec((STEP, width), lambda i: (at(i), 0))
+def row_block(width):
+    return pl.BlockSpec((STEP, width), lambda i: (now(i), 0))
+
+
+def base_block(width, lag):
+    return pl.BlockSpec((2 * SUB, width), lambda i: (jnp.clip(i - lag - 1, 0, PAIRS - 1), 0))
+
+
+def lane(start):
+    return pl.ds(pl.multiple_of(start, B), B)
 
 
 def gelu_parts(z):
@@ -796,88 +811,357 @@
     part_ref[pl.ds(step * 2, 2), :, :, cols] = value.astype(LOW).reshape(2, 2, SUB, value.shape[1])
 
 
+FORWARD_LAG = 2
+FORWARD_GRID = FORWARD_LAG + PAIRS + 2
+
+
+def weight_unit(a_t, b_ref, cols, stage, slot):
+    for n in range(cols // 512):
+        part = slice(n * 512, (n + 1) * 512)
+        stage[pl.ds(pl.multiple_of(slot * B, B), B), part] = dot(a_t, b_ref[:, part]).astype(LOW)
+
+
 def forward_kernel(
     h_ref,
     g_ref,
     ctx_ref,
     x_ref,
-    up_ref,
-    od_ref,
     bias_ref,
     shift_ref,
-    act_ref,
-    hg_ref,
+    up_hbm,
+    od_hbm,
+    h1_hbm,
+    h2_hbm,
+    ctx_hbm,
+    cot_hbm,
+    qg_hbm,
     out_ref,
+    hg_hbm,
+    wq_hbm,
+    wo_hbm,
+    wu_hbm,
+    sums_ref,
+    up_buf,
+    od_buf,
+    act_all,
+    hg_all,
     part,
     got,
     across,
     sems,
+    load_sem,
+    panel_sem,
+    stage_sem,
+    hg_sem,
 ):
     step = pl.program_id(0)
     line = Line(out_ref, part, got, across, sems)
     heads = ctx_ref.shape[1]
+    rows, units = act_all.shape
+    qkv_cols = qg_hbm.shape[1]
     width = 512
+    tiles = units // width
+    stage = od_buf.at[pl.ds(rows, 2 * B), :]
+
+    def load_up(n):
+        cols = pl.ds(n * width, width)
+        return pltpu.make_async_copy(up_hbm.at[:, cols], up_buf.at[:, cols], load_sem.at[n])
+
+    def load_down(n):
+        part_rows = pl.ds(heads + n * width, width)
+        return pltpu.make_async_copy(
+            od_hbm.at[part_rows, :], od_buf.at[part_rows, :], load_sem.at[tiles + n]
+        )
+
+    def load_out():
+        part_rows = pl.ds(0, heads)
+        return pltpu.make_async_copy(
+            od_hbm.at[part_rows, :], od_buf.at[part_rows, :], load_sem.at[2 * tiles]
+        )
+
+    def load_cot():
+        return pltpu.make_async_copy(
+            cot_hbm, od_buf.at[pl.ds(0, rows), :], load_sem.at[2 * tiles + 1]
+        )
+
+    def load_qg():
+        return pltpu.make_async_copy(
+            qg_hbm, up_buf.at[:, pl.ds(0, qkv_cols)], load_sem.at[2 * tiles + 2]
+        )
+
+    def panel_cols(slot):
+        return lane(qkv_cols + slot * B)
+
+    def panel(src, i, slot):
+        return pltpu.make_async_copy(
+            src.at[:, lane(i * B)], up_buf.at[:, panel_cols(slot)], panel_sem.at[slot]
+        )
+
+    def store_hg(i):
+        part_rows = pl.ds(pl.multiple_of(i * STEP, STEP), STEP)
+        return pltpu.make_async_copy(
+            hg_all.at[part_rows, :], hg_hbm.at[part_rows, :], hg_sem.at[i]
+        )
+
+    def stage_out(dst, row, cols, slot):
+        return pltpu.make_async_copy(
+            stage.at[lane(slot * B), pl.ds(0, cols)],
+            dst.at[lane(row), :],
+            stage_sem.at[slot],
+        )
 
     @pl.when(step == 0)
     def _():
+        for n in range(tiles):
+            load_up(n).start()
+            load_down(n).start()
+        load_out().start()
         line.greet()
+        sums_ref[...] = jnp.zeros_like(sums_ref)
 
     @pl.when(step < STEPS)
     def _():
-        for n in range(up_ref.shape[1] // width):
+        here = pl.ds(pl.multiple_of(step * STEP, STEP), STEP)
+        for n in range(tiles):
             cols = slice(n * width, (n + 1) * width)
-            hidden = dot(h_ref[...], up_ref[:, cols]) + bias_ref[:, cols]
-            act_grad = dot_nt(g_ref[...], od_ref[heads + n * width : heads + (n + 1) * width, :])
+
+            @pl.when(step == 0)
+            def _():
+                load_up(n).wait()
+                load_down(n).wait()
+
+            hidden = dot(h_ref[...], up_buf[:, cols]) + bias_ref[:, cols]
+            act_grad = dot_nt(g_ref[...], od_buf[heads + n * width : heads + (n + 1) * width, :])
             cdf, density = gelu_parts(hidden)
-            act_ref[:, cols] = (hidden * cdf).astype(LOW)
-            hg_ref[:, cols] = (act_grad * (cdf + hidden * density)).astype(LOW)
-        for n in range(od_ref.shape[1] // width):
+            act_all[here, cols] = (hidden * cdf).astype(LOW)
+            grad = (act_grad * (cdf + hidden * density)).astype(LOW)
+            hg_all[here, cols] = grad
+            sums_ref[0:1, cols] += jnp.sum(grad.astype(WIDE), axis=0, keepdims=True)
+
+        @pl.when(step == 0)
+        def _():
+            load_out().wait()
+
+        store_hg(step).start()
+        for n in range(od_buf.shape[1] // width):
             cols = slice(n * width, (n + 1) * width)
-            value = dot(ctx_ref[...], od_ref[:heads, cols]) + dot(act_ref[...], od_ref[heads:, cols])
+            value = dot(ctx_ref[...], od_buf[:heads, cols]) + dot(
+                act_all[here, :], od_buf[heads:, cols]
+            )
             store_part(part, step, cols, value)
         for s in range(2):
             line.send_up(step * 2 + s)
 
-    line.tick(
-        step, lambda offset: x_ref[pl.ds(offset, SUB), :].astype(WIDE) + shift_ref[...]
-    )
-
-    @pl.when(step == LINE_STEPS - 1)
+    @pl.when(step == STEPS - 1)
+    def _():
+        panel(h2_hbm, 0, 0).start()
+        load_cot().start()
+        load_qg().start()
+
+    def unit(index, a_t, b_ref, cols, dst, row):
+        slot = index % 2
+
+        @pl.when(index >= 2)
+        def _():
+            stage_out(dst, row, cols, slot).wait()
+
+        weight_unit(a_t, b_ref, cols, stage, slot)
+        stage_out(dst, row, cols, slot).start()
+
+    def settle(dst, cols):
+        for slot in range(2):
+            stage_out(dst, 0, cols, slot).wait()
+
+    @pl.when((step == 8) | (step == 9))
+    def _():
+        @pl.loop(0, 4)
+        def _(k):
+            i = (step - 8) * 4 + k
+            panel(h2_hbm, i, i % 2).wait()
+
+            @pl.when(i < 7)
+            def _():
+                panel(h2_hbm, i + 1, (i + 1) % 2).start()
+
+            unit(i, up_buf[:, panel_cols(i % 2)].T, hg_all, units, wu_hbm, i * B)
+
+    @pl.when(step == 10)
+    def _():
+        settle(wu_hbm, units)
+        load_cot().wait()
+
+    @pl.when((step == 10) | (step == 11))
+    def _():
+        @pl.loop(0, 4)
+        def _(k):
+            i = (step - 10) * 4 + k
+            cot = od_buf.at[pl.ds(0, rows), :]
+            unit(i, act_all[:, lane(i * B)].T, cot, units, wo_hbm, heads + i * B)
+
+    @pl.when(step == 12)
+    def _():
+        settle(wo_hbm, units)
+        for j in range(2):
+            panel(ctx_hbm, j, j).start()
+        load_qg().wait()
+        for j in range(2):
+            panel(ctx_hbm, j, j).wait()
+
+        @pl.loop(0, 2)
+        def _(j):
+            cot = od_buf.at[pl.ds(0, rows), :]
+            unit(j, up_buf[:, panel_cols(j)].T, cot, units, wo_hbm, j * B)
+
+        settle(wo_hbm, units)
+        panel(h1_hbm, 0, 0).start()
+
+    @pl.when((step == 13) | (step == 14))
+    def _():
+        @pl.loop(0, 4)
+        def _(k):
+            i = (step - 13) * 4 + k
+            panel(h1_hbm, i, i % 2).wait()
+
+            @pl.when(i < 7)
+            def _():
+                panel(h1_hbm, i + 1, (i + 1) % 2).start()
+
+            grads = up_buf.at[:, pl.ds(0, qkv_cols)]
+            unit(i, up_buf[:, panel_cols(i % 2)].T, grads, qkv_cols, wq_hbm, i * B)
+
+    @pl.when(step == 15)
+    def _():
+        settle(wq_hbm, qkv_cols)
+
+        @pl.loop(0, STEPS)
+        def _(i):
+            store_hg(i).wait()
+
+    def base():
+        near = pl.ds(pl.multiple_of(line.near * SUB, SUB), SUB)
+        return x_ref[near, :].astype(WIDE) + shift_ref[...]
+
+    line.tick(step, FORWARD_LAG, base)
+
+    @pl.when(step == FORWARD_GRID - 1)
     def _():
         line.drain()
 
 
-def forward_line(h2, cotangent, ctx, tokens, up_w, od_w, bias, shift):
+def forward_line(h1, h2, cotangent, ctx, qkv_grad, tokens, up_w, od_w, bias, shift):
     rows, d = tokens.shape
     units = up_w.shape[1]
+    qkv_cols = qkv_grad.shape[1]
     return pl.pallas_call(
         forward_kernel,
-        grid=(LINE_STEPS,),
+        grid=(FORWARD_GRID,),
         in_specs=[
-            row_block(d, now),
-            row_block(d, now),
-            row_block(ctx.shape[1], now),
-            row_block(d, later),
-            resident(up_w.shape),
-            resident(od_w.shape),
+            row_block(d),
+            row_block(d),
+            row_block(ctx.shape[1]),
+            base_block(d, FORWARD_LAG),
             resident(bias.shape),
             resident(shift.shape),
+        ]
+        + [ANY] * 7,
+        out_specs=[ANY] * 5 + [pl.BlockSpec((8, units), lambda i: (0, 0))],
+        out_shape=[
+            jax.ShapeDtypeStruct((rows, d), LOW),
+            jax.ShapeDtypeStruct((rows, units), LOW),
+            jax.ShapeDtypeStruct((d, qkv_cols), LOW),
+            jax.ShapeDtypeStruct(od_w.shape, LOW),
+            jax.ShapeDtypeStruct((d, units), LOW),
+            jax.ShapeDtypeStruct((8, units), WIDE),
         ],
-        out_specs=[row_block(units, now), row_block(units, now), ANY],
-        out_shape=[
-            jax.ShapeDtypeStruct((rows, units), LOW),
-            jax.ShapeDtypeStruct((rows, units), LOW),
-            jax.ShapeDtypeStruct((rows, d), LOW),
+        scratch_shapes=[
+            pltpu.VMEM(up_w.shape, LOW),
+            pltpu.VMEM(od_w.shape, LOW),
+            pltpu.VMEM((rows, units), LOW),
+            pltpu.VMEM((rows, units), LOW),
+        ]
+        + line_scratch(d)
+        + [
+            pltpu.SemaphoreType.DMA((11,)),
+            pltpu.SemaphoreType.DMA((2,)),
+            pltpu.SemaphoreType.DMA((2,)),
+            pltpu.SemaphoreType.DMA((STEPS,)),
         ],
-        scratch_shapes=line_scratch(d),
         compiler_params=pltpu.CompilerParams(
-            vmem_limit_bytes=VMEM_BYTES, collective_id=1, has_side_effects=True
+            vmem_limit_bytes=FORWARD_VMEM, collective_id=1, has_side_effects=True
         ),
         cost_estimate=pl.CostEstimate(
             flops=200_000_000_000, bytes_accessed=80 << 20, transcendentals=0
         ),
         name="forward_line",
-    )(h2, cotangent, ctx, tokens, up_w, od_w, bias, shift)
+    )(h2, cotangent, ctx, tokens, bias, shift, up_w, od_w, h1, h2, ctx, cotangent, qkv_grad)
+
+
+BACKWARD_LAG = 1
+BACKWARD_GRID = BACKWARD_LAG + PAIRS + 2
+
+
+class Spread:
+    def __init__(self, own, along_mp, along_dp, sems):
+        self.own = own
+        self.stages = [
+            ("dp", along_dp, sems.at[0], sems.at[1]),
+            ("mp", along_mp, sems.at[2], sems.at[3]),
+        ]
+
+    def others(self, stage):
+        axis, buf, send, recv = self.stages[stage]
+        me = lax.axis_index(axis)
+        return axis, buf, send, recv, me, [lax.rem(me + k, buf.shape[0]) for k in range(1, buf.shape[0])]
+
+    def greet(self):
+        barrier = pltpu.get_barrier_semaphore()
+        count = 0
+        for stage in range(2):
+            axis, _, _, _, _, others = self.others(stage)
+            for other in others:
+                pl.semaphore_signal(barrier, inc=1, device_id={axis: other}, device_id_type=MESH)
+            count += len(others)
+        pl.semaphore_wait(barrier, count)
+
+    def copies(self, stage):
+        axis, buf, send, recv, me, others = self.others(stage)
+        return [
+            (
+                pltpu.make_async_remote_copy(
+                    src_ref=self.own,
+                    dst_ref=buf.at[me],
+                    send_sem=send.at[k],
+                    recv_sem=recv.at[me],
+                    device_id={axis: other},
+                    device_id_type=MESH,
+                ),
+                pltpu.make_async_remote_copy(
+                    src_ref=self.own,
+                    dst_ref=buf.at[other],
+                    send_sem=send.at[k],
+                    recv_sem=recv.at[other],
+                    device_id={axis: other},
+                    device_id_type=MESH,
+                ),
+            )
+            for k, other in enumerate(others)
+        ]
+
+    def start(self, stage):
+        _, buf, _, _, me, _ = self.others(stage)
+        buf[me] = self.own[...]
+        for out, _ in self.copies(stage):
+            out.start()
+
+    def finish(self, stage):
+        _, buf, _, _, _, _ = self.others(stage)
+        for out, back in self.copies(stage):
+            out.wait_send()
+            back.wait_recv()
+        total = buf[0]
+        for i in range(1, buf.shape[0]):
+            total = total + buf[i]
+        return total
 
 
 def backward_kernel(
@@ -889,10 +1173,15 @@
     up_ref,
     one_ref,
     two_ref,
-    norm_ref,
+    sums_in,
+    sums_ref,
     out_ref,
     gc_scr,
     xhat_scr,
+    own,
+    along_mp,
+    along_dp,
+    spread_sems,
     part,
     got,
     across,
@@ -900,13 +1189,14 @@
 ):
     step = pl.program_id(0)
     line = Line(out_ref, part, got, across, sems)
+    spread = Spread(own, along_mp, along_dp, spread_sems)
     d = x_ref.shape[1]
     width = 512
 
     @pl.when(step == 0)
     def _():
-        line.greet()
-        norm_ref[...] = jnp.zeros_like(norm_ref)
+        spread.greet()
+        own[...] = sums_in[...]
 
     @pl.when(step < STEPS)
     def _():
@@ -925,10 +1215,10 @@
             gc_scr[:, cols] = gc
             mean = mean + jnp.sum(gc, axis=1, keepdims=True)
             slope = slope + jnp.sum(gc * xhat, axis=1, keepdims=True)
-            norm_ref[0:1, cols] += jnp.sum(e1 * xhat, axis=0, keepdims=True)
-            norm_ref[1:2, cols] += jnp.sum(e1, axis=0, keepdims=True)
-            norm_ref[2:3, cols] += jnp.sum(e2 * xhat, axis=0, keepdims=True)
-            norm_ref[3:4, cols] += jnp.sum(e2, axis=0, keepdims=True)
+            own[0:1, cols] += jnp.sum(e1 * xhat, axis=0, keepdims=True)
+            own[1:2, cols] += jnp.sum(e1, axis=0, keepdims=True)
+            own[2:3, cols] += jnp.sum(e2 * xhat, axis=0, keepdims=True)
+            own[3:4, cols] += jnp.sum(e2, axis=0, keepdims=True)
         mean = mean * (1.0 / d)
         slope = slope * (1.0 / d)
         for n in range(d // width):
@@ -938,31 +1228,57 @@
         for s in range(2):
             line.send_up(step * 2 + s)
 
-    line.tick(step, lambda offset: g_ref[pl.ds(offset, SUB), :].astype(WIDE))
-
-    @pl.when(step == LINE_STEPS - 1)
+    @pl.when(step == STEPS)
+    def _():
+        spread.start(0)
+
+    @pl.when(step == STEPS + 4)
+    def _():
+        own[...] = spread.finish(0)
+        spread.start(1)
+
+    def base():
+        near = pl.ds(pl.multiple_of(line.near * SUB, SUB), SUB)
+        return g_ref[near, :].astype(WIDE)
+
+    line.tick(step, BACKWARD_LAG, base)
+
+    @pl.when(step == BACKWARD_GRID - 1)
     def _():
         line.drain()
-
-
-def backward_line(qkv_grad, hidden_grad, tokens, cotangent, qkv_w, up_w, gain_one, gain_two):
+        total = spread.finish(1)
+        row = lax.broadcasted_iota(jnp.int32, total.shape, 0)
+        sums_ref[...] = jnp.where(row < 4, total, own[...])
+
+
+def backward_line(qkv_grad, hidden_grad, tokens, cotangent, qkv_w, up_w, gain_one, gain_two, sums):
     rows, d = tokens.shape
+    small = sums.shape
     return pl.pallas_call(
         backward_kernel,
-        grid=(LINE_STEPS,),
+        grid=(BACKWARD_GRID,),
         in_specs=[
-            row_block(qkv_grad.shape[1], now),
-            row_block(hidden_grad.shape[1], now),
-            row_block(d, now),
-            row_block(d, later),
+            row_block(qkv_grad.shape[1]),
+            row_block(hidden_grad.shape[1]),
+            row_block(d),
+            base_block(d, BACKWARD_LAG),
             resident(qkv_w.shape),
             resident(up_w.shape),
             resident((1, d)),
             resident((1, d)),
+            resident(small),
         ],
-        out_specs=[pl.BlockSpec((8, d), lambda i: (0, 0)), ANY],
-        out_shape=[jax.ShapeDtypeStruct((8, d), WIDE), jax.ShapeDtypeStruct((rows, d), LOW)],
-        scratch_shapes=[pltpu.VMEM((STEP, d), WIDE), pltpu.VMEM((STEP, d), WIDE)] + line_scratch(d),
+        out_specs=[pl.BlockSpec(small, lambda i: (0, 0)), ANY],
+        out_shape=[jax.ShapeDtypeStruct(small, WIDE), jax.ShapeDtypeStruct((rows, d), LOW)],
+        scratch_shapes=[
+            pltpu.VMEM((STEP, d), WIDE),
+            pltpu.VMEM((STEP, d), WIDE),
+            pltpu.VMEM(small, WIDE),
+            pltpu.VMEM((4,) + small, WIDE),
+            pltpu.VMEM((8,) + small, WIDE),
+            pltpu.SemaphoreType.DMA((4, 8)),
+        ]
+        + line_scratch(d),
         compiler_params=pltpu.CompilerParams(
             vmem_limit_bytes=VMEM_BYTES, collective_id=2, has_side_effects=True
         ),
@@ -970,7 +1286,9 @@
             flops=200_000_000_000, bytes_accessed=60 << 20, transcendentals=0
         ),
         name="backward_line",
-    )(qkv_grad, hidden_grad, tokens, cotangent, qkv_w, up_w, gain_one, gain_two)
+    )(
+        qkv_grad, hidden_grad, tokens, cotangent, qkv_w, up_w, gain_one, gain_two, sums
+    )
 
 
 def halves(values):
@@ -979,8 +1297,45 @@
 
 
 def shampoo_kernel(
-    g_ref, w_ref, ls_ref, rs_ref, lr_ref, rr_ref, grad_ref, left_ref, right_ref, weight_ref
+    g_ref,
+    w_ref,
+    ls_ref,
+    rs_ref,
+    lr_ref,
+    rr_ref,
+    one_in,
+    two_in,
+    grad_ref,
+    left_ref,
+    right_ref,
+    weight_ref,
+    one_out,
+    two_out,
+    hold,
+    sems,
 ):
+    step = pl.program_id(0)
+    pairs = ((one_in, one_out), (two_in, two_out))
+    fetch = [pltpu.make_async_copy(a, hold.at[i], sems.at[0, i]) for i, (a, _) in enumerate(pairs)]
+    store = [pltpu.make_async_copy(hold.at[i], b, sems.at[1, i]) for i, (_, b) in enumerate(pairs)]
+
+    @pl.when(step == 0)
+    def _():
+        for copy in fetch:
+            copy.start()
+
+    for i in range(2):
+
+        @pl.when(step == pl.num_programs(0) * (i + 1) // 3)
+        def _():
+            fetch[i].wait()
+            store[i].start()
+
+    @pl.when(step == pl.num_programs(0) - 1)
+    def _():
+        for copy in store:
+            copy.wait()
+
     for n in range(g_ref.shape[0]):
         g = g_ref[n]
         grad_ref[n] = g.astype(WIDE)
@@ -997,19 +1352,24 @@
         weight_ref[n] = weight - direction * (step_share * weight_size / step_size)
 
 
-def shampoo(grads, weights, left_stat, right_stat, left_root, right_root):
+def shampoo(grads, weights, left_stat, right_stat, left_root, right_root, one, two):
     count = grads.shape[0]
     group = 2
     spec = pl.BlockSpec((group, B, B), lambda i: (i, 0, 0))
     return pl.pallas_call(
         shampoo_kernel,
         grid=(count // group,),
-        in_specs=[spec] * 6,
-        out_specs=[spec] * 4,
-        out_shape=[jax.ShapeDtypeStruct((count, B, B), WIDE)] * 4,
+        in_specs=[spec] * 6 + [ANY] * 2,
+        out_specs=[spec] * 4 + [ANY] * 2,
+        out_shape=[jax.ShapeDtypeStruct((count, B, B), WIDE)] * 4
+        + [jax.ShapeDtypeStruct(one.shape, one.dtype)] * 2,
+        scratch_shapes=[
+            pltpu.VMEM((2,) + one.shape, one.dtype),
+            pltpu.SemaphoreType.DMA((2, 2)),
+        ],
         compiler_params=pltpu.CompilerParams(vmem_limit_bytes=VMEM_BYTES),
         name="shampoo",
-    )(grads, weights, left_stat, right_stat, left_root, right_root)
+    )(grads, weights, left_stat, right_stat, left_root, right_root, one, two)
 
 
 def per_device_line(
@@ -1051,7 +1411,8 @@
     inputs = tokens.astype(WIDE)
     normed_one = layer_norm(inputs, vectors[0], vectors[1]).astype(LOW)
     normed_two = layer_norm(inputs, vectors[2], vectors[3]).astype(LOW)
-    out_sum = jnp.sum(cotangent.astype(WIDE), axis=0)
+    out_sum = jnp.sum(cotangent.astype(WIDE), axis=0, keepdims=True)
+    normed_one, normed_two, out_sum = lax.optimization_barrier((normed_one, normed_two, out_sum))
     shift = (vectors[4] + vectors[5])[None]
     unit_shift = unit_bias[0]
 
@@ -1067,26 +1428,33 @@
     qkv_w, od_w, up_w = place_blocks(gathered, order, shapes)
 
     q, k, v = project_qkv(normed_one, qkv_w, unit_shift[None, :qkv_cols], tables)
-    ctx_grad = jnp.einsum(
-        "td,id->ti", cotangent, od_w[:head_cols], preferred_element_type=WIDE
-    ).astype(LOW)
-    ctx, qkv_grad = attention_both(start, q, k, v, ctx_grad, tables)
-    act, hidden_grad, block_out = forward_line(
-        normed_two, cotangent, ctx, tokens, up_w, od_w, unit_shift[None, qkv_cols:], shift
-    )
-    mats = [
-        lax.dot_general(a, b, (((0,), (0,)), ((), ())), preferred_element_type=WIDE).astype(LOW)
-        for a, b in (
-            (normed_one, qkv_grad),
-            (ctx, cotangent),
-            (normed_two, hidden_grad),
-            (act, cotangent),
-        )
-    ]
-    slots = unplace_blocks(mats, owner_map)
+    ctx, qkv_grad, qkv_sums = attention_both(start, q, k, v, cotangent, od_w, tables)
+    block_out, hidden_grad, qkv_wg, od_wg, up_wg, hidden_sums = forward_line(
+        normed_one,
+        normed_two,
+        cotangent,
+        ctx,
+        qkv_grad,
+        tokens,
+        up_w,
+        od_w,
+        unit_shift[None, qkv_cols:],
+        shift,
+    )
+    slots = unplace_blocks([qkv_wg, od_wg, up_wg], order)
     owned = lax.psum_scatter(slots, "dp", scatter_dimension=0, tiled=True)
     qkv_grad, hidden_grad, slots = lax.optimization_barrier((qkv_grad, hidden_grad, slots))
-    norm_part, input_grad = backward_line(
+    sums = jnp.concatenate(
+        [
+            jnp.zeros((4, d), WIDE),
+            out_sum,
+            jnp.pad(qkv_sums[:1], ((0, 0), (0, d - qkv_cols))),
+            jnp.pad(hidden_sums[:1], ((0, 0), (0, d - unit_cols))),
+            jnp.zeros((1, d), WIDE),
+        ],
+        axis=0,
+    )
+    sums, input_grad = backward_line(
         qkv_grad,
         hidden_grad,
         tokens,
@@ -1095,19 +1463,20 @@
         up_w,
         vectors[0:1],
         vectors[2:3],
-    )
-    block_grad, left_new, right_new, weight_new = shampoo(
-        owned, weight_blocks[0], left_stat[0], right_stat[0], left_root[0], right_root[0]
-    )
-    unit_part = jnp.concatenate(
-        [
-            jnp.sum(qkv_grad.astype(WIDE), axis=0),
-            jnp.sum(hidden_grad.astype(WIDE), axis=0),
-        ]
-    )
-    norm_sum = lax.psum(norm_part[:4], "mp")
-    vector_part = jnp.concatenate([norm_sum, jnp.stack([out_sum, out_sum])], axis=0)
-    vector_grad, unit_grad = lax.psum((vector_part, unit_part), "dp")
+        sums,
+    )
+    block_grad, left_new, right_new, weight_new, block_out, input_grad = shampoo(
+        owned,
+        weight_blocks[0],
+        left_stat[0],
+        right_stat[0],
+        left_root[0],
+        right_root[0],
+        block_out,
+        input_grad,
+    )
+    vector_grad = jnp.concatenate([sums[:5], sums[4:5]], axis=0)
+    unit_grad = jnp.concatenate([sums[5, :qkv_cols], sums[6, :unit_cols]])
     vector_stat_new, vector_new = vector_update(vectors, vector_stat, vector_grad)
     unit_stat_new, unit_new = vector_update(unit_shift, unit_stat[0], unit_grad)
     return (

time: 947 us -> 758 us (0.80)
  matrix products: 83 us -> 0 us
  blocking collectives: 41 us -> 0 us
  Pallas kernels: 631 us -> 598 us
  local copies, waits for them, and re-layouts: 22.3 us -> 6.74 us
    dot_general x5 -> x0, matrix products: 83 us -> none  [the longest x4 73.1 us: per_device_line(): lax.dot_general(a, b, (((0,), (0,)), ((), ())), preferred_element_type=WIDE)]
    pallas_call x2, Pallas kernels: 513 us -> 467 us  [the longest x1 235 us: forward_line(): pl.pallas_call(forward_kernel, grid=(FORWARD_GRID,), in_specs=[row_block(...]
    psum x2 -> x0, blocking collectives: 41 us -> none  [the longest x1 23.6 us: per_device_line(): vector_grad, unit_grad = lax.psum((vector_part, unit_part), 'dp')]
    unnamed x42 -> x28, local copies, waits for them, and re-layouts: 17.7 us -> 0.07 us
  transfers between devices with their start and end apart: 2 -> 2, of which waited for: 1 -> 1; matrix products, arithmetic and copies ran while one was open for 5% -> 6% of each run, Pallas kernels for 27% -> 31%
where the time goes in v2:
time: 758 us; the launch traced here: 753 us
  Pallas kernels  598 us (79%)
  waiting for transfers between devices  90.5 us (12%)
  other arithmetic  42.7 us (6%)
  between operations  14.5 us (2%)
    pallas_call x1, Pallas kernels, forward_line(): pl.pallas_call(forward_kernel, grid=(FORWARD_GRID,), in_specs=[row_block(...  235 us
    pallas_call x1, Pallas kernels, backward_line(): pl.pallas_call(backward_kernel, grid=(BACKWARD_GRID,), in_specs=[row_bloc...  231 us
    all_gather x1, waiting for transfers between devices, per_device_line(): lax.all_gather(weight_blocks[0].astype(LOW), 'dp', axis=0, tiled=True)  90.5 us
    pallas_call x1, Pallas kernels, attention_both(): pl.pallas_call(functools.partial(attention_kernel, tile), grid=(heads, ro...  37.8 us
    pallas_call x1, Pallas kernels, shampoo(): pl.pallas_call(shampoo_kernel, grid=(count // group,), in_specs=[spec] *...  32.8 us
    pallas_call x1, Pallas kernels, unplace_blocks(): pl.pallas_call(functools.partial(unplace_kernel, shapes), grid_spec=pltpu...  21.2 us
    pallas_call x1, Pallas kernels, place_blocks(): pl.pallas_call(functools.partial(place_kernel, shapes), grid_spec=pltpu.P...  21 us
    pallas_call x1, Pallas kernels, project_qkv(): pl.pallas_call(functools.partial(qkv_kernel, 1.0 / math.sqrt(HD)), grid=(...  18.8 us
  transfers between devices with their start and end apart: 2, of which 1 were waited for; matrix products, arithmetic and copies ran while one was open for 6% of the time, Pallas kernels for 31%

profile of v2, /device:TPU:0, one launch (start us, length us, event | category | flops | bytes accessed | tf_op | source)
XLA Modules:
  0.0 752.8 jit_solution(2773919096945557661)
XLA Ops:
  7.2 0.0 copy-start.3
  7.2 0.0 copy-start.11
  7.2 0.0 copy-start.10
  7.2 0.0 all-gather.2.cloned.1.call-start
  7.3 4.9 bitcast_convert_fusion
  12.1 0.0 all-gather.2.cloned.1.call-update
  12.2 0.0 reduce-scatter.2.cloned.1.call-start
  12.2 0.0 copy-done.3
  12.2 0.6 slice.62.bias_ref
  12.8 0.6 slice.63.bias_ref
  13.4 0.1 pad.16.clone
  13.5 0.1 pad.19.clone
  13.6 0.0 copy-done.11
  13.6 0.0 copy-done.10
  13.6 0.1 copy.31
  13.7 0.1 reduce-window.8
  13.7 0.1 reduce
  13.9 0.2 select_reduce_fusion
  14.0 0.4 copy.32
  14.4 0.0 copy-start
  14.4 4.6 convert_reduce_fusion
  19.0 0.0 slice-start
  19.0 6.6 fusion.8
  25.6 0.0 copy-done
  25.7 0.0 slice-start.1
  25.7 0.6 slice_add_fusion
  26.3 0.0 copy-start.6
  26.3 0.0 copy-start.7
  26.3 6.8 convert_reduce_fusion.1
  33.1 0.0 slice-done
  33.1 0.0 slice-done.1
  33.1 8.6 %fusion.7 = (bf16[2048,2048]{1,0:T(8,128)(2,1)}, bf16[2048,2048]{1,0:T(8,128)(2,1)}) fusion(bf16[2048,2048]{1,0:T(8,128)(2,1)S(1)} %bitcast.21, f32[2048]{0:T(1024)S(1)} %bitcast.33, f32[2048]{0:T(1024)S(1)} %bitcast.31, f32[2048]{0:T(1024)S(1)} %add_rsqrt_fusion, f32[2048]{0:T(1024)S(1)} %broadcast_multiply_fusion, f32[2048]{0:T(1024)S(1)} %bitcast.34, ...), kind=kLoop, calls=%fused_computation.9 | loop fusion | flops 37748736 | bytes 25214976 | tf_op jit(solution)/shard_map/convert_element_type | solution.py:1413
  41.7 0.0 copy-done.6
  41.7 0.0 copy-done.7
  41.8 0.0 copy-done.9
  41.8 0.1 fusion.16
  41.8 0.7 pad_add_fusion.order_ref
  42.5 1.1 subtract_subtract_fusion.start_ref
  43.6 3.7 multiply_sine_fusion
  47.3 0.1 broadcast_in_dim.63
  47.4 2.5 maximum_maximum_fusion.2
  49.9 90.5 %all-gather.2.cloned.1.call-done.slots_ref = bf16[192,256,256]{2,1,0:T(8,128)(2,1)} async-done(((bf16[24,256,256]{2,1,0:T(8,128)(2,1)}), bf16[192,256,256]{2,1,0:T(8,128)(2,1)}) %all-gather.2.cloned.1.call-update) | async-done | bytes 25165840 | tf_op jit(solution)/shard_map/all_gather | solution.py:1397
  140.3 21.0 %place_blocks.1 = (bf16[2048,1536]{1,0:T(8,128)(2,1)}, bf16[2560,2048]{1,0:T(8,128)(2,1)}, bf16[2048,2048]{1,0:T(8,128)(2,1)}) custom-call(s32[192]{0:T(256)} %pad_add_fusion.order_ref, bf16[192,256,256]{2,1,0:T(8,128)(2,1)} %all-gather.2.cloned.1.call-done.slots_ref), custom_call_target="tpu_custom_call" | custom-call | tf_op jit(solution)/shard_map/place_blocks/pallas_call | solution.py:405
  161.4 18.8 %project_qkv.1 = (bf16[2048,512]{1,0:T(8,128)(2,1)}, bf16[2048,512]{1,0:T(8,128)(2,1)}, bf16[2048,512]{1,0:T(8,128)(2,1)}) custom-call(bf16[2048,2048]{1,0:T(8,128)(2,1)} %get-tuple-element.41.h_ref.h1_hbm, bf16[2048,1536]{1,0:T(8,128)(2,1)} %get-tuple-element.42.w_ref.qkv_ref, f32[1,1536]{1,0:T(1,128)} %slice.62.bias_ref, ...), custom_call_target="tpu_custom_call" | custom-call | tf_op jit(solution)/shard_map/project_qkv/pallas_call | solution.py:491
  180.2 37.8 %attention_both.1 = (bf16[2048,512]{1,0:T(8,128)(2,1)}, bf16[2048,1536]{1,0:T(8,128)(2,1)}, f32[8,1536]{1,0:T(8,128)}) custom-call(s32[2048,1]{1,0:T(8,128)} %subtract_subtract_fusion.start_ref, bf16[2048,512]{1,0:T(8,128)(2,1)} %get-tuple-element.43.q_ref, bf16[2048,512]{1,0:T(8,128)(2,1)} %get-tuple-element.44.k_ref, ...), custom_call_target="tpu_custom_call" | custom-call | flops 12884901888 | bytes 31457280 | tf_op jit(solution)/shard_map/attention_both/pallas_call | solution.py:600
  218.0 235.5 %forward_line.1 = (bf16[2048,2048]{1,0:T(8,128)(2,1)}, bf16[2048,2048]{1,0:T(8,128)(2,1)}, bf16[2048,1536]{1,0:T(8,128)(2,1)}, bf16[2560,2048]{1,0:T(8,128)(2,1)...) custom-call(bf16[2048,2048]{1,0:T(8,128)(2,1)} %get-tuple-element.40.h_ref.h2_hbm, bf16[2048,2048]{1,0:T(8,128)(2,1)} %g_ref.3, ...), custom_call_target="tpu_custom_call" | custom-call | flops 199999995904 | bytes 83886080 | tf_op jit(solution)/shard_map/forward_line/pallas_call | solution.py:1055
  453.5 21.2 %unplace_blocks.1 = bf16[192,256,256]{2,1,0:T(8,128)(2,1)} custom-call(s32[192]{0:T(256)} %pad_add_fusion.order_ref, bf16[2048,1536]{1,0:T(8,128)(2,1)} %get-tuple-element.50.refs_0_, bf16[2560,2048]{1,0:T(8,128)(2,1)} %get-tuple-element.51.refs_1_, bf16[2048,2048]{1,0:T(8,128)(2,1)} %get-tuple-element.52.refs_2_), custom_call_target="tpu_custom_call" | custom-call | tf_op jit(solution)/shard_map/unplace_blocks/pallas_call | solution.py:438
  474.7 0.0 copy-start.5
  474.7 0.0 reduce-scatter.2.cloned.1.call-update
  474.8 0.8 slice.66
  475.6 0.8 slice.67
  476.4 0.0 copy-done.5
  476.5 0.7 concatenate.47.sums_in
  477.2 231.2 %backward_line.1 = (f32[8,2048]{1,0:T(8,128)}, bf16[2048,2048]{1,0:T(8,128)(2,1)}) custom-call(bf16[2048,1536]{1,0:T(8,128)(2,1)} %get-tuple-element.55.qg_hbm.qg_ref, bf16[2048,2048]{1,0:T(8,128)(2,1)} %get-tuple-element.56.hg_ref, bf16[2048,2048]{1,0:T(8,128)(2,1)} %x_ref.3, bf16[2048,2048]{1,0:T(8,128)(2,1)} %g_ref.3, ...), custom_call_target="tpu_custom_call" | custom-call | flops 199999995904 | bytes 62914560 | tf_op jit(solution)/shard_map/backward_line/pallas_call | solution.py:1257
  708.3 0.8 fusion.14
  709.1 0.9 fusion.15
  710.1 0.6 broadcast_in_dim.71
  710.7 0.0 copy-done.1
  710.7 0.0 copy-done.2
  710.7 1.5 multiply_subtract_fusion
  712.2 0.0 copy-done.4
  712.2 0.0 copy-done.8
  712.2 0.6 multiply_subtract_fusion.1
  712.9 32.8 %shampoo.1 = (f32[24,256,256]{2,1,0:T(8,128)}, f32[24,256,256]{2,1,0:T(8,128)}, f32[24,256,256]{2,1,0:T(8,128)}, f32[24,256,256]{2,1,0:T(8,128)}, bf16[2048,2048...) custom-call(bf16[24,256,256]{2,1,0:T(8,128)(2,1)} %reduce-scatter.2.cloned.1.call-done.g_ref, f32[24,256,256]{2,1,0:T(8,128)} %bitcast.22, ...), custom_call_target="tpu_custom_call" | custom-call | tf_op jit(solution)/shard_map/shampoo/pallas_call | solution.py:1359
  (18 shorter events, 0.1 us)
Async XLA Ops:
  7.2 5.0 copy-start.3
  7.2 6.4 copy-start.11
  7.2 6.4 copy-start.10
  7.2 133.1 %all-gather.2.cloned.1.call-start = ((), (), s32[]{:S(2)}) async-start(), calls=%async_computation.1 | async-start | bytes 28311552 | tf_op jit(solution)/shard_map/all_gather | solution.py:1397
  12.2 700.7 %reduce-scatter.2.cloned.1.call-start = ((), (), s32[]{:S(2)}) async-start(), calls=%async_computation.2 | async-start | bytes 28311552 | tf_op jit(solution)/shard_map/reduce_scatter | solution.py:1445
  14.4 11.3 %copy-start = (f32[6,2048]{1,0:T(8,128)S(1)}, f32[6,2048]{1,0:T(8,128)}, u32[]{:S(2)}) copy-start(f32[6,2048]{1,0:T(8,128)} %param.24) | copy-start | bytes 147460
  19.0 14.1 %slice-start = ((s8[8388608]{0:T(1024)(128)(4,1)}), s8[4194304]{0:T(1024)(128)(4,1)S(1)}, s32[]{:S(2)}) async-start(s8[8388608]{0:T(1024)(128)(4,1)} %bitcast.20), calls=%async_computation.3 | async-start | bytes 8388608
  25.7 7.4 slice-start.1
  26.3 15.4 %copy-start.6 = (f32[1,2048]{1,0:T(1,128)}, f32[1,2048]{1,0:T(1,128)S(1)}, u32[]{:S(2)}) copy-start(f32[1,2048]{1,0:T(1,128)S(1)} %get-tuple-element.85.two_ref) | copy-start | bytes 24580
  26.3 15.4 %copy-start.7 = (f32[1,2048]{1,0:T(1,128)}, f32[1,2048]{1,0:T(1,128)S(1)}, u32[]{:S(2)}) copy-start(f32[1,2048]{1,0:T(1,128)S(1)} %get-tuple-element.87.one_ref) | copy-start | bytes 24580
  33.1 8.7 %copy-start.9 = (s32[192]{0:T(256)S(1)}, s32[192]{0:T(256)}, u32[]{:S(2)}) copy-start(s32[192]{0:T(256)} %param.18) | copy-start | bytes 2308
  474.7 1.7 copy-start.5
  477.1 233.6 %copy-start.1 = (f32[6,2048]{1,0:T(8,128)S(1)}, f32[6,2048]{1,0:T(8,128)}, u32[]{:S(2)}) copy-start(f32[6,2048]{1,0:T(8,128)} %param.24) | copy-start | bytes 147460
  477.1 233.6 %copy-start.2 = (f32[6,2048]{1,0:T(8,128)S(1)}, f32[6,2048]{1,0:T(8,128)}, u32[]{:S(2)}) copy-start(f32[6,2048]{1,0:T(8,128)} %param.25) | copy-start | bytes 147460
  477.2 235.1 %copy-start.4 = (f32[1,3584]{1,0:T(1,128)S(1)}, f32[1,3584]{1,0:T(1,128)}, u32[]{:S(2)}) copy-start(f32[1,3584]{1,0:T(1,128)} %param.26) | copy-start | bytes 43012
  477.2 235.1 %copy-start.8 = (f32[1,3584]{1,0:T(1,128)S(1)}, f32[1,3584]{1,0:T(1,128)}, u32[]{:S(2)}) copy-start(f32[1,3584]{1,0:T(1,128)} %param.27) | copy-start | bytes 43012
Sparse Core Ops, SparseCore 0:
  12.3 128.0 all-gather.1
  474.9 160.8 reduce-scatter.1

commit v3 on v2

--- a/solution.py
+++ b/solution.py
@@ -335,9 +335,13 @@
 MESH = pl.DeviceIdType.MESH
 ANY = pl.BlockSpec(memory_space=pl.ANY)
 STEP = 256
-SUB = 64
-PAIRS = 16
+SUB = 32
+PAIRS = 32
 STEPS = 8
+PER_STEP = PAIRS // STEPS
+TICKS = PAIRS // 2
+GOT = 16
+ACROSS = 8
 VMEM_BYTES = 60 * 1024 * 1024
 FORWARD_VMEM = 63 * 1024 * 1024
 
@@ -377,44 +381,12 @@
         copy.wait()
 
 
-def place_kernel(shapes, order_ref, slots_ref, *refs):
-    mats, (hold, sem_in, sem_out) = refs[:-3], refs[-3:]
-    total = slots_ref.shape[0]
-    move_blocks(
-        [
-            pltpu.make_async_copy(slots_ref.at[order_ref[b]], hold.at[b], sem_in.at[b])
-            for b in range(total)
-        ],
-        [
-            pltpu.make_async_copy(hold.at[b], tile_of(mats, shapes, b), sem_out.at[b])
-            for b in range(total)
-        ],
-    )
-
-
 def block_scratch(total):
     return [
         pltpu.VMEM((total, B, B), LOW),
         pltpu.SemaphoreType.DMA((total,)),
         pltpu.SemaphoreType.DMA((total,)),
     ]
-
-
-def place_blocks(slots, order, shapes):
-    total = slots.shape[0]
-    return pl.pallas_call(
-        functools.partial(place_kernel, shapes),
-        grid_spec=pltpu.PrefetchScalarGridSpec(
-            num_scalar_prefetch=1,
-            grid=(1,),
-            in_specs=[ANY],
-            out_specs=[ANY] * len(shapes),
-            scratch_shapes=block_scratch(total),
-        ),
-        out_shape=[jax.ShapeDtypeStruct(s, LOW) for s in shapes],
-        compiler_params=pltpu.CompilerParams(vmem_limit_bytes=VMEM_BYTES),
-        name="place_blocks",
-    )(order, slots)
 
 
 def unplace_kernel(shapes, order_ref, *refs):
@@ -450,23 +422,246 @@
     )(order, *mats)
 
 
-def turn(values, cos, sin_high, sin_low):
-    return (
-        values * cos
-        + pltpu.roll(values, 32, 1) * sin_high
-        - pltpu.roll(values, 96, 1) * sin_low
-    )
-
-
-def turn_back(values, cos, sin_high, sin_low):
-    return (
-        values * cos
-        - pltpu.roll(values, 32, 1) * sin_high
-        + pltpu.roll(values, 96, 1) * sin_low
-    )
-
-
-def qkv_kernel(scale, h_ref, w_ref, bias_ref, cos_ref, high_ref, low_ref, q_ref, k_ref, v_ref):
+PIECES = 4
+ROUTES = ((0, 2), (0, 4), (0, 1), (2, 4), (4, 2), (2, 1), (4, 1), (6, 1))
+
+
+def flip(index, mask):
+    for bit in range(3):
+        if mask >> bit & 1:
+            unit = 2**bit
+            index = index + (1 - 2 * lax.rem(lax.div(index, unit), 2)) * unit
+    return index
+
+
+def gather_kernel(
+    shapes,
+    order_ref,
+    vec_ref,
+    w_hbm,
+    x_hbm,
+    cot_hbm,
+    qkv_hbm,
+    od_hbm,
+    up_hbm,
+    h1_hbm,
+    h2_hbm,
+    sum_ref,
+    slots,
+    wide,
+    x_buf,
+    c_buf,
+    h_buf,
+    stage,
+    send_sem,
+    recv_sem,
+    load_sem,
+    row_sem,
+    norm_sem,
+    stage_sem,
+):
+    me = lax.axis_index("dp")
+    each = w_hbm.shape[0]
+    size = each // PIECES
+    steps = x_hbm.shape[0] // STEP
+
+    def piece(mask, q):
+        return slots.at[pl.ds(flip(me, mask) * each + q * size, size)]
+
+    def send(source, target, q):
+        return pltpu.make_async_remote_copy(
+            src_ref=piece(source, q),
+            dst_ref=piece(source, q),
+            send_sem=send_sem.at[ROUTES.index((source, target)), q],
+            recv_sem=recv_sem.at[source ^ target, q],
+            device_id={"dp": flip(me, target)},
+            device_id_type=MESH,
+        )
+
+    def arrived(source, q):
+        pltpu.make_async_remote_copy(
+            src_ref=piece(source, q),
+            dst_ref=piece(source, q),
+            send_sem=send_sem.at[0, q],
+            recv_sem=recv_sem.at[source, q],
+            device_id={"dp": flip(me, 1)},
+            device_id_type=MESH,
+        ).wait_recv()
+
+    def load(q):
+        return pltpu.make_async_copy(
+            w_hbm.at[pl.ds(q * size, size)], wide.at[q % 2], load_sem.at[q % 2]
+        )
+
+    def tile(i):
+        return pl.ds(pl.multiple_of(i * STEP, STEP), STEP)
+
+    def fetch(i, slot):
+        return (
+            pltpu.make_async_copy(x_hbm.at[tile(i), :], x_buf.at[slot], row_sem.at[0, slot]),
+            pltpu.make_async_copy(cot_hbm.at[tile(i), :], c_buf.at[slot], row_sem.at[1, slot]),
+        )
+
+    def keep(i, slot):
+        return (
+            pltpu.make_async_copy(h_buf.at[slot, 0], h1_hbm.at[tile(i), :], norm_sem.at[0, slot]),
+            pltpu.make_async_copy(h_buf.at[slot, 1], h2_hbm.at[tile(i), :], norm_sem.at[1, slot]),
+        )
+
+    def norm_step(i, slot, first):
+        for copy in fetch(i, slot):
+            copy.wait()
+
+        @pl.when(jnp.logical_not(first))
+        def _():
+            for copy in keep(i, slot):
+                copy.wait()
+
+        x = x_buf[slot].astype(WIDE)
+        center = x - jnp.mean(x, axis=1, keepdims=True)
+        scale = lax.rsqrt(jnp.mean(center * center, axis=1, keepdims=True) + norm_eps)
+        xhat = center * scale
+        h_buf[slot, 0] = (xhat * vec_ref[0:1, :] + vec_ref[1:2, :]).astype(LOW)
+        h_buf[slot, 1] = (xhat * vec_ref[2:3, :] + vec_ref[3:4, :]).astype(LOW)
+        sum_ref[0:1, :] += jnp.sum(c_buf[slot].astype(WIDE), axis=0, keepdims=True)
+        for copy in keep(i, slot):
+            copy.start()
+
+    for q in range(2):
+        load(q).start()
+    for slot in range(2):
+        for copy in fetch(slot, slot):
+            copy.start()
+    barrier = pltpu.get_barrier_semaphore()
+    for target in (1, 2, 4):
+        pl.semaphore_signal(
+            barrier, inc=1, device_id={"dp": flip(me, target)}, device_id_type=MESH
+        )
+    sum_ref[...] = jnp.zeros_like(sum_ref)
+    for q in range(PIECES):
+        load(q).wait()
+        slots[pl.ds(me * each + q * size, size)] = wide[q % 2].astype(LOW)
+        if q + 2 < PIECES:
+            load(q + 2).start()
+        if q == 0:
+            pl.semaphore_wait(barrier, 3)
+        for target in (2, 4, 1):
+            send(0, target, q).start()
+
+    for q in range(PIECES):
+
+        @pl.loop(0, steps // (2 * PIECES))
+        def _(k):
+            i = (q * (steps // (2 * PIECES)) + k) * 2
+            for slot in range(2):
+                norm_step(i + slot, slot, i == 0)
+
+                @pl.when(i + slot + 2 < steps)
+                def _():
+                    for copy in fetch(i + slot + 2, slot):
+                        copy.start()
+
+        arrived(2, q)
+        if q % 2:
+            send(2, 4, q).start()
+        send(2, 1, q).start()
+        arrived(4, q)
+        if q % 2 == 0:
+            send(4, 2, q).start()
+        send(4, 1, q).start()
+    for slot in range(2):
+        for copy in keep(slot, slot):
+            copy.wait()
+    for q in range(PIECES):
+        arrived(6, q)
+        send(6, 1, q).start()
+    for source in (1, 3, 5, 7):
+        for q in range(PIECES):
+            arrived(source, q)
+
+    block = 0
+    for ref, (rows, cols) in zip((qkv_hbm, od_hbm, up_hbm), shapes):
+        across = cols // B
+
+        def panel(i, slot):
+            return pltpu.make_async_copy(
+                stage.at[slot, :, pl.ds(0, cols)], ref.at[lane(i * B), :], stage_sem.at[slot]
+            )
+
+        @pl.loop(0, rows // B // 2)
+        def _(k):
+            for slot in range(2):
+                i = k * 2 + slot
+
+                @pl.when(k > 0)
+                def _():
+                    panel(i, slot).wait()
+
+                for j in range(across):
+                    stage[slot, :, j * B : (j + 1) * B] = slots[order_ref[block + i * across + j]]
+                panel(i, slot).start()
+
+        for slot in range(2):
+            panel(slot, slot).wait()
+        block += rows // B * across
+
+    for source, target in ROUTES:
+        for q in range(PIECES):
+            if (source, target) == (2, 4) and q % 2 == 0:
+                continue
+            if (source, target) == (4, 2) and q % 2:
+                continue
+            send(source, target, q).wait_send()
+
+
+def gather_weights(blocks, order, tokens, cotangent, vectors, shapes):
+    rows, d = tokens.shape
+    each = blocks.shape[0]
+    return pl.pallas_call(
+        functools.partial(gather_kernel, shapes),
+        in_specs=[
+            pl.BlockSpec(memory_space=pltpu.SMEM),
+            pl.BlockSpec(memory_space=pltpu.VMEM),
+            ANY,
+            ANY,
+            ANY,
+        ],
+        out_specs=[ANY] * 5 + [pl.BlockSpec(memory_space=pltpu.VMEM)],
+        out_shape=[jax.ShapeDtypeStruct(s, LOW) for s in shapes]
+        + [jax.ShapeDtypeStruct((rows, d), LOW)] * 2
+        + [jax.ShapeDtypeStruct((8, d), WIDE)],
+        scratch_shapes=[
+            pltpu.VMEM((order.shape[0], B, B), LOW),
+            pltpu.VMEM((2, each // PIECES, B, B), WIDE),
+            pltpu.VMEM((2, STEP, d), LOW),
+            pltpu.VMEM((2, STEP, d), LOW),
+            pltpu.VMEM((2, 2, STEP, d), LOW),
+            pltpu.VMEM((2, B, d), LOW),
+            pltpu.SemaphoreType.DMA((8, PIECES)),
+            pltpu.SemaphoreType.DMA((8, PIECES)),
+            pltpu.SemaphoreType.DMA((2,)),
+            pltpu.SemaphoreType.DMA((2, 2)),
+            pltpu.SemaphoreType.DMA((2, 2)),
+            pltpu.SemaphoreType.DMA((2,)),
+        ],
+        compiler_params=pltpu.CompilerParams(
+            vmem_limit_bytes=VMEM_BYTES, collective_id=3, has_side_effects=True
+        ),
+        cost_estimate=pl.CostEstimate(
+            flops=100_000_000_000, bytes_accessed=80 << 20, transcendentals=0
+        ),
+        name="gather_weights",
+    )(order, vectors, blocks, tokens, cotangent)
+
+
+def turn(values, cos, sin, back=False):
+    lanes = lax.broadcasted_iota(jnp.int32, values.shape, 1)
+    lower, upper = pltpu.roll(values, 96, 1), pltpu.roll(values, 32, 1)
+    other = jnp.where(lanes < 32, -lower, upper)
+    return values * cos - other * sin if back else values * cos + other * sin
+
+
+def qkv_kernel(scale, h_ref, w_ref, bias_ref, cos_ref, sin_ref, q_ref, k_ref, v_ref):
     for j in range(w_ref.shape[1] // HD):
         head, part = divmod(j, 3)
         cols = slice(head * HD, head * HD + HD)
@@ -474,7 +669,7 @@
         if part == 2:
             v_ref[:, cols] = proj.astype(LOW)
             continue
-        front = turn(proj[:, :128], cos_ref[...], high_ref[...], low_ref[...])
+        front = turn(proj[:, :128], cos_ref[...], sin_ref[...])
         turned = jnp.concatenate([front, proj[:, 128:]], axis=1).astype(LOW)
         if part == 0:
             q_ref[:, cols] = (turned.astype(WIDE) * scale).astype(LOW)
@@ -491,7 +686,7 @@
     return pl.pallas_call(
         functools.partial(qkv_kernel, 1.0 / math.sqrt(HD)),
         grid=(rows // tile,),
-        in_specs=[row_spec(d), resident((d, cols)), resident((1, cols))] + [row_spec(128)] * 3,
+        in_specs=[row_spec(d), resident((d, cols)), resident((1, cols))] + [row_spec(128)] * 2,
         out_specs=[row_spec(out_cols)] * 3,
         out_shape=[jax.ShapeDtypeStruct((rows, out_cols), LOW)] * 3,
         compiler_params=pltpu.CompilerParams(vmem_limit_bytes=VMEM_BYTES),
@@ -507,29 +702,15 @@
     v_ref,
     cot_ref,
     out_ref,
-    cos_ref,
-    high_ref,
-    low_ref,
     ctx_ref,
     grad_ref,
-    sums_ref,
-    p_scr,
-    dp_scr,
-    dk_scr,
-    dv_scr,
+    stats_ref,
+    s_scr,
 ):
     step = pl.program_id(1)
-    count = pl.num_programs(1)
-    scale = 1.0 / math.sqrt(HD)
-
-    @pl.when(step == 0)
-    def _():
-        dk_scr[...] = jnp.zeros_like(dk_scr)
-        dv_scr[...] = jnp.zeros_like(dv_scr)
 
     def rows(c):
         q = q_ref[...]
-        g = dot_nt(cot_ref[...], out_ref[...]).astype(LOW)
         first = start_ref[...]
         top = jnp.full((tile, 1), masked_score, WIDE)
         for j in range(c + 1):
@@ -541,62 +722,37 @@
                 row = lax.broadcasted_iota(jnp.int32, (tile, tile), 0) + c * tile
                 ok = ok & (col <= row)
             s = jnp.where(ok, s, masked_score)
-            p_scr[:, keys] = s
+            s_scr[:, keys] = s
             top = jnp.maximum(top, jnp.max(s, axis=1, keepdims=True))
         total = jnp.zeros((tile, 1), WIDE)
+        ctx = jnp.zeros((tile, HD), WIDE)
         for j in range(c + 1):
             keys = slice(j * tile, (j + 1) * tile)
-            e = jnp.exp(p_scr[:, keys] - top)
-            p_scr[:, keys] = e
+            e = jnp.exp(s_scr[:, keys] - top)
             total = total + jnp.sum(e, axis=1, keepdims=True)
-        inverse = 1.0 / total
-        ctx = jnp.zeros((tile, HD), WIDE)
-        delta = jnp.zeros((tile, 1), WIDE)
-        for j in range(c + 1):
-            keys = slice(j * tile, (j + 1) * tile)
-            p = p_scr[:, keys] * inverse
-            p_scr[:, keys] = p
-            pb = p.astype(LOW)
-            dp = dot_nt(g, v_ref[keys, :])
-            dp_scr[:, keys] = dp
-            delta = delta + jnp.sum(p * dp, axis=1, keepdims=True)
-            ctx = ctx + dot(pb, v_ref[keys, :])
-            dv_scr[keys, :] += dot_tn(pb, g)
+            ctx = ctx + dot(e.astype(LOW), v_ref[keys, :])
+        ctx = ctx * (1.0 / total)
+        grad = dot_nt(cot_ref[...], out_ref[...]).astype(LOW)
+        delta = jnp.sum(ctx * grad.astype(WIDE), axis=1, keepdims=True)
         ctx_ref[...] = ctx.astype(LOW)
-        dq = jnp.zeros((tile, HD), WIDE)
-        for j in range(c + 1):
-            keys = slice(j * tile, (j + 1) * tile)
-            ds = (p_scr[:, keys] * (dp_scr[:, keys] - delta)).astype(LOW)
-            dq = dq + dot(ds, k_ref[keys, :])
-            dk_scr[keys, :] += dot_tn(ds, q)
-        dq = dq * scale
-        here = slice(c * tile, (c + 1) * tile)
-        front = turn_back(dq[:, :128], cos_ref[here, :], high_ref[here, :], low_ref[here, :])
-        grad_ref[here, 0:128] = front.astype(LOW)
-        grad_ref[here, 128:HD] = dq[:, 128:].astype(LOW)
-
-    for c in range(dk_scr.shape[0] // tile):
+        grad_ref[...] = grad
+        lanes = lax.broadcasted_iota(jnp.int32, (tile, 128), 1)
+        stats_ref[...] = jnp.where(
+            lanes == 0, top + jnp.log(total), jnp.where(lanes == 1, delta, first.astype(WIDE))
+        )
+
+    for c in range(k_ref.shape[0] // tile):
         pl.when(step == c)(functools.partial(rows, c))
 
-    @pl.when(step == count - 1)
-    def _():
-        dk = dk_scr[...]
-        front = turn_back(dk[:, :128], cos_ref[...], high_ref[...], low_ref[...])
-        grad_ref[:, HD : HD + 128] = front.astype(LOW)
-        grad_ref[:, HD + 128 : 2 * HD] = dk[:, 128:].astype(LOW)
-        grad_ref[:, 2 * HD :] = dv_scr[...].astype(LOW)
-        total = jnp.sum(grad_ref[...].astype(WIDE), axis=0, keepdims=True)
-        sums_ref[...] = jnp.broadcast_to(total, sums_ref.shape)
-
-
-def attention_both(start, q, k, v, cotangent, od_w, tables):
+
+def attention_forward_rows(start, q, k, v, cotangent, od_w):
     rows, cols = q.shape
     d = cotangent.shape[1]
     heads = cols // HD
     tile = 512
     tile_spec = pl.BlockSpec((tile, HD), lambda h, i: (i, h))
     full_spec = pl.BlockSpec((rows, HD), lambda h, i: (0, h))
-    flops = heads * rows * rows * HD * 6
+    flops = heads * rows * rows * HD * 3
     return pl.pallas_call(
         functools.partial(attention_kernel, tile),
         grid=(heads, rows // tile),
@@ -607,28 +763,18 @@
             full_spec,
             pl.BlockSpec((tile, d), lambda h, i: (i, 0)),
             pl.BlockSpec((HD, d), lambda h, i: (h, 0)),
-        ]
-        + [resident((rows, 128))] * 3,
-        out_specs=[
-            tile_spec,
-            pl.BlockSpec((rows, 3 * HD), lambda h, i: (0, h)),
-            pl.BlockSpec((8, 3 * HD), lambda h, i: (0, h)),
         ],
+        out_specs=[tile_spec, tile_spec, pl.BlockSpec((tile, 128), lambda h, i: (i, h))],
         out_shape=[
             jax.ShapeDtypeStruct((rows, cols), LOW),
-            jax.ShapeDtypeStruct((rows, 3 * cols), LOW),
-            jax.ShapeDtypeStruct((8, 3 * cols), WIDE),
+            jax.ShapeDtypeStruct((rows, cols), LOW),
+            jax.ShapeDtypeStruct((rows, heads * 128), WIDE),
         ],
-        scratch_shapes=[
-            pltpu.VMEM((tile, rows), WIDE),
-            pltpu.VMEM((tile, rows), WIDE),
-            pltpu.VMEM((rows, HD), WIDE),
-            pltpu.VMEM((rows, HD), WIDE),
-        ],
+        scratch_shapes=[pltpu.VMEM((tile, rows), WIDE)],
         compiler_params=pltpu.CompilerParams(vmem_limit_bytes=VMEM_BYTES),
         cost_estimate=pl.CostEstimate(flops=flops, bytes_accessed=30 << 20, transcendentals=0),
-        name="attention_both",
-    )(start, q, k, v, cotangent, od_w, *tables)
+        name="attention_forward",
+    )(start, q, k, v, cotangent, od_w)
 
 
 class Line:
@@ -681,12 +827,13 @@
         )
 
     def up(self, pair):
-        return self.copy(self.part.at[pair], self.got.at[pair], self.up_send, self.up_recv, pair, self.partner)
+        return self.copy(
+            self.part.at[pair], self.got.at[pair % GOT], self.up_send, self.up_recv, pair, self.partner
+        )
 
     def far_sum(self, pair):
-        return self.copy(
-            self.part.at[pair, self.far], self.across.at[pair], self.far_send, self.far_recv, pair, self.other
-        )
+        src, dst = self.part.at[pair, self.far], self.across.at[pair % ACROSS]
+        return self.copy(src, dst, self.far_send, self.far_recv, pair, self.other)
 
     def over(self, pair, which):
         src = self.part.at[pair, self.near]
@@ -707,13 +854,15 @@
         return pltpu.make_async_copy(src, self.rows(pair, self.near), self.own.at[pair])
 
     def send_up(self, pair):
-        @pl.when(jnp.logical_not(self.inner))
+        @pl.when(pair >= GOT)
         def _():
-            self.up(pair).start()
+            self.down(pair - GOT).wait_recv()
+
+        self.up(pair).start()
 
     def add_far(self, pair):
         self.up(pair).wait_recv()
-        far = self.part[pair, self.far].astype(WIDE) + self.got[pair, self.far].astype(WIDE)
+        far = self.part[pair, self.far].astype(WIDE) + self.got[pair % GOT, self.far].astype(WIDE)
         self.part[pair, self.far] = far.astype(LOW)
         self.far_sum(pair).start()
 
@@ -721,8 +870,8 @@
         self.far_sum(pair).wait_recv()
         total = (
             self.part[pair, self.near].astype(WIDE)
-            + self.got[pair, self.near].astype(WIDE)
-            + self.across[pair].astype(WIDE)
+            + self.got[pair % GOT, self.near].astype(WIDE)
+            + self.across[pair % ACROSS].astype(WIDE)
         )
         self.part[pair, self.near] = (base + total).astype(LOW)
         self.over(pair, self.near).start()
@@ -749,28 +898,39 @@
             @pl.loop(0, PAIRS)
             def _(pair):
                 self.up(pair).wait_send()
+                self.relay(pair).wait_recv()
+
+            @pl.loop(PAIRS - GOT, PAIRS)
+            def _(pair):
                 self.down(pair).wait_recv()
-                self.relay(pair).wait_recv()
 
     def tick(self, step, lag, base):
-        @pl.when(self.inner & (step >= lag + 2) & (step < lag + 2 + PAIRS))
+        @pl.when(jnp.logical_not(self.inner) & (step < TICKS))
         def _():
-            self.send_relay(step - lag - 2)
-
-        @pl.when(self.inner & (step >= lag + 1) & (step < lag + 1 + PAIRS))
+            for s in range(2):
+                self.send_up(step * 2 + s)
+
+        @pl.when(self.inner & (step >= lag + 2) & (step < lag + 2 + TICKS))
         def _():
-            self.finish_near(step - lag - 1, base())
-
-        @pl.when(self.inner & (step >= lag) & (step < lag + PAIRS))
+            for s in range(2):
+                self.send_relay((step - lag - 2) * 2 + s)
+
+        @pl.when(self.inner & (step >= lag + 1) & (step < lag + 1 + TICKS))
         def _():
-            self.add_far(step - lag)
+            for s in range(2):
+                self.finish_near((step - lag - 1) * 2 + s, base(s))
+
+        @pl.when(self.inner & (step >= lag) & (step < lag + TICKS))
+        def _():
+            for s in range(2):
+                self.add_far((step - lag) * 2 + s)
 
 
 def line_scratch(d):
     return [
         pltpu.VMEM((PAIRS, 2, SUB, d), LOW),
-        pltpu.VMEM((PAIRS, 2, SUB, d), LOW),
-        pltpu.VMEM((PAIRS, SUB, d), LOW),
+        pltpu.VMEM((GOT, 2, SUB, d), LOW),
+        pltpu.VMEM((ACROSS, SUB, d), LOW),
         pltpu.SemaphoreType.DMA((11, PAIRS)),
     ]
 
@@ -784,7 +944,7 @@
 
 
 def base_block(width, lag):
-    return pl.BlockSpec((2 * SUB, width), lambda i: (jnp.clip(i - lag - 1, 0, PAIRS - 1), 0))
+    return pl.BlockSpec((4 * SUB, width), lambda i: (jnp.clip(i - lag - 1, 0, TICKS - 1), 0))
 
 
 def lane(start):
@@ -808,11 +968,12 @@
 
 
 def store_part(part_ref, step, cols, value):
-    part_ref[pl.ds(step * 2, 2), :, :, cols] = value.astype(LOW).reshape(2, 2, SUB, value.shape[1])
+    value = value.astype(LOW).reshape(PER_STEP, 2, SUB, value.shape[1])
+    part_ref[pl.ds(step * PER_STEP, PER_STEP), :, :, cols] = value
 
 
 FORWARD_LAG = 2
-FORWARD_GRID = FORWARD_LAG + PAIRS + 2
+FORWARD_GRID = FORWARD_LAG + TICKS + 2
 
 
 def weight_unit(a_t, b_ref, cols, stage, slot):
@@ -828,19 +989,27 @@
     x_ref,
     bias_ref,
     shift_ref,
+    cos_ref,
+    sin_ref,
     up_hbm,
     od_hbm,
     h1_hbm,
     h2_hbm,
     ctx_hbm,
     cot_hbm,
-    qg_hbm,
+    q_hbm,
+    k_hbm,
+    v_hbm,
+    cg_hbm,
+    stats_hbm,
     out_ref,
     hg_hbm,
+    qg_hbm,
     wq_hbm,
     wo_hbm,
     wu_hbm,
     sums_ref,
+    qkv_sums_ref,
     up_buf,
     od_buf,
     act_all,
@@ -849,10 +1018,15 @@
     got,
     across,
     sems,
+    stats,
+    dq_scr,
+    dk_scr,
+    dv_scr,
     load_sem,
     panel_sem,
     stage_sem,
     hg_sem,
+    head_sem,
 ):
     step = pl.program_id(0)
     line = Line(out_ref, part, got, across, sems)
@@ -884,10 +1058,20 @@
             cot_hbm, od_buf.at[pl.ds(0, rows), :], load_sem.at[2 * tiles + 1]
         )
 
-    def load_qg():
-        return pltpu.make_async_copy(
-            qg_hbm, up_buf.at[:, pl.ds(0, qkv_cols)], load_sem.at[2 * tiles + 2]
-        )
+    def load_head(h):
+        cols = pl.ds(pl.multiple_of(h * HD, HD), HD)
+        copies = [
+            pltpu.make_async_copy(
+                src.at[:, cols], act_all.at[:, pl.ds(i * HD, HD)], head_sem.at[i]
+            )
+            for i, src in enumerate((q_hbm, k_hbm, v_hbm, cg_hbm))
+        ]
+        lanes = pl.ds(pl.multiple_of(h * 128, 128), 128)
+        copies.append(pltpu.make_async_copy(stats_hbm.at[:, lanes], stats, head_sem.at[4]))
+        return copies
+
+    def store_qg():
+        return pltpu.make_async_copy(hg_all.at[:, pl.ds(0, qkv_cols)], qg_hbm, head_sem.at[5])
 
     def panel_cols(slot):
         return lane(qkv_cols + slot * B)
@@ -949,14 +1133,11 @@
                 act_all[here, :], od_buf[heads:, cols]
             )
             store_part(part, step, cols, value)
-        for s in range(2):
-            line.send_up(step * 2 + s)
 
     @pl.when(step == STEPS - 1)
     def _():
         panel(h2_hbm, 0, 0).start()
         load_cot().start()
-        load_qg().start()
 
     def unit(index, a_t, b_ref, cols, dst, row):
         slot = index % 2
@@ -998,12 +1179,92 @@
             cot = od_buf.at[pl.ds(0, rows), :]
             unit(i, act_all[:, lane(i * B)].T, cot, units, wo_hbm, heads + i * B)
 
+    @pl.when(step == 11)
+    def _():
+        for copy in load_head(0):
+            copy.start()
+
     @pl.when(step == 12)
     def _():
         settle(wo_hbm, units)
+
+        @pl.loop(0, STEPS)
+        def _(i):
+            store_hg(i).wait()
+
+    def head_grads(h, start, stop):
+        tile = 512
+        count = rows // tile
+
+        def tile_rows(i):
+            return pl.ds(pl.multiple_of(i * tile, tile), tile)
+
+        def put(i, part, values):
+            cols = pl.ds(pl.multiple_of(h * 3 * HD + part * HD, HD), HD)
+            hg_all[tile_rows(i), cols] = values.astype(LOW)
+
+        def turned_back(i, values):
+            front = turn(values[:, :128], cos_ref[tile_rows(i), :], sin_ref[tile_rows(i), :], True)
+            return jnp.concatenate([front, values[:, 128:]], axis=1)
+
+        @pl.loop(start, stop)
+        def _(j):
+            keys = act_all[tile_rows(j), HD : 2 * HD]
+            values = act_all[tile_rows(j), 2 * HD : 3 * HD]
+            dk_scr[...] = jnp.zeros_like(dk_scr)
+            dv_scr[...] = jnp.zeros_like(dv_scr)
+
+            @pl.loop(j, count)
+            def _(i):
+                q = act_all[tile_rows(i), 0:HD]
+                g = act_all[tile_rows(i), 3 * HD : 4 * HD]
+                info = stats[tile_rows(i), :]
+                log_total, delta = info[:, 0:1], info[:, 1:2]
+                first = info[:, 2:3].astype(jnp.int32) - j * tile
+                col = lax.broadcasted_iota(jnp.int32, (tile, tile), 1)
+                row = lax.broadcasted_iota(jnp.int32, (tile, tile), 0) + (i - j) * tile
+                ok = (col >= first) & (col <= row)
+                p = jnp.where(ok, jnp.exp(dot_nt(q, keys) - log_total), 0.0)
+                ds = (p * (dot_nt(g, values) - delta)).astype(LOW)
+                dv_scr[...] += dot_tn(p.astype(LOW), g)
+                dk_scr[...] += dot_tn(ds, q)
+                dq_scr[tile_rows(i), :] += dot(ds, keys)
+
+            put(j, 1, turned_back(j, dk_scr[...]))
+            put(j, 2, dv_scr[...])
+
+        @pl.when(stop == count)
+        def _():
+            @pl.loop(0, count)
+            def _(i):
+                put(i, 0, turned_back(i, dq_scr[tile_rows(i), :] * (1.0 / math.sqrt(HD))))
+
+    @pl.when((step == 12) | (step == 14))
+    def _():
+        for copy in load_head((step - 12) // 2):
+            copy.wait()
+        dq_scr[...] = jnp.zeros_like(dq_scr)
+
+    @pl.when((step >= 12) & (step < 16))
+    def _():
+        second = (step - 12) % 2
+        head_grads((step - 12) // 2, second, 1 + 3 * second)
+
+    @pl.when(step == 13)
+    def _():
+        for copy in load_head(1):
+            copy.start()
+
+    @pl.when(step == 16)
+    def _():
+        store_qg().start()
         for j in range(2):
             panel(ctx_hbm, j, j).start()
-        load_qg().wait()
+        total = jnp.zeros((1, qkv_cols), WIDE)
+        for i in range(rows // 512):
+            part_rows = slice(i * 512, (i + 1) * 512)
+            total = total + jnp.sum(hg_all[part_rows, :qkv_cols].astype(WIDE), axis=0, keepdims=True)
+        qkv_sums_ref[...] = jnp.broadcast_to(total, qkv_sums_ref.shape)
         for j in range(2):
             panel(ctx_hbm, j, j).wait()
 
@@ -1015,30 +1276,27 @@
         settle(wo_hbm, units)
         panel(h1_hbm, 0, 0).start()
 
-    @pl.when((step == 13) | (step == 14))
+    @pl.when((step == 17) | (step == 18))
     def _():
         @pl.loop(0, 4)
         def _(k):
-            i = (step - 13) * 4 + k
+            i = (step - 17) * 4 + k
             panel(h1_hbm, i, i % 2).wait()
 
             @pl.when(i < 7)
             def _():
                 panel(h1_hbm, i + 1, (i + 1) % 2).start()
 
-            grads = up_buf.at[:, pl.ds(0, qkv_cols)]
+            grads = hg_all.at[:, pl.ds(0, qkv_cols)]
             unit(i, up_buf[:, panel_cols(i % 2)].T, grads, qkv_cols, wq_hbm, i * B)
 
-    @pl.when(step == 15)
+    @pl.when(step == 19)
     def _():
         settle(wq_hbm, qkv_cols)
-
-        @pl.loop(0, STEPS)
-        def _(i):
-            store_hg(i).wait()
-
-    def base():
-        near = pl.ds(pl.multiple_of(line.near * SUB, SUB), SUB)
+        store_qg().wait()
+
+    def base(s):
+        near = pl.ds(pl.multiple_of(s * 2 * SUB + line.near * SUB, SUB), SUB)
         return x_ref[near, :].astype(WIDE) + shift_ref[...]
 
     line.tick(step, FORWARD_LAG, base)
@@ -1048,10 +1306,12 @@
         line.drain()
 
 
-def forward_line(h1, h2, cotangent, ctx, qkv_grad, tokens, up_w, od_w, bias, shift):
+def forward_line(
+    h1, h2, cotangent, ctx, heads, stats, tables, tokens, up_w, od_w, bias, shift
+):
     rows, d = tokens.shape
     units = up_w.shape[1]
-    qkv_cols = qkv_grad.shape[1]
+    qkv_cols = 3 * ctx.shape[1]
     return pl.pallas_call(
         forward_kernel,
         grid=(FORWARD_GRID,),
@@ -1062,16 +1322,21 @@
             base_block(d, FORWARD_LAG),
             resident(bias.shape),
             resident(shift.shape),
+            resident((rows, 128)),
+            resident((rows, 128)),
         ]
-        + [ANY] * 7,
-        out_specs=[ANY] * 5 + [pl.BlockSpec((8, units), lambda i: (0, 0))],
+        + [ANY] * 11,
+        out_specs=[ANY] * 6
+        + [pl.BlockSpec((8, units), lambda i: (0, 0)), pl.BlockSpec((8, qkv_cols), lambda i: (0, 0))],
         out_shape=[
             jax.ShapeDtypeStruct((rows, d), LOW),
             jax.ShapeDtypeStruct((rows, units), LOW),
+            jax.ShapeDtypeStruct((rows, qkv_cols), LOW),
             jax.ShapeDtypeStruct((d, qkv_cols), LOW),
             jax.ShapeDtypeStruct(od_w.shape, LOW),
             jax.ShapeDtypeStruct((d, units), LOW),
             jax.ShapeDtypeStruct((8, units), WIDE),
+            jax.ShapeDtypeStruct((8, qkv_cols), WIDE),
         ],
         scratch_shapes=[
             pltpu.VMEM(up_w.shape, LOW),
@@ -1081,10 +1346,15 @@
         ]
         + line_scratch(d)
         + [
-            pltpu.SemaphoreType.DMA((11,)),
+            pltpu.VMEM((rows, 128), WIDE),
+            pltpu.VMEM((rows, HD), WIDE),
+            pltpu.VMEM((512, HD), WIDE),
+            pltpu.VMEM((512, HD), WIDE),
+            pltpu.SemaphoreType.DMA((10,)),
             pltpu.SemaphoreType.DMA((2,)),
             pltpu.SemaphoreType.DMA((2,)),
             pltpu.SemaphoreType.DMA((STEPS,)),
+            pltpu.SemaphoreType.DMA((6,)),
         ],
         compiler_params=pltpu.CompilerParams(
             vmem_limit_bytes=FORWARD_VMEM, collective_id=1, has_side_effects=True
@@ -1093,11 +1363,27 @@
             flops=200_000_000_000, bytes_accessed=80 << 20, transcendentals=0
         ),
         name="forward_line",
-    )(h2, cotangent, ctx, tokens, bias, shift, up_w, od_w, h1, h2, ctx, cotangent, qkv_grad)
+    )(
+        h2,
+        cotangent,
+        ctx,
+        tokens,
+        bias,
+        shift,
+        *tables,
+        up_w,
+        od_w,
+        h1,
+        h2,
+        ctx,
+        cotangent,
+        *heads,
+        stats,
+    )
 
 
 BACKWARD_LAG = 1
-BACKWARD_GRID = BACKWARD_LAG + PAIRS + 2
+BACKWARD_GRID = BACKWARD_LAG + TICKS + 2
 
 
 class Spread:
@@ -1225,8 +1511,6 @@
             cols = slice(n * width, (n + 1) * width)
             value = (gc_scr[:, cols] - mean - xhat_scr[:, cols] * slope) * scale
             store_part(part, step, cols, value)
-        for s in range(2):
-            line.send_up(step * 2 + s)
 
     @pl.when(step == STEPS)
     def _():
@@ -1237,8 +1521,8 @@
         own[...] = spread.finish(0)
         spread.start(1)
 
-    def base():
-        near = pl.ds(pl.multiple_of(line.near * SUB, SUB), SUB)
+    def base(s):
+        near = pl.ds(pl.multiple_of(s * 2 * SUB + line.near * SUB, SUB), SUB)
         return g_ref[near, :].astype(WIDE)
 
     line.tick(step, BACKWARD_LAG, base)
@@ -1394,25 +1678,16 @@
     qkv_cols = 3 * d // groups
     head_cols = d // groups
     unit_cols = FF // groups
-    gathered = lax.all_gather(weight_blocks[0].astype(LOW), "dp", axis=0, tiled=True)
-
     segment, position = segment_layout(seq_len, seq_device, device, row_count)
     start = (jnp.arange(row_count, dtype=jnp.int32) - position)[:, None]
     frequency = 10000.0 ** (-2.0 * jnp.arange(ROT // 2, dtype=WIDE) / ROT)
     angles = position.astype(WIDE)[:, None] * frequency[None, :]
     cos, sin = jnp.cos(angles), jnp.sin(angles)
     pad = jnp.zeros((row_count, 128 - ROT), WIDE)
-    empty = jnp.zeros_like(sin)
     tables = (
         jnp.concatenate([cos, cos, pad + 1.0], axis=1),
-        jnp.concatenate([empty, sin, pad], axis=1),
-        jnp.concatenate([sin, empty, pad], axis=1),
-    )
-    inputs = tokens.astype(WIDE)
-    normed_one = layer_norm(inputs, vectors[0], vectors[1]).astype(LOW)
-    normed_two = layer_norm(inputs, vectors[2], vectors[3]).astype(LOW)
-    out_sum = jnp.sum(cotangent.astype(WIDE), axis=0, keepdims=True)
-    normed_one, normed_two, out_sum = lax.optimization_barrier((normed_one, normed_two, out_sum))
+        jnp.concatenate([sin, sin, pad], axis=1),
+    )
     shift = (vectors[4] + vectors[5])[None]
     unit_shift = unit_bias[0]
 
@@ -1425,16 +1700,20 @@
             owner_map[blocks[0] + blocks[1] : blocks[0] + blocks[1] + blocks[2]],
         ]
     )
-    qkv_w, od_w, up_w = place_blocks(gathered, order, shapes)
+    qkv_w, od_w, up_w, normed_one, normed_two, out_sum = gather_weights(
+        weight_blocks[0], order, tokens, cotangent, vectors, shapes
+    )
 
     q, k, v = project_qkv(normed_one, qkv_w, unit_shift[None, :qkv_cols], tables)
-    ctx, qkv_grad, qkv_sums = attention_both(start, q, k, v, cotangent, od_w, tables)
-    block_out, hidden_grad, qkv_wg, od_wg, up_wg, hidden_sums = forward_line(
+    ctx, ctx_grad, stats = attention_forward_rows(start, q, k, v, cotangent, od_w)
+    block_out, hidden_grad, qkv_grad, qkv_wg, od_wg, up_wg, hidden_sums, qkv_sums = forward_line(
         normed_one,
         normed_two,
         cotangent,
         ctx,
-        qkv_grad,
+        (q, k, v, ctx_grad),
+        stats,
+        tables,
         tokens,
         up_w,
         od_w,
@@ -1447,7 +1726,7 @@
     sums = jnp.concatenate(
         [
             jnp.zeros((4, d), WIDE),
-            out_sum,
+            out_sum[:1],
             jnp.pad(qkv_sums[:1], ((0, 0), (0, d - qkv_cols))),
             jnp.pad(hidden_sums[:1], ((0, 0), (0, d - unit_cols))),
             jnp.zeros((1, d), WIDE),

time: 758 us -> 748 us (0.987)
  Pallas kernels: 598 us -> 702 us
  waiting for transfers between devices: 90.5 us -> 0.02 us
  other arithmetic: 42.7 us -> 12.2 us
    all_gather x1 -> x0, waiting for transfers between devices: 90.5 us -> none  [per_device_line(): lax.all_gather(weight_blocks[0].astype(LOW), 'dp', axis=0, tiled=True)]
    pallas_call x2, Pallas kernels: 58.8 us -> 146 us  [the longest x1 126 us: gather_weights(): pl.pallas_call(functools.partial(gather_kernel, shapes), in_specs=[pl.Blo...]
    reduce_sum x3 -> x0, other arithmetic: 18 us -> none  [the longest x1 6.78 us: per_device_line(): out_sum = jnp.sum(cotangent.astype(WIDE), axis=0, keepdims=True)]
    pallas_call x1, Pallas kernels: 235 us -> 251 us  [forward_line(): pl.pallas_call(forward_kernel, grid=(FORWARD_GRID,), in_specs=[row_block(...]
    convert_element_type x2 -> x0, other arithmetic: 13.5 us -> none  [the longest x1 8.65 us: per_device_line(): normed_two = layer_norm(inputs, vectors[2], vectors[3]).astype(LOW)]
  transfers between devices with their start and end apart: 2 -> 1, of which waited for: 1 -> 0; matrix products, arithmetic and copies ran while one was open for 6% -> 1% of each run, Pallas kernels for 31% -> 31%
where the time goes in v3:
time: 748 us; the launch traced here: 738 us
  Pallas kernels  702 us (94%)
  between operations  14.6 us (2%)
  other arithmetic  12.2 us (2%)
  local copies, waits for them, and re-layouts  9.63 us (1%)
    pallas_call x1, Pallas kernels, forward_line(): pl.pallas_call(forward_kernel, grid=(FORWARD_GRID,), in_specs=[row_block(...  251 us
    pallas_call x1, Pallas kernels, backward_line(): pl.pallas_call(backward_kernel, grid=(BACKWARD_GRID,), in_specs=[row_bloc...  231 us
    pallas_call x1, Pallas kernels, gather_weights(): pl.pallas_call(functools.partial(gather_kernel, shapes), in_specs=[pl.Blo...  126 us
    pallas_call x1, Pallas kernels, shampoo(): pl.pallas_call(shampoo_kernel, grid=(count // group,), in_specs=[spec] *...  32.8 us
    pallas_call x1, Pallas kernels, unplace_blocks(): pl.pallas_call(functools.partial(unplace_kernel, shapes), grid_spec=pltpu...  21.3 us
    pallas_call x1, Pallas kernels, attention_forward_rows(): pl.pallas_call(functools.partial(attention_kernel, tile), grid=(heads, ro...  20.1 us
    pallas_call x1, Pallas kernels, project_qkv(): pl.pallas_call(functools.partial(qkv_kernel, 1.0 / math.sqrt(HD)), grid=(...  18.7 us
  transfers between devices with their start and end apart: 1, of which 0 were waited for; matrix products, arithmetic and copies ran while one was open for 1% of the time, Pallas kernels for 31%

profile of v3, /device:TPU:0, one launch (start us, length us, event | category | flops | bytes accessed | tf_op | source)
XLA Modules:
  0.0 738.1 jit_solution(4451403609133040761)
XLA Ops:
  7.2 0.0 reduce-scatter.2.cloned.1.call-start
  7.2 1.3 slice.53.bias_ref
  8.5 1.3 slice.54.bias_ref
  9.8 0.1 pad.16.clone
  9.9 0.1 pad.13.clone
  10.0 0.9 fusion.8
  10.8 0.7 select_bitcast_fusion
  11.5 0.1 copy.29
  11.6 0.1 reduce-window.8
  11.7 0.1 reduce
  11.8 0.2 select_reduce_fusion
  12.0 1.6 fusion.7
  13.6 0.4 copy.30
  13.9 1.1 subtract_subtract_fusion.start_ref
  15.1 3.7 multiply_sine_fusion
  18.7 0.6 pad_add_fusion.order_ref
  19.4 1.9 maximum_maximum_fusion
  21.3 126.4 %gather_weights.1 = (bf16[2048,1536]{1,0:T(8,128)(2,1)}, bf16[2560,2048]{1,0:T(8,128)(2,1)}, bf16[2048,2048]{1,0:T(8,128)(2,1)}, bf16[2048,2048]{1,0:T(8,128)(2,...) custom-call(s32[192]{0:T(256)} %pad_add_fusion.order_ref, f32[6,2048]{1,0:T(8,128)} %vec_ref.1, ...), custom_call_target="tpu_custom_call" | custom-call | flops 99999997952 | bytes 83886080 | tf_op jit(solution)/shard_map/gather_weights/pallas_call | solution.py:620
  147.7 18.7 %project_qkv.1 = (bf16[2048,512]{1,0:T(8,128)(2,1)}, bf16[2048,512]{1,0:T(8,128)(2,1)}, bf16[2048,512]{1,0:T(8,128)(2,1)}) custom-call(bf16[2048,2048]{1,0:T(8,128)(2,1)} %get-tuple-element.43.h_ref.h1_hbm, bf16[2048,1536]{1,0:T(8,128)(2,1)} %get-tuple-element.44.w_ref.qkv_ref, f32[1,1536]{1,0:T(1,128)} %slice.53.bias_ref, ...), custom_call_target="tpu_custom_call" | custom-call | tf_op jit(solution)/shard_map/project_qkv/pallas_call | solution.py:686
  166.4 20.1 %attention_forward.1 = (bf16[2048,512]{1,0:T(8,128)(2,1)}, bf16[2048,512]{1,0:T(8,128)(2,1)}, f32[2048,256]{1,0:T(8,128)}) custom-call(s32[2048,1]{1,0:T(8,128)} %subtract_subtract_fusion.start_ref, bf16[2048,512]{1,0:T(8,128)(2,1)} %get-tuple-element.45.q_ref.q_hbm, bf16[2048,512]{1,0:T(8,128)(2,1)} %get-tuple-element.46.k_ref.k_hbm, ...), custom_call_target="tpu_custom_call" | custom-call | flops 6442450944 | bytes 31457280 | tf_op jit(solution)/shard_map/attention_forward/pallas_call | solution.py:756
  186.5 251.0 %forward_line.1 = (bf16[2048,2048]{1,0:T(8,128)(2,1)}, bf16[2048,2048]{1,0:T(8,128)(2,1)}, bf16[2048,1536]{1,0:T(8,128)(2,1)}, bf16[2048,1536]{1,0:T(8,128)(2,1)...) custom-call(bf16[2048,2048]{1,0:T(8,128)(2,1)} %get-tuple-element.42.h_ref.h2, ...), custom_call_target="tpu_custom_call" | custom-call | flops 199999995904 | bytes 83886080 | tf_op jit(solution)/shard_map/forward_line/pallas_call | solution.py:1315
  437.6 21.3 %unplace_blocks.1 = bf16[192,256,256]{2,1,0:T(8,128)(2,1)} custom-call(s32[192]{0:T(256)} %pad_add_fusion.order_ref, bf16[2048,1536]{1,0:T(8,128)(2,1)} %get-tuple-element.53.refs_0_, bf16[2560,2048]{1,0:T(8,128)(2,1)} %get-tuple-element.54.refs_1_, bf16[2048,2048]{1,0:T(8,128)(2,1)} %get-tuple-element.55.refs_2_), custom_call_target="tpu_custom_call" | custom-call | tf_op jit(solution)/shard_map/unplace_blocks/pallas_call | solution.py:410
  458.8 0.0 reduce-scatter.2.cloned.1.call-update
  458.9 0.8 slice.59
  459.7 0.8 slice.60
  460.5 0.8 slice.61
  461.4 0.7 concatenate.43.sums_in
  462.1 0.0 copy-start
  462.1 0.0 copy-start.1
  462.1 0.0 copy-start.2
  462.1 0.0 copy-start.3
  462.1 231.3 %backward_line.1 = (f32[8,2048]{1,0:T(8,128)}, bf16[2048,2048]{1,0:T(8,128)(2,1)}) custom-call(bf16[2048,1536]{1,0:T(8,128)(2,1)} %get-tuple-element.59.qg_ref, bf16[2048,2048]{1,0:T(8,128)(2,1)} %get-tuple-element.60.hg_ref, bf16[2048,2048]{1,0:T(8,128)(2,1)} %x_ref.3, bf16[2048,2048]{1,0:T(8,128)(2,1)} %g_ref.3, ...), custom_call_target="tpu_custom_call" | custom-call | flops 199999995904 | bytes 62914560 | tf_op jit(solution)/shard_map/backward_line/pallas_call | solution.py:1541
  693.4 0.8 fusion.5
  694.2 0.9 fusion.6
  695.2 0.6 broadcast_in_dim.59
  695.8 0.0 copy-done
  695.8 0.0 copy-done.1
  695.8 1.5 multiply_subtract_fusion
  697.3 0.0 copy-done.2
  697.3 0.0 copy-done.3
  697.3 0.6 multiply_subtract_fusion.1
  698.0 0.0 reduce-scatter.2.cloned.1.call-done.g_ref
  698.0 32.8 %shampoo.1 = (f32[24,256,256]{2,1,0:T(8,128)}, f32[24,256,256]{2,1,0:T(8,128)}, f32[24,256,256]{2,1,0:T(8,128)}, f32[24,256,256]{2,1,0:T(8,128)}, bf16[2048,2048...) custom-call(bf16[24,256,256]{2,1,0:T(8,128)(2,1)} %reduce-scatter.2.cloned.1.call-done.g_ref, f32[24,256,256]{2,1,0:T(8,128)} %bitcast.15, ...), custom_call_target="tpu_custom_call" | custom-call | tf_op jit(solution)/shard_map/shampoo/pallas_call | solution.py:1643
  (8 shorter events, 0.0 us)
Async XLA Ops:
  7.2 690.8 %reduce-scatter.2.cloned.1.call-start = ((), (), s32[]{:S(2)}) async-start(), calls=%async_computation.1 | async-start | bytes 28311552 | tf_op jit(solution)/shard_map/reduce_scatter | solution.py:1724
  462.1 233.7 %copy-start = (f32[6,2048]{1,0:T(8,128)S(1)}, f32[6,2048]{1,0:T(8,128)}, u32[]{:S(2)}) copy-start(f32[6,2048]{1,0:T(8,128)} %vec_ref.1) | copy-start | bytes 147460
  462.1 233.7 %copy-start.1 = (f32[6,2048]{1,0:T(8,128)S(1)}, f32[6,2048]{1,0:T(8,128)}, u32[]{:S(2)}) copy-start(f32[6,2048]{1,0:T(8,128)} %param.25) | copy-start | bytes 147460
  462.1 235.2 %copy-start.2 = (f32[1,3584]{1,0:T(1,128)S(1)}, f32[1,3584]{1,0:T(1,128)}, u32[]{:S(2)}) copy-start(f32[1,3584]{1,0:T(1,128)} %param.26) | copy-start | bytes 43012
  462.1 235.2 %copy-start.3 = (f32[1,3584]{1,0:T(1,128)S(1)}, f32[1,3584]{1,0:T(1,128)}, u32[]{:S(2)}) copy-start(f32[1,3584]{1,0:T(1,128)} %param.27) | copy-start | bytes 43012
Sparse Core Ops, SparseCore 0:
  459.0 160.4 reduce-scatter.1

commit v4 on v3

--- a/solution.py
+++ b/solution.py
@@ -340,8 +340,8 @@
 STEPS = 8
 PER_STEP = PAIRS // STEPS
 TICKS = PAIRS // 2
-GOT = 16
-ACROSS = 8
+GOT = 8
+ACROSS = 4
 VMEM_BYTES = 60 * 1024 * 1024
 FORWARD_VMEM = 63 * 1024 * 1024
 
@@ -362,64 +362,46 @@
     return pl.BlockSpec(shape, lambda *_: (0,) * len(shape), pipeline_mode=pl.Buffered(1))
 
 
-def tile_of(refs, widths, block):
-    for ref, (rows, cols) in zip(refs, widths):
-        count = (rows // B) * (cols // B)
-        if block < count:
-            i, j = divmod(block, cols // B)
-            return ref.at[pl.ds(i * B, B), pl.ds(j * B, B)]
-        block -= count
-
-
-def move_blocks(copies_in, copies_out):
-    for copy in copies_in:
-        copy.start()
-    for first, second in zip(copies_in, copies_out):
-        first.wait()
-        second.start()
-    for copy in copies_out:
-        copy.wait()
-
-
-def block_scratch(total):
-    return [
-        pltpu.VMEM((total, B, B), LOW),
-        pltpu.SemaphoreType.DMA((total,)),
-        pltpu.SemaphoreType.DMA((total,)),
-    ]
-
-
-def unplace_kernel(shapes, order_ref, *refs):
-    mats, (slots_ref, hold, sem_in, sem_out) = refs[:-4], refs[-4:]
-    total = slots_ref.shape[0]
-    move_blocks(
-        [
-            pltpu.make_async_copy(tile_of(mats, shapes, b), hold.at[b], sem_in.at[b])
-            for b in range(total)
-        ],
-        [
-            pltpu.make_async_copy(hold.at[b], slots_ref.at[order_ref[b]], sem_out.at[b])
-            for b in range(total)
-        ],
-    )
-
-
-def unplace_blocks(mats, order):
-    shapes = [m.shape for m in mats]
+def unplace_kernel(order_ref, blocks_ref, slots_ref, hold, sem_in, sem_out):
+    total = blocks_ref.shape[0]
+    chunk = total // sem_in.shape[0]
+
+    def read(i):
+        part = pl.ds(i * chunk, chunk)
+        return pltpu.make_async_copy(blocks_ref.at[part], hold.at[part], sem_in.at[i])
+
+    def write(b):
+        return pltpu.make_async_copy(hold.at[b], slots_ref.at[order_ref[b]], sem_out.at[b])
+
+    for i in range(total // chunk):
+        read(i).start()
+    for i in range(total // chunk):
+        read(i).wait()
+        for b in range(i * chunk, (i + 1) * chunk):
+            write(b).start()
+    for b in range(total):
+        write(b).wait()
+
+
+def unplace_blocks(blocks, order):
     total = order.shape[0]
     return pl.pallas_call(
-        functools.partial(unplace_kernel, shapes),
+        unplace_kernel,
         grid_spec=pltpu.PrefetchScalarGridSpec(
             num_scalar_prefetch=1,
             grid=(1,),
-            in_specs=[ANY] * len(mats),
+            in_specs=[ANY],
             out_specs=ANY,
-            scratch_shapes=block_scratch(total),
+            scratch_shapes=[
+                pltpu.VMEM((total, B, B), LOW),
+                pltpu.SemaphoreType.DMA((48,)),
+                pltpu.SemaphoreType.DMA((total,)),
+            ],
         ),
         out_shape=jax.ShapeDtypeStruct((total, B, B), LOW),
         compiler_params=pltpu.CompilerParams(vmem_limit_bytes=VMEM_BYTES),
         name="unplace_blocks",
-    )(order, *mats)
+    )(order, blocks)
 
 
 PIECES = 4
@@ -434,10 +416,25 @@
     return index
 
 
+def segments(qkv, od, up):
+    wide, down = od.shape[1] // B, up.shape[1] // B
+    out = od.shape[0] // B - down
+    deep, cols = qkv.shape[0] // B, qkv.shape[1] // B
+    starts = [deep * cols, out * wide, deep * down]
+    return (
+        (qkv, 0, deep, cols, 0),
+        (od, 0, out, wide, starts[0]),
+        (up, 0, deep, down, sum(starts[:2])),
+        (od, out, down, wide, sum(starts)),
+    )
+
+
 def gather_kernel(
-    shapes,
     order_ref,
+    len_ref,
+    place_ref,
     vec_ref,
+    freq_ref,
     w_hbm,
     x_hbm,
     cot_hbm,
@@ -446,12 +443,14 @@
     up_hbm,
     h1_hbm,
     h2_hbm,
+    table_hbm,
     sum_ref,
     slots,
     wide,
     x_buf,
     c_buf,
     h_buf,
+    table_buf,
     stage,
     send_sem,
     recv_sem,
@@ -506,6 +505,9 @@
         return (
             pltpu.make_async_copy(h_buf.at[slot, 0], h1_hbm.at[tile(i), :], norm_sem.at[0, slot]),
             pltpu.make_async_copy(h_buf.at[slot, 1], h2_hbm.at[tile(i), :], norm_sem.at[1, slot]),
+            pltpu.make_async_copy(
+                table_buf.at[slot], table_hbm.at[:, tile(i), :], norm_sem.at[2, slot]
+            ),
         )
 
     def norm_step(i, slot, first):
@@ -524,6 +526,17 @@
         h_buf[slot, 0] = (xhat * vec_ref[0:1, :] + vec_ref[1:2, :]).astype(LOW)
         h_buf[slot, 1] = (xhat * vec_ref[2:3, :] + vec_ref[3:4, :]).astype(LOW)
         sum_ref[0:1, :] += jnp.sum(c_buf[slot].astype(WIDE), axis=0, keepdims=True)
+        row = lax.broadcasted_iota(jnp.int32, (STEP, 128), 0) + i * STEP
+        first = jnp.zeros((STEP, 128), jnp.int32)
+        end = jnp.int32(0)
+        for j in range(len_ref.shape[0]):
+            mine = place_ref[j] == me
+            end = end + jnp.where(mine, len_ref[j], 0)
+            first = jnp.where(row >= jnp.where(mine, end, 1 << 30), end, first)
+        angle = (row - first).astype(WIDE) * freq_ref[...]
+        table_buf[slot, 0] = jnp.cos(angle)
+        table_buf[slot, 1] = jnp.sin(angle)
+        table_buf[slot, 2] = first.astype(WIDE)
         for copy in keep(i, slot):
             copy.start()
 
@@ -579,16 +592,16 @@
         for q in range(PIECES):
             arrived(source, q)
 
-    block = 0
-    for ref, (rows, cols) in zip((qkv_hbm, od_hbm, up_hbm), shapes):
-        across = cols // B
+    for ref, skip, panels, across, block in segments(qkv_hbm, od_hbm, up_hbm):
 
         def panel(i, slot):
             return pltpu.make_async_copy(
-                stage.at[slot, :, pl.ds(0, cols)], ref.at[lane(i * B), :], stage_sem.at[slot]
+                stage.at[slot, :, pl.ds(0, across * B)],
+                ref.at[lane((skip + i) * B), :],
+                stage_sem.at[slot],
             )
 
-        @pl.loop(0, rows // B // 2)
+        @pl.loop(0, panels // 2)
         def _(k):
             for slot in range(2):
                 i = k * 2 + slot
@@ -603,7 +616,6 @@
 
         for slot in range(2):
             panel(slot, slot).wait()
-        block += rows // B * across
 
     for source, target in ROUTES:
         for q in range(PIECES):
@@ -614,21 +626,20 @@
             send(source, target, q).wait_send()
 
 
-def gather_weights(blocks, order, tokens, cotangent, vectors, shapes):
+def gather_weights(blocks, order, seq_len, seq_device, tokens, cotangent, vectors, shapes):
     rows, d = tokens.shape
     each = blocks.shape[0]
+    half = 10000.0 ** (-2.0 * jnp.arange(ROT // 2, dtype=WIDE) / ROT)
+    frequency = jnp.concatenate([half, half, jnp.zeros((128 - ROT,), WIDE)])[None]
+    smem = pl.BlockSpec(memory_space=pltpu.SMEM)
+    vmem = pl.BlockSpec(memory_space=pltpu.VMEM)
     return pl.pallas_call(
-        functools.partial(gather_kernel, shapes),
-        in_specs=[
-            pl.BlockSpec(memory_space=pltpu.SMEM),
-            pl.BlockSpec(memory_space=pltpu.VMEM),
-            ANY,
-            ANY,
-            ANY,
-        ],
-        out_specs=[ANY] * 5 + [pl.BlockSpec(memory_space=pltpu.VMEM)],
+        gather_kernel,
+        in_specs=[smem, smem, smem, vmem, vmem, ANY, ANY, ANY],
+        out_specs=[ANY] * 6 + [vmem],
         out_shape=[jax.ShapeDtypeStruct(s, LOW) for s in shapes]
         + [jax.ShapeDtypeStruct((rows, d), LOW)] * 2
+        + [jax.ShapeDtypeStruct((3, rows, 128), WIDE)]
         + [jax.ShapeDtypeStruct((8, d), WIDE)],
         scratch_shapes=[
             pltpu.VMEM((order.shape[0], B, B), LOW),
@@ -636,12 +647,13 @@
             pltpu.VMEM((2, STEP, d), LOW),
             pltpu.VMEM((2, STEP, d), LOW),
             pltpu.VMEM((2, 2, STEP, d), LOW),
+            pltpu.VMEM((2, 3, STEP, 128), WIDE),
             pltpu.VMEM((2, B, d), LOW),
             pltpu.SemaphoreType.DMA((8, PIECES)),
             pltpu.SemaphoreType.DMA((8, PIECES)),
             pltpu.SemaphoreType.DMA((2,)),
             pltpu.SemaphoreType.DMA((2, 2)),
-            pltpu.SemaphoreType.DMA((2, 2)),
+            pltpu.SemaphoreType.DMA((3, 2)),
             pltpu.SemaphoreType.DMA((2,)),
         ],
         compiler_params=pltpu.CompilerParams(
@@ -651,7 +663,7 @@
             flops=100_000_000_000, bytes_accessed=80 << 20, transcendentals=0
         ),
         name="gather_weights",
-    )(order, vectors, blocks, tokens, cotangent)
+    )(order, seq_len, seq_device, vectors, frequency, blocks, tokens, cotangent)
 
 
 def turn(values, cos, sin, back=False):
@@ -661,7 +673,7 @@
     return values * cos - other * sin if back else values * cos + other * sin
 
 
-def qkv_kernel(scale, h_ref, w_ref, bias_ref, cos_ref, sin_ref, q_ref, k_ref, v_ref):
+def qkv_kernel(scale, h_ref, w_ref, bias_ref, table_ref, q_ref, k_ref, v_ref):
     for j in range(w_ref.shape[1] // HD):
         head, part = divmod(j, 3)
         cols = slice(head * HD, head * HD + HD)
@@ -669,7 +681,7 @@
         if part == 2:
             v_ref[:, cols] = proj.astype(LOW)
             continue
-        front = turn(proj[:, :128], cos_ref[...], sin_ref[...])
+        front = turn(proj[:, :128], table_ref[0], table_ref[1])
         turned = jnp.concatenate([front, proj[:, 128:]], axis=1).astype(LOW)
         if part == 0:
             q_ref[:, cols] = (turned.astype(WIDE) * scale).astype(LOW)
@@ -677,7 +689,7 @@
             k_ref[:, cols] = turned
 
 
-def project_qkv(h1, qkv_w, bias, tables):
+def project_qkv(h1, qkv_w, bias, table):
     rows, d = h1.shape
     cols = qkv_w.shape[1]
     out_cols = cols // 3
@@ -686,95 +698,77 @@
     return pl.pallas_call(
         functools.partial(qkv_kernel, 1.0 / math.sqrt(HD)),
         grid=(rows // tile,),
-        in_specs=[row_spec(d), resident((d, cols)), resident((1, cols))] + [row_spec(128)] * 2,
+        in_specs=[
+            row_spec(d),
+            resident((d, cols)),
+            resident(bias.shape),
+            pl.BlockSpec((3, tile, 128), lambda i: (0, i, 0)),
+        ],
         out_specs=[row_spec(out_cols)] * 3,
         out_shape=[jax.ShapeDtypeStruct((rows, out_cols), LOW)] * 3,
         compiler_params=pltpu.CompilerParams(vmem_limit_bytes=VMEM_BYTES),
         name="project_qkv",
-    )(h1, qkv_w, bias, *tables)
-
-
-def attention_kernel(
-    tile,
-    start_ref,
-    q_ref,
-    k_ref,
-    v_ref,
-    cot_ref,
-    out_ref,
-    ctx_ref,
-    grad_ref,
-    stats_ref,
-    s_scr,
-):
-    step = pl.program_id(1)
+    )(h1, qkv_w, bias, table)
+
+
+def attention_kernel(tile, table_ref, q_ref, k_ref, v_ref, ctx_ref, stats_ref, s_scr):
+    step = pl.program_id(0)
+    heads = q_ref.shape[1] // HD
+    lanes = lax.broadcasted_iota(jnp.int32, (tile, 128), 1)
 
     def rows(c):
-        q = q_ref[...]
-        first = start_ref[...]
-        top = jnp.full((tile, 1), masked_score, WIDE)
-        for j in range(c + 1):
-            keys = slice(j * tile, (j + 1) * tile)
-            s = dot_nt(q, k_ref[keys, :])
-            col = lax.broadcasted_iota(jnp.int32, (tile, tile), 1) + j * tile
-            ok = col >= first
-            if j == c:
-                row = lax.broadcasted_iota(jnp.int32, (tile, tile), 0) + c * tile
-                ok = ok & (col <= row)
-            s = jnp.where(ok, s, masked_score)
-            s_scr[:, keys] = s
-            top = jnp.maximum(top, jnp.max(s, axis=1, keepdims=True))
-        total = jnp.zeros((tile, 1), WIDE)
-        ctx = jnp.zeros((tile, HD), WIDE)
-        for j in range(c + 1):
-            keys = slice(j * tile, (j + 1) * tile)
-            e = jnp.exp(s_scr[:, keys] - top)
-            total = total + jnp.sum(e, axis=1, keepdims=True)
-            ctx = ctx + dot(e.astype(LOW), v_ref[keys, :])
-        ctx = ctx * (1.0 / total)
-        grad = dot_nt(cot_ref[...], out_ref[...]).astype(LOW)
-        delta = jnp.sum(ctx * grad.astype(WIDE), axis=1, keepdims=True)
-        ctx_ref[...] = ctx.astype(LOW)
-        grad_ref[...] = grad
-        lanes = lax.broadcasted_iota(jnp.int32, (tile, 128), 1)
-        stats_ref[...] = jnp.where(
-            lanes == 0, top + jnp.log(total), jnp.where(lanes == 1, delta, first.astype(WIDE))
-        )
+        first = table_ref[0][:, 0:1].astype(jnp.int32)
+        stats = jnp.broadcast_to(first.astype(WIDE), (tile, 128))
+        for h in range(heads):
+            cols = slice(h * HD, (h + 1) * HD)
+            q = q_ref[:, cols]
+            top = jnp.full((tile, 1), masked_score, WIDE)
+            for j in range(c + 1):
+                keys = slice(j * tile, (j + 1) * tile)
+                s = dot_nt(q, k_ref[keys, cols])
+                col = lax.broadcasted_iota(jnp.int32, (tile, tile), 1) + j * tile
+                ok = col >= first
+                if j == c:
+                    row = lax.broadcasted_iota(jnp.int32, (tile, tile), 0) + c * tile
+                    ok = ok & (col <= row)
+                s = jnp.where(ok, s, masked_score)
+                s_scr[h, :, keys] = s
+                top = jnp.maximum(top, jnp.max(s, axis=1, keepdims=True))
+            total = jnp.zeros((tile, 1), WIDE)
+            ctx = jnp.zeros((tile, HD), WIDE)
+            for j in range(c + 1):
+                keys = slice(j * tile, (j + 1) * tile)
+                e = jnp.exp(s_scr[h, :, keys] - top)
+                total = total + jnp.sum(e, axis=1, keepdims=True)
+                ctx = ctx + dot(e.astype(LOW), v_ref[keys, cols])
+            ctx_ref[:, cols] = (ctx * (1.0 / total)).astype(LOW)
+            stats = jnp.where(lanes == h, top + jnp.log(total), stats)
+        stats_ref[...] = stats
 
     for c in range(k_ref.shape[0] // tile):
         pl.when(step == c)(functools.partial(rows, c))
 
 
-def attention_forward_rows(start, q, k, v, cotangent, od_w):
+def attention_forward_rows(table, q, k, v):
     rows, cols = q.shape
-    d = cotangent.shape[1]
-    heads = cols // HD
     tile = 512
-    tile_spec = pl.BlockSpec((tile, HD), lambda h, i: (i, h))
-    full_spec = pl.BlockSpec((rows, HD), lambda h, i: (0, h))
-    flops = heads * rows * rows * HD * 3
+    tile_spec = pl.BlockSpec((tile, cols), lambda i: (i, 0))
+    full_spec = resident((rows, cols))
+    flops = rows * rows * cols * 3
     return pl.pallas_call(
         functools.partial(attention_kernel, tile),
-        grid=(heads, rows // tile),
-        in_specs=[
-            pl.BlockSpec((tile, 1), lambda h, i: (i, 0)),
-            tile_spec,
-            full_spec,
-            full_spec,
-            pl.BlockSpec((tile, d), lambda h, i: (i, 0)),
-            pl.BlockSpec((HD, d), lambda h, i: (h, 0)),
-        ],
-        out_specs=[tile_spec, tile_spec, pl.BlockSpec((tile, 128), lambda h, i: (i, h))],
+        grid=(rows // tile,),
+        in_specs=[pl.BlockSpec((1, tile, 128), lambda i: (2, i, 0)), tile_spec, full_spec, full_spec],
+        out_specs=[tile_spec, pl.BlockSpec((tile, 128), lambda i: (i, 0))],
         out_shape=[
             jax.ShapeDtypeStruct((rows, cols), LOW),
-            jax.ShapeDtypeStruct((rows, cols), LOW),
-            jax.ShapeDtypeStruct((rows, heads * 128), WIDE),
+            jax.ShapeDtypeStruct((rows, 128), WIDE),
         ],
-        scratch_shapes=[pltpu.VMEM((tile, rows), WIDE)],
+        scratch_shapes=[pltpu.VMEM((cols // HD, tile, rows), WIDE)],
         compiler_params=pltpu.CompilerParams(vmem_limit_bytes=VMEM_BYTES),
         cost_estimate=pl.CostEstimate(flops=flops, bytes_accessed=30 << 20, transcendentals=0),
         name="attention_forward",
-    )(start, q, k, v, cotangent, od_w)
+    )(table, q, k, v)
 
 
 class Line:
@@ -905,10 +899,19 @@
                 self.down(pair).wait_recv()
 
     def tick(self, step, lag, base):
-        @pl.when(jnp.logical_not(self.inner) & (step < TICKS))
+        ahead = GOT // PER_STEP
+
+        @pl.when(jnp.logical_not(self.inner) & (step < ahead))
+        def _():
+            for s in range(PER_STEP):
+                self.send_up(step * PER_STEP + s)
+
+        @pl.when(
+            jnp.logical_not(self.inner) & (step >= ahead) & (step < ahead + (PAIRS - GOT) // 2)
+        )
         def _():
             for s in range(2):
-                self.send_up(step * 2 + s)
+                self.send_up(GOT + (step - ahead) * 2 + s)
 
         @pl.when(self.inner & (step >= lag + 2) & (step < lag + 2 + TICKS))
         def _():
@@ -972,7 +975,7 @@
     part_ref[pl.ds(step * PER_STEP, PER_STEP), :, :, cols] = value
 
 
-FORWARD_LAG = 2
+FORWARD_LAG = 1
 FORWARD_GRID = FORWARD_LAG + TICKS + 2
 
 
@@ -987,10 +990,10 @@
     g_ref,
     ctx_ref,
     x_ref,
+    stats_ref,
     bias_ref,
-    shift_ref,
-    cos_ref,
-    sin_ref,
+    vec_ref,
+    table_ref,
     up_hbm,
     od_hbm,
     h1_hbm,
@@ -1000,14 +1003,10 @@
     q_hbm,
     k_hbm,
     v_hbm,
-    cg_hbm,
-    stats_hbm,
     out_ref,
     hg_hbm,
     qg_hbm,
-    wq_hbm,
-    wo_hbm,
-    wu_hbm,
+    wg_hbm,
     sums_ref,
     qkv_sums_ref,
     up_buf,
@@ -1018,6 +1017,7 @@
     got,
     across,
     sems,
+    grad_all,
     stats,
     dq_scr,
     dk_scr,
@@ -1060,15 +1060,12 @@
 
     def load_head(h):
         cols = pl.ds(pl.multiple_of(h * HD, HD), HD)
-        copies = [
+        return [
             pltpu.make_async_copy(
                 src.at[:, cols], act_all.at[:, pl.ds(i * HD, HD)], head_sem.at[i]
             )
-            for i, src in enumerate((q_hbm, k_hbm, v_hbm, cg_hbm))
+            for i, src in enumerate((q_hbm, k_hbm, v_hbm))
         ]
-        lanes = pl.ds(pl.multiple_of(h * 128, 128), 128)
-        copies.append(pltpu.make_async_copy(stats_hbm.at[:, lanes], stats, head_sem.at[4]))
-        return copies
 
     def store_qg():
         return pltpu.make_async_copy(hg_all.at[:, pl.ds(0, qkv_cols)], qg_hbm, head_sem.at[5])
@@ -1087,12 +1084,14 @@
             hg_all.at[part_rows, :], hg_hbm.at[part_rows, :], hg_sem.at[i]
         )
 
-    def stage_out(dst, row, cols, slot):
+    def stage_out(block, j, slot):
         return pltpu.make_async_copy(
-            stage.at[lane(slot * B), pl.ds(0, cols)],
-            dst.at[lane(row), :],
-            stage_sem.at[slot],
-        )
+            stage.at[lane(slot * B), pl.ds(j * B, B)], wg_hbm.at[block + j], stage_sem.at[slot]
+        )
+
+    def stage_wait(cols, slot):
+        place = stage.at[lane(slot * B), pl.ds(0, cols)]
+        pltpu.make_async_copy(place, place, stage_sem.at[slot]).wait()
 
     @pl.when(step == 0)
     def _():
@@ -1114,7 +1113,8 @@
                 load_up(n).wait()
                 load_down(n).wait()
 
-            hidden = dot(h_ref[...], up_buf[:, cols]) + bias_ref[:, cols]
+            bias = bias_ref[:, qkv_cols + n * width : qkv_cols + (n + 1) * width]
+            hidden = dot(h_ref[...], up_buf[:, cols]) + bias
             act_grad = dot_nt(g_ref[...], od_buf[heads + n * width : heads + (n + 1) * width, :])
             cdf, density = gelu_parts(hidden)
             act_all[here, cols] = (hidden * cdf).astype(LOW)
@@ -1127,6 +1127,15 @@
             load_out().wait()
 
         store_hg(step).start()
+        grad = dot_nt(g_ref[...], od_buf[:heads, :]).astype(LOW)
+        grad_all[here, :] = grad
+        lanes = lax.broadcasted_iota(jnp.int32, (STEP, 128), 1)
+        info = stats_ref[...]
+        for h in range(heads // HD):
+            cols = slice(h * HD, (h + 1) * HD)
+            both = ctx_ref[:, cols].astype(WIDE) * grad[:, cols].astype(WIDE)
+            info = jnp.where(lanes == 64 + h, jnp.sum(both, axis=1, keepdims=True), info)
+        stats[here, :] = info
         for n in range(od_buf.shape[1] // width):
             cols = slice(n * width, (n + 1) * width)
             value = dot(ctx_ref[...], od_buf[:heads, cols]) + dot(
@@ -1139,19 +1148,25 @@
         panel(h2_hbm, 0, 0).start()
         load_cot().start()
 
-    def unit(index, a_t, b_ref, cols, dst, row):
+    wide = od_buf.shape[1] // B
+    out_first = rows // B * (qkv_cols // B)
+    up_first = out_first + heads // B * wide
+    down_first = up_first + rows // B * (units // B)
+
+    def unit(index, a_t, b_ref, cols, first):
         slot = index % 2
 
         @pl.when(index >= 2)
         def _():
-            stage_out(dst, row, cols, slot).wait()
+            stage_wait(cols, slot)
 
         weight_unit(a_t, b_ref, cols, stage, slot)
-        stage_out(dst, row, cols, slot).start()
-
-    def settle(dst, cols):
+        for j in range(cols // B):
+            stage_out(first + index * (cols // B), j, slot).start()
+
+    def settle(cols):
         for slot in range(2):
-            stage_out(dst, 0, cols, slot).wait()
+            stage_wait(cols, slot)
 
     @pl.when((step == 8) | (step == 9))
     def _():
@@ -1164,11 +1179,11 @@
             def _():
                 panel(h2_hbm, i + 1, (i + 1) % 2).start()
 
-            unit(i, up_buf[:, panel_cols(i % 2)].T, hg_all, units, wu_hbm, i * B)
+            unit(i, up_buf[:, panel_cols(i % 2)].T, hg_all, units, up_first)
 
     @pl.when(step == 10)
     def _():
-        settle(wu_hbm, units)
+        settle(units)
         load_cot().wait()
 
     @pl.when((step == 10) | (step == 11))
@@ -1177,7 +1192,7 @@
         def _(k):
             i = (step - 10) * 4 + k
             cot = od_buf.at[pl.ds(0, rows), :]
-            unit(i, act_all[:, lane(i * B)].T, cot, units, wo_hbm, heads + i * B)
+            unit(i, act_all[:, lane(i * B)].T, cot, wide * B, down_first)
 
     @pl.when(step == 11)
     def _():
@@ -1186,7 +1201,7 @@
 
     @pl.when(step == 12)
     def _():
-        settle(wo_hbm, units)
+        settle(wide * B)
 
         @pl.loop(0, STEPS)
         def _(i):
@@ -1204,7 +1219,7 @@
             hg_all[tile_rows(i), cols] = values.astype(LOW)
 
         def turned_back(i, values):
-            front = turn(values[:, :128], cos_ref[tile_rows(i), :], sin_ref[tile_rows(i), :], True)
+            front = turn(values[:, :128], table_ref[0, tile_rows(i), :], table_ref[1, tile_rows(i), :], True)
             return jnp.concatenate([front, values[:, 128:]], axis=1)
 
         @pl.loop(start, stop)
@@ -1217,9 +1232,10 @@
             @pl.loop(j, count)
             def _(i):
                 q = act_all[tile_rows(i), 0:HD]
-                g = act_all[tile_rows(i), 3 * HD : 4 * HD]
+                g = grad_all[tile_rows(i), pl.ds(pl.multiple_of(h * HD, HD), HD)]
                 info = stats[tile_rows(i), :]
-                log_total, delta = info[:, 0:1], info[:, 1:2]
+                log_total = jnp.where(h == 0, info[:, 0:1], info[:, 1:2])
+                delta = jnp.where(h == 0, info[:, 64:65], info[:, 65:66])
                 first = info[:, 2:3].astype(jnp.int32) - j * tile
                 col = lax.broadcasted_iota(jnp.int32, (tile, tile), 1)
                 row = lax.broadcasted_iota(jnp.int32, (tile, tile), 0) + (i - j) * tile
@@ -1271,9 +1287,9 @@
         @pl.loop(0, 2)
         def _(j):
             cot = od_buf.at[pl.ds(0, rows), :]
-            unit(j, up_buf[:, panel_cols(j)].T, cot, units, wo_hbm, j * B)
-
-        settle(wo_hbm, units)
+            unit(j, up_buf[:, panel_cols(j)].T, cot, wide * B, out_first)
+
+        settle(wide * B)
         panel(h1_hbm, 0, 0).start()
 
     @pl.when((step == 17) | (step == 18))
@@ -1288,16 +1304,16 @@
                 panel(h1_hbm, i + 1, (i + 1) % 2).start()
 
             grads = hg_all.at[:, pl.ds(0, qkv_cols)]
-            unit(i, up_buf[:, panel_cols(i % 2)].T, grads, qkv_cols, wq_hbm, i * B)
-
-    @pl.when(step == 19)
-    def _():
-        settle(wq_hbm, qkv_cols)
+            unit(i, up_buf[:, panel_cols(i % 2)].T, grads, qkv_cols, 0)
+
+    @pl.when(step == FORWARD_GRID - 1)
+    def _():
+        settle(qkv_cols)
         store_qg().wait()
 
     def base(s):
         near = pl.ds(pl.multiple_of(s * 2 * SUB + line.near * SUB, SUB), SUB)
-        return x_ref[near, :].astype(WIDE) + shift_ref[...]
+        return x_ref[near, :].astype(WIDE) + (vec_ref[4:5, :] + vec_ref[5:6, :])
 
     line.tick(step, FORWARD_LAG, base)
 
@@ -1306,35 +1322,33 @@
         line.drain()
 
 
-def forward_line(
-    h1, h2, cotangent, ctx, heads, stats, tables, tokens, up_w, od_w, bias, shift
-):
+def forward_line(h1, h2, cotangent, ctx, heads, stats, table, tokens, up_w, od_w, bias, vectors):
     rows, d = tokens.shape
     units = up_w.shape[1]
-    qkv_cols = 3 * ctx.shape[1]
+    head_cols = ctx.shape[1]
+    qkv_cols = 3 * head_cols
+    total = (d * qkv_cols + od_w.shape[0] * d + d * units) // (B * B)
     return pl.pallas_call(
         forward_kernel,
         grid=(FORWARD_GRID,),
         in_specs=[
             row_block(d),
             row_block(d),
-            row_block(ctx.shape[1]),
+            row_block(head_cols),
             base_block(d, FORWARD_LAG),
+            row_block(128),
             resident(bias.shape),
-            resident(shift.shape),
-            resident((rows, 128)),
-            resident((rows, 128)),
+            resident(vectors.shape),
+            resident((2, rows, 128)),
         ]
-        + [ANY] * 11,
-        out_specs=[ANY] * 6
+        + [ANY] * 9,
+        out_specs=[ANY] * 4
         + [pl.BlockSpec((8, units), lambda i: (0, 0)), pl.BlockSpec((8, qkv_cols), lambda i: (0, 0))],
         out_shape=[
             jax.ShapeDtypeStruct((rows, d), LOW),
             jax.ShapeDtypeStruct((rows, units), LOW),
             jax.ShapeDtypeStruct((rows, qkv_cols), LOW),
-            jax.ShapeDtypeStruct((d, qkv_cols), LOW),
-            jax.ShapeDtypeStruct(od_w.shape, LOW),
-            jax.ShapeDtypeStruct((d, units), LOW),
+            jax.ShapeDtypeStruct((total, B, B), LOW),
             jax.ShapeDtypeStruct((8, units), WIDE),
             jax.ShapeDtypeStruct((8, qkv_cols), WIDE),
         ],
@@ -1346,6 +1360,7 @@
         ]
         + line_scratch(d)
         + [
+            pltpu.VMEM((rows, head_cols), LOW),
             pltpu.VMEM((rows, 128), WIDE),
             pltpu.VMEM((rows, HD), WIDE),
             pltpu.VMEM((512, HD), WIDE),
@@ -1368,9 +1383,10 @@
         cotangent,
         ctx,
         tokens,
+        stats,
         bias,
-        shift,
-        *tables,
+        vectors,
+        table,
         up_w,
         od_w,
         h1,
@@ -1378,7 +1394,6 @@
         ctx,
         cotangent,
         *heads,
-        stats,
     )
 
 
@@ -1457,9 +1472,10 @@
     g_ref,
     qkv_ref,
     up_ref,
-    one_ref,
-    two_ref,
-    sums_in,
+    vec_ref,
+    cot_sums,
+    qkv_sums,
+    hidden_sums,
     sums_ref,
     out_ref,
     gc_scr,
@@ -1482,7 +1498,10 @@
     @pl.when(step == 0)
     def _():
         spread.greet()
-        own[...] = sums_in[...]
+        own[...] = jnp.zeros_like(own)
+        own[4:5, :] = cot_sums[0:1, :]
+        own[5:6, : qkv_sums.shape[1]] = qkv_sums[0:1, :]
+        own[6:7, : hidden_sums.shape[1]] = hidden_sums[0:1, :]
 
     @pl.when(step < STEPS)
     def _():
@@ -1497,7 +1516,7 @@
             e1 = dot_nt(qg_ref[...], qkv_ref[cols, :])
             e2 = dot_nt(hg_ref[...], up_ref[cols, :])
             xhat = xhat_scr[:, cols]
-            gc = e1 * one_ref[:, cols] + e2 * two_ref[:, cols]
+            gc = e1 * vec_ref[0:1, cols] + e2 * vec_ref[2:3, cols]
             gc_scr[:, cols] = gc
             mean = mean + jnp.sum(gc, axis=1, keepdims=True)
             slope = slope + jnp.sum(gc * xhat, axis=1, keepdims=True)
@@ -1535,9 +1554,9 @@
         sums_ref[...] = jnp.where(row < 4, total, own[...])
 
 
-def backward_line(qkv_grad, hidden_grad, tokens, cotangent, qkv_w, up_w, gain_one, gain_two, sums):
+def backward_line(qkv_grad, hidden_grad, tokens, cotangent, qkv_w, up_w, vectors, *sums):
     rows, d = tokens.shape
-    small = sums.shape
+    small = (8, d)
     return pl.pallas_call(
         backward_kernel,
         grid=(BACKWARD_GRID,),
@@ -1548,10 +1567,9 @@
             base_block(d, BACKWARD_LAG),
             resident(qkv_w.shape),
             resident(up_w.shape),
-            resident((1, d)),
-            resident((1, d)),
-            resident(small),
-        ],
+            resident(vectors.shape),
+        ]
+        + [resident(part.shape) for part in sums],
         out_specs=[pl.BlockSpec(small, lambda i: (0, 0)), ANY],
         out_shape=[jax.ShapeDtypeStruct(small, WIDE), jax.ShapeDtypeStruct((rows, d), LOW)],
         scratch_shapes=[
@@ -1571,7 +1589,7 @@
         ),
         name="backward_line",
     )(
-        qkv_grad, hidden_grad, tokens, cotangent, qkv_w, up_w, gain_one, gain_two, sums
+        qkv_grad, hidden_grad, tokens, cotangent, qkv_w, up_w, vectors, *sums
     )
 
 
@@ -1587,12 +1605,23 @@
     rs_ref,
     lr_ref,
     rr_ref,
+    sums_ref,
+    vec_ref,
+    vec_stat_ref,
+    unit_ref,
+    unit_stat_ref,
     one_in,
     two_in,
     grad_ref,
     left_ref,
     right_ref,
     weight_ref,
+    vec_grad_out,
+    vec_stat_out,
+    vec_out,
+    unit_grad_out,
+    unit_stat_out,
+    unit_out,
     one_out,
     two_out,
     hold,
@@ -1607,6 +1636,17 @@
     def _():
         for copy in fetch:
             copy.start()
+        vec_grad_out[0:5, :] = sums_ref[0:5, :]
+        vec_grad_out[5:6, :] = sums_ref[4:5, :]
+        vec_stat_out[...], vec_out[...] = vector_update(
+            vec_ref[...], vec_stat_ref[...], vec_grad_out[...]
+        )
+        qkv_cols = unit_ref.shape[1] * 3 // 7
+        unit_grad_out[:, :qkv_cols] = sums_ref[5:6, :qkv_cols]
+        unit_grad_out[:, qkv_cols:] = sums_ref[6:7, : unit_ref.shape[1] - qkv_cols]
+        unit_stat_out[...], unit_out[...] = vector_update(
+            unit_ref[...], unit_stat_ref[...], unit_grad_out[...]
+        )
 
     for i in range(2):
 
@@ -1636,24 +1676,27 @@
         weight_ref[n] = weight - direction * (step_share * weight_size / step_size)
 
 
-def shampoo(grads, weights, left_stat, right_stat, left_root, right_root, one, two):
+def shampoo(grads, weights, left_stat, right_stat, left_root, right_root, small, one, two):
     count = grads.shape[0]
     group = 2
     spec = pl.BlockSpec((group, B, B), lambda i: (i, 0, 0))
+    results = [small[1]] * 3 + [small[3]] * 3
     return pl.pallas_call(
         shampoo_kernel,
         grid=(count // group,),
-        in_specs=[spec] * 6 + [ANY] * 2,
-        out_specs=[spec] * 4 + [ANY] * 2,
+        in_specs=[spec] * 6 + [resident(part.shape) for part in small] + [ANY] * 2,
+        out_specs=[spec] * 4
+        + [pl.BlockSpec(part.shape, lambda i: (0, 0)) for part in results]
+        + [ANY] * 2,
         out_shape=[jax.ShapeDtypeStruct((count, B, B), WIDE)] * 4
-        + [jax.ShapeDtypeStruct(one.shape, one.dtype)] * 2,
+        + [jax.ShapeDtypeStruct(part.shape, part.dtype) for part in results + [one, two]],
         scratch_shapes=[
             pltpu.VMEM((2,) + one.shape, one.dtype),
             pltpu.SemaphoreType.DMA((2, 2)),
         ],
         compiler_params=pltpu.CompilerParams(vmem_limit_bytes=VMEM_BYTES),
         name="shampoo",
-    )(grads, weights, left_stat, right_stat, left_root, right_root, one, two)
+    )(grads, weights, left_stat, right_stat, left_root, right_root, *small, one, two)
 
 
 def per_device_line(
@@ -1673,66 +1716,33 @@
     unit_stat,
 ):
     groups = lax.axis_size("mp")
-    device = lax.axis_index("dp")
-    row_count, d = tokens.shape
+    d = tokens.shape[1]
     qkv_cols = 3 * d // groups
     head_cols = d // groups
     unit_cols = FF // groups
-    segment, position = segment_layout(seq_len, seq_device, device, row_count)
-    start = (jnp.arange(row_count, dtype=jnp.int32) - position)[:, None]
-    frequency = 10000.0 ** (-2.0 * jnp.arange(ROT // 2, dtype=WIDE) / ROT)
-    angles = position.astype(WIDE)[:, None] * frequency[None, :]
-    cos, sin = jnp.cos(angles), jnp.sin(angles)
-    pad = jnp.zeros((row_count, 128 - ROT), WIDE)
-    tables = (
-        jnp.concatenate([cos, cos, pad + 1.0], axis=1),
-        jnp.concatenate([sin, sin, pad], axis=1),
-    )
-    shift = (vectors[4] + vectors[5])[None]
-    unit_shift = unit_bias[0]
-
     shapes = ((d, qkv_cols), (head_cols + unit_cols, d), (d, unit_cols))
-    blocks = [(a // B) * (b // B) for a, b in ((d, qkv_cols), (head_cols, d), (d, unit_cols))]
-    order = jnp.concatenate(
-        [
-            owner_map[: blocks[0] + blocks[1]],
-            owner_map[blocks[0] + blocks[1] + blocks[2] :],
-            owner_map[blocks[0] + blocks[1] : blocks[0] + blocks[1] + blocks[2]],
-        ]
-    )
-    qkv_w, od_w, up_w, normed_one, normed_two, out_sum = gather_weights(
-        weight_blocks[0], order, tokens, cotangent, vectors, shapes
-    )
-
-    q, k, v = project_qkv(normed_one, qkv_w, unit_shift[None, :qkv_cols], tables)
-    ctx, ctx_grad, stats = attention_forward_rows(start, q, k, v, cotangent, od_w)
-    block_out, hidden_grad, qkv_grad, qkv_wg, od_wg, up_wg, hidden_sums, qkv_sums = forward_line(
+    qkv_w, od_w, up_w, normed_one, normed_two, table, cot_sums = gather_weights(
+        weight_blocks[0], owner_map, seq_len, seq_device, tokens, cotangent, vectors, shapes
+    )
+    q, k, v = project_qkv(normed_one, qkv_w, unit_bias, table)
+    ctx, stats = attention_forward_rows(table, q, k, v)
+    block_out, hidden_grad, qkv_grad, weight_grads, hidden_sums, qkv_sums = forward_line(
         normed_one,
         normed_two,
         cotangent,
         ctx,
-        (q, k, v, ctx_grad),
+        (q, k, v),
         stats,
-        tables,
+        table,
         tokens,
         up_w,
         od_w,
-        unit_shift[None, qkv_cols:],
-        shift,
-    )
-    slots = unplace_blocks([qkv_wg, od_wg, up_wg], order)
+        unit_bias,
+        vectors,
+    )
+    slots = unplace_blocks(weight_grads, owner_map)
     owned = lax.psum_scatter(slots, "dp", scatter_dimension=0, tiled=True)
     qkv_grad, hidden_grad, slots = lax.optimization_barrier((qkv_grad, hidden_grad, slots))
-    sums = jnp.concatenate(
-        [
-            jnp.zeros((4, d), WIDE),
-            out_sum[:1],
-            jnp.pad(qkv_sums[:1], ((0, 0), (0, d - qkv_cols))),
-            jnp.pad(hidden_sums[:1], ((0, 0), (0, d - unit_cols))),
-            jnp.zeros((1, d), WIDE),
-        ],
-        axis=0,
-    )
     sums, input_grad = backward_line(
         qkv_grad,
         hidden_grad,
@@ -1740,24 +1750,35 @@
         cotangent,
         qkv_w,
         up_w,
-        vectors[0:1],
-        vectors[2:3],
-        sums,
-    )
-    block_grad, left_new, right_new, weight_new, block_out, input_grad = shampoo(
+        vectors,
+        cot_sums,
+        qkv_sums,
+        hidden_sums,
+    )
+    (
+        block_grad,
+        left_new,
+        right_new,
+        weight_new,
+        vector_grad,
+        vector_stat_new,
+        vector_new,
+        unit_grad,
+        unit_stat_new,
+        unit_new,
+        block_out,
+        input_grad,
+    ) = shampoo(
         owned,
         weight_blocks[0],
         left_stat[0],
         right_stat[0],
         left_root[0],
         right_root[0],
+        (sums, vectors, vector_stat, unit_bias, unit_stat),
         block_out,
         input_grad,
     )
-    vector_grad = jnp.concatenate([sums[:5], sums[4:5]], axis=0)
-    unit_grad = jnp.concatenate([sums[5, :qkv_cols], sums[6, :unit_cols]])
-    vector_stat_new, vector_new = vector_update(vectors, vector_stat, vector_grad)
-    unit_stat_new, unit_new = vector_update(unit_shift, unit_stat[0], unit_grad)
     return (
         block_out,
         input_grad,
@@ -1768,9 +1789,9 @@
         vector_grad,
         vector_stat_new,
         vector_new,
-        unit_grad[None],
-        unit_stat_new[None],
-        unit_new[None],
+        unit_grad,
+        unit_stat_new,
+        unit_new,
     )
 
 

time: 748 us -> 701 us (0.937)
  Pallas kernels: 702 us -> 677 us
  other arithmetic: 12.2 us -> 0.6 us
  local copies, waits for them, and re-layouts: 9.63 us -> 0.01 us
    pallas_call x1, Pallas kernels: 251 us -> 236 us  [forward_line(): pl.pallas_call(forward_kernel, grid=(FORWARD_GRID,), in_specs=[row_block(...]
    slice x8 -> x0, local copies, waits for them, and re-layouts: 7.69 us -> none  [the longest x2 1.75 us: per_device_line(): unit_grad = jnp.concatenate([sums[5, :qkv_cols], sums[6, :unit_cols]])]
  transfers between devices with their start and end apart: 1 -> 1, of which waited for: 0 -> 0; matrix products, arithmetic and copies ran while one was open for 1% -> 0% of each run, Pallas kernels for 31% -> 33%
where the time goes in v4:
time: 701 us; the launch traced here: 692 us
  Pallas kernels  677 us (97%)
  between operations  14.5 us (2%)
    pallas_call x1, Pallas kernels, forward_line(): pl.pallas_call(forward_kernel, grid=(FORWARD_GRID,), in_specs=[row_block(...  236 us
    pallas_call x1, Pallas kernels, backward_line(): pl.pallas_call(backward_kernel, grid=(BACKWARD_GRID,), in_specs=[row_bloc...  228 us
    pallas_call x1, Pallas kernels, gather_weights(): pl.pallas_call(gather_kernel, in_specs=[smem, smem, smem, vmem, vmem, ANY...  127 us
    pallas_call x1, Pallas kernels, shampoo(): pl.pallas_call(shampoo_kernel, grid=(count // group,), in_specs=[spec] *...  33.3 us
    pallas_call x1, Pallas kernels, unplace_blocks(): pl.pallas_call(unplace_kernel, grid_spec=pltpu.PrefetchScalarGridSpec(num...  19.5 us
    pallas_call x1, Pallas kernels, project_qkv(): pl.pallas_call(functools.partial(qkv_kernel, 1.0 / math.sqrt(HD)), grid=(...  18.7 us
    pallas_call x1, Pallas kernels, attention_forward_rows(): pl.pallas_call(functools.partial(attention_kernel, tile), grid=(rows // t...  14.6 us
  transfers between devices with their start and end apart: 1, of which 0 were waited for; matrix products, arithmetic and copies ran while one was open for 0% of the time, Pallas kernels for 33%

profile of v4, /device:TPU:0, one launch (start us, length us, event | category | flops | bytes accessed | tf_op | source)
XLA Modules:
  0.0 691.8 jit_solution(12065123353430838504)
XLA Ops:
  7.2 0.0 reduce-scatter.2.cloned.1.call-start
  7.2 0.6 maximum_bitcast_fusion.freq_ref
  7.8 126.6 %gather_weights.1 = (bf16[2048,1536]{1,0:T(8,128)(2,1)}, bf16[2560,2048]{1,0:T(8,128)(2,1)}, bf16[2048,2048]{1,0:T(8,128)(2,1)}, bf16[2048,2048]{1,0:T(8,128)(2,...) custom-call(s32[192]{0:T(256)} %order_ref.3, s32[32]{0:T(128)} %len_ref.1, ...), custom_call_target="tpu_custom_call" | custom-call | flops 99999997952 | bytes 83886080 | tf_op jit(solution)/shard_map/gather_weights/pallas_call | solution.py:636
  134.5 18.7 %project_qkv.1 = (bf16[2048,512]{1,0:T(8,128)(2,1)}, bf16[2048,512]{1,0:T(8,128)(2,1)}, bf16[2048,512]{1,0:T(8,128)(2,1)}) custom-call(bf16[2048,2048]{1,0:T(8,128)(2,1)} %get-tuple-element.48.h_ref.h1_hbm, bf16[2048,1536]{1,0:T(8,128)(2,1)} %get-tuple-element.49.w_ref.qkv_ref, f32[1,3584]{1,0:T(1,128)} %unit_ref.1, f32[3,2048,128]{2,1,0:T(8,128)} %get-tuple-element.47.table_ref), custom_call_target="tpu_custom_call" | custom-call | tf_op jit(solution)/shard_map/project_qkv/pallas_call | solution.py:698
  153.2 14.6 %attention_forward.1 = (bf16[2048,512]{1,0:T(8,128)(2,1)}, f32[2048,128]{1,0:T(8,128)}) custom-call(f32[3,2048,128]{2,1,0:T(8,128)} %get-tuple-element.47.table_ref, bf16[2048,512]{1,0:T(8,128)(2,1)} %get-tuple-element.50.q_ref.q_hbm, bf16[2048,512]{1,0:T(8,128)(2,1)} %get-tuple-element.51.k_ref.k_hbm, bf16[2048,512]{1,0:T(8,128)(2,1)} %get-tuple-element.52.v_ref.v_hbm), custom_call_target="tpu_custom_call" | custom-call | flops 6442450944 | bytes 31457280 | tf_op jit(solution)/shard_map/attention_forward/pallas_call | solution.py:758
  167.8 236.0 %forward_line.1 = (bf16[2048,2048]{1,0:T(8,128)(2,1)}, bf16[2048,2048]{1,0:T(8,128)(2,1)}, bf16[2048,1536]{1,0:T(8,128)(2,1)}, bf16[192,256,256]{2,1,0:T(8,128)(...) custom-call(bf16[2048,2048]{1,0:T(8,128)(2,1)} %get-tuple-element.46.h_ref.h2_hbm, bf16[2048,2048]{1,0:T(8,128)(2,1)} %g_ref.3, ...), custom_call_target="tpu_custom_call" | custom-call | flops 199999995904 | bytes 83886080 | tf_op jit(solution)/shard_map/forward_line/pallas_call | solution.py:1331
  403.7 19.5 %unplace_blocks.1 = bf16[192,256,256]{2,1,0:T(8,128)(2,1)} custom-call(s32[192]{0:T(256)} %order_ref.3, bf16[192,256,256]{2,1,0:T(8,128)(2,1)} %get-tuple-element.57.blocks_ref), custom_call_target="tpu_custom_call" | custom-call | tf_op jit(solution)/shard_map/unplace_blocks/pallas_call | solution.py:388
  423.3 0.0 reduce-scatter.2.cloned.1.call-update
  423.3 227.9 %backward_line.1 = (f32[8,2048]{1,0:T(8,128)}, bf16[2048,2048]{1,0:T(8,128)(2,1)}) custom-call(bf16[2048,1536]{1,0:T(8,128)(2,1)} %get-tuple-element.60.qg_ref, bf16[2048,2048]{1,0:T(8,128)(2,1)} %get-tuple-element.61.hg_ref, bf16[2048,2048]{1,0:T(8,128)(2,1)} %x_ref.3, bf16[2048,2048]{1,0:T(8,128)(2,1)} %g_ref.3, ...), custom_call_target="tpu_custom_call" | custom-call | flops 199999995904 | bytes 62914560 | tf_op jit(solution)/shard_map/backward_line/pallas_call | solution.py:1560
  651.2 0.0 reduce-scatter.2.cloned.1.call-done.g_ref
  651.3 33.3 %shampoo.1 = (f32[24,256,256]{2,1,0:T(8,128)}, f32[24,256,256]{2,1,0:T(8,128)}, f32[24,256,256]{2,1,0:T(8,128)}, f32[24,256,256]{2,1,0:T(8,128)}, f32[6,2048]{1,...) custom-call(bf16[24,256,256]{2,1,0:T(8,128)(2,1)} %reduce-scatter.2., ...), custom_call_target="tpu_custom_call" | custom-call | tf_op jit(solution)/shard_map/shampoo/pallas_call | solution.py:1684
  (2 shorter events, 0.0 us)
Async XLA Ops:
  7.2 644.1 %reduce-scatter.2.cloned.1.call-start = ((), (), s32[]{:S(2)}) async-start(), calls=%async_computation.1 | async-start | bytes 28311552 | tf_op jit(solution)/shard_map/reduce_scatter | solution.py:1744
Sparse Core Ops, SparseCore 0:
  423.4 161.2 reduce-scatter.1

commit v5 on v4

--- a/solution.py
+++ b/solution.py
@@ -344,6 +344,7 @@
 ACROSS = 4
 VMEM_BYTES = 60 * 1024 * 1024
 FORWARD_VMEM = 63 * 1024 * 1024
+GATHER_VMEM = 63 * 1024 * 1024
 
 
 def dot(left, right):
@@ -404,6 +405,44 @@
     )(order, blocks)
 
 
+def turn(values, cos, sin, back=False):
+    lanes = lax.broadcasted_iota(jnp.int32, values.shape, 1)
+    lower, upper = pltpu.roll(values, 96, 1), pltpu.roll(values, 32, 1)
+    other = jnp.where(lanes < 32, -lower, upper)
+    return values * cos - other * sin if back else values * cos + other * sin
+
+
+def attention_rows(c, tile, first, q_ref, k_ref, v_ref, s_scr, ctx_ref, stats_ref):
+    here = slice(c * tile, (c + 1) * tile)
+    lanes = lax.broadcasted_iota(jnp.int32, (tile, 128), 1)
+    stats = jnp.broadcast_to(first.astype(WIDE), (tile, 128))
+    for h in range(q_ref.shape[1] // HD):
+        cols = slice(h * HD, (h + 1) * HD)
+        q = q_ref[here, cols]
+        top = jnp.full((tile, 1), masked_score, WIDE)
+        for j in range(c + 1):
+            keys = slice(j * tile, (j + 1) * tile)
+            s = dot_nt(q, k_ref[keys, cols])
+            col = lax.broadcasted_iota(jnp.int32, (tile, tile), 1) + j * tile
+            ok = col >= first
+            if j == c:
+                row = lax.broadcasted_iota(jnp.int32, (tile, tile), 0) + c * tile
+                ok = ok & (col <= row)
+            s = jnp.where(ok, s, masked_score)
+            s_scr[:, keys] = s
+            top = jnp.maximum(top, jnp.max(s, axis=1, keepdims=True))
+        total = jnp.zeros((tile, 1), WIDE)
+        ctx = jnp.zeros((tile, HD), WIDE)
+        for j in range(c + 1):
+            keys = slice(j * tile, (j + 1) * tile)
+            e = jnp.exp(s_scr[:, keys] - top)
+            total = total + jnp.sum(e, axis=1, keepdims=True)
+            ctx = ctx + dot(e.astype(LOW), v_ref[keys, cols])
+        ctx_ref[:, cols] = (ctx * (1.0 / total)).astype(LOW)
+        stats = jnp.where(lanes == h, top + jnp.log(total), stats)
+    stats_ref[...] = stats
+
+
 PIECES = 4
 ROUTES = ((0, 2), (0, 4), (0, 1), (2, 4), (4, 2), (2, 1), (4, 1), (6, 1))
 
@@ -435,6 +474,7 @@
     place_ref,
     vec_ref,
     freq_ref,
+    bias_ref,
     w_hbm,
     x_hbm,
     cot_hbm,
@@ -444,20 +484,34 @@
     h1_hbm,
     h2_hbm,
     table_hbm,
+    q_hbm,
+    k_hbm,
+    v_hbm,
+    ctx_hbm,
+    stats_hbm,
     sum_ref,
     slots,
     wide,
     x_buf,
     c_buf,
     h_buf,
-    table_buf,
+    table_all,
     stage,
+    qkv_buf,
+    q_all,
+    k_all,
+    v_all,
+    s_scr,
+    stats_buf,
     send_sem,
     recv_sem,
     load_sem,
     row_sem,
     norm_sem,
     stage_sem,
+    out_sem,
+    row_out_sem,
+    q_sem,
 ):
     me = lax.axis_index("dp")
     each = w_hbm.shape[0]
@@ -503,11 +557,8 @@
 
     def keep(i, slot):
         return (
-            pltpu.make_async_copy(h_buf.at[slot, 0], h1_hbm.at[tile(i), :], norm_sem.at[0, slot]),
-            pltpu.make_async_copy(h_buf.at[slot, 1], h2_hbm.at[tile(i), :], norm_sem.at[1, slot]),
-            pltpu.make_async_copy(
-                table_buf.at[slot], table_hbm.at[:, tile(i), :], norm_sem.at[2, slot]
-            ),
+            pltpu.make_async_copy(h_buf.at[slot], h1_hbm.at[tile(i), :], norm_sem.at[0, slot]),
+            pltpu.make_async_copy(stage.at[slot], h2_hbm.at[tile(i), :], norm_sem.at[1, slot]),
         )
 
     def norm_step(i, slot, first):
@@ -523,8 +574,8 @@
         center = x - jnp.mean(x, axis=1, keepdims=True)
         scale = lax.rsqrt(jnp.mean(center * center, axis=1, keepdims=True) + norm_eps)
         xhat = center * scale
-        h_buf[slot, 0] = (xhat * vec_ref[0:1, :] + vec_ref[1:2, :]).astype(LOW)
-        h_buf[slot, 1] = (xhat * vec_ref[2:3, :] + vec_ref[3:4, :]).astype(LOW)
+        h_buf[slot] = (xhat * vec_ref[0:1, :] + vec_ref[1:2, :]).astype(LOW)
+        stage[slot] = (xhat * vec_ref[2:3, :] + vec_ref[3:4, :]).astype(LOW)
         sum_ref[0:1, :] += jnp.sum(c_buf[slot].astype(WIDE), axis=0, keepdims=True)
         row = lax.broadcasted_iota(jnp.int32, (STEP, 128), 0) + i * STEP
         first = jnp.zeros((STEP, 128), jnp.int32)
@@ -534,9 +585,9 @@
             end = end + jnp.where(mine, len_ref[j], 0)
             first = jnp.where(row >= jnp.where(mine, end, 1 << 30), end, first)
         angle = (row - first).astype(WIDE) * freq_ref[...]
-        table_buf[slot, 0] = jnp.cos(angle)
-        table_buf[slot, 1] = jnp.sin(angle)
-        table_buf[slot, 2] = first.astype(WIDE)
+        table_all[0, tile(i), :] = jnp.cos(angle)
+        table_all[1, tile(i), :] = jnp.sin(angle)
+        table_all[2, tile(i), :] = first.astype(WIDE)
         for copy in keep(i, slot):
             copy.start()
 
@@ -592,30 +643,122 @@
         for q in range(PIECES):
             arrived(source, q)
 
-    for ref, skip, panels, across, block in segments(qkv_hbm, od_hbm, up_hbm):
-
-        def panel(i, slot):
-            return pltpu.make_async_copy(
-                stage.at[slot, :, pl.ds(0, across * B)],
-                ref.at[lane((skip + i) * B), :],
-                stage_sem.at[slot],
+    _, out, up, down = segments(qkv_hbm, od_hbm, up_hbm)
+    qkv_across = qkv_hbm.shape[1] // B
+    whole = [
+        pltpu.make_async_copy(src, dst, out_sem.at[i])
+        for i, (src, dst) in enumerate(
+            (
+                (qkv_buf, qkv_hbm),
+                (table_all, table_hbm),
+                (k_all, k_hbm),
+                (v_all, v_hbm),
             )
-
-        @pl.loop(0, panels // 2)
-        def _(k):
-            for slot in range(2):
-                i = k * 2 + slot
-
-                @pl.when(k > 0)
-                def _():
-                    panel(i, slot).wait()
-
-                for j in range(across):
-                    stage[slot, :, j * B : (j + 1) * B] = slots[order_ref[block + i * across + j]]
-                panel(i, slot).start()
-
+        )
+    ]
+
+    def q_out(i):
+        return pltpu.make_async_copy(
+            q_all.at[tile(i), :], q_hbm.at[tile(i), :], q_sem.at[i]
+        )
+
+    def panel(part, i, slot):
+        ref, skip = part[:2]
+        return pltpu.make_async_copy(
+            stage.at[slot], ref.at[lane((skip + i) * B), :], stage_sem.at[slot]
+        )
+
+    def put(part, i, slot):
+        across, block = part[3:]
+        for j in range(across):
+            stage[slot, :, j * B : (j + 1) * B] = slots[order_ref[block + i * across + j]]
+        panel(part, i, slot).start()
+
+    def fetch_h(i, slot):
+        return pltpu.make_async_copy(h1_hbm.at[tile(i), :], x_buf.at[slot], row_sem.at[0, slot])
+
+    for slot in range(2):
+        fetch_h(slot, slot).start()
+
+    @pl.loop(0, qkv_hbm.shape[0] // B)
+    def _(i):
+        for j in range(qkv_across):
+            qkv_buf[lane(i * B), j * B : (j + 1) * B] = slots[order_ref[i * qkv_across + j]]
+
+    whole[0].start()
+    whole[1].start()
+    for slot in range(2):
+        put(out, slot, slot)
+
+    def project(i, slot):
+        scale = 1.0 / math.sqrt(HD)
+        for j in range(qkv_across):
+            head, part = divmod(j, 3)
+            cols = slice(head * HD, head * HD + HD)
+            proj = dot(x_buf[slot], qkv_buf[:, j * B : (j + 1) * B])
+            proj = proj + bias_ref[:, j * B : (j + 1) * B]
+            if part == 2:
+                v_all[tile(i), cols] = proj.astype(LOW)
+                continue
+            front = turn(proj[:, :128], table_all[0, tile(i), :], table_all[1, tile(i), :])
+            turned = jnp.concatenate([front, proj[:, 128:]], axis=1).astype(LOW)
+            if part == 0:
+                q_all[tile(i), cols] = (turned.astype(WIDE) * scale).astype(LOW)
+            else:
+                k_all[tile(i), cols] = turned
+
+    @pl.loop(0, steps // 2)
+    def _(k):
         for slot in range(2):
-            panel(slot, slot).wait()
+            i = k * 2 + slot
+            fetch_h(i, slot).wait()
+            project(i, slot)
+            q_out(i).start()
+
+            @pl.when(i + 2 < steps)
+            def _():
+                fetch_h(i + 2, slot).start()
+
+            panel(out, 0, 0).wait()
+            put(up, i, 0)
+            panel(out, 0, 1).wait()
+            put(down, i, 1)
+
+    for copy in whole[2:]:
+        copy.start()
+    rows = 512
+
+    @pl.loop(0, steps)
+    def _(i):
+        q_out(i).wait()
+
+
+    def row_out(c):
+        part, slot = pl.ds(c * rows, rows), c % 2
+        return (
+            pltpu.make_async_copy(q_all.at[part, :], ctx_hbm.at[part, :], row_out_sem.at[0, slot]),
+            pltpu.make_async_copy(
+                stats_buf.at[slot], stats_hbm.at[part, :], row_out_sem.at[1, slot]
+            ),
+        )
+
+    count = x_hbm.shape[0] // rows
+    for c in range(count):
+        if c >= 2:
+            for copy in row_out(c - 2):
+                copy.wait()
+        first = table_all[2, c * rows : (c + 1) * rows, :][:, 0:1].astype(jnp.int32)
+        place = q_all.at[pl.ds(c * rows, rows), :]
+        attention_rows(c, rows, first, q_all, k_all, v_all, s_scr, place, stats_buf.at[c % 2])
+        for copy in row_out(c):
+            copy.start()
+    for c in range(count - 2, count):
+        for copy in row_out(c):
+            copy.wait()
+    for slot in range(2):
+        panel(out, 0, slot).wait()
+    for copy in whole:
+        copy.wait()
 
     for source, target in ROUTES:
         for q in range(PIECES):
@@ -626,7 +769,9 @@
             send(source, target, q).wait_send()
 
 
-def gather_weights(blocks, order, seq_len, seq_device, tokens, cotangent, vectors, shapes):
+def gather_weights(
+    blocks, order, seq_len, seq_device, tokens, cotangent, vectors, bias, shapes
+):
     rows, d = tokens.shape
     each = blocks.shape[0]
     half = 10000.0 ** (-2.0 * jnp.arange(ROT // 2, dtype=WIDE) / ROT)
@@ -635,140 +780,46 @@
     vmem = pl.BlockSpec(memory_space=pltpu.VMEM)
     return pl.pallas_call(
         gather_kernel,
-        in_specs=[smem, smem, smem, vmem, vmem, ANY, ANY, ANY],
-        out_specs=[ANY] * 6 + [vmem],
+        in_specs=[smem, smem, smem, vmem, vmem, vmem, ANY, ANY, ANY],
+        out_specs=[ANY] * 11 + [vmem],
         out_shape=[jax.ShapeDtypeStruct(s, LOW) for s in shapes]
         + [jax.ShapeDtypeStruct((rows, d), LOW)] * 2
         + [jax.ShapeDtypeStruct((3, rows, 128), WIDE)]
+        + [jax.ShapeDtypeStruct((rows, shapes[0][1] // 3), LOW)] * 4
+        + [jax.ShapeDtypeStruct((rows, 128), WIDE)]
         + [jax.ShapeDtypeStruct((8, d), WIDE)],
         scratch_shapes=[
             pltpu.VMEM((order.shape[0], B, B), LOW),
             pltpu.VMEM((2, each // PIECES, B, B), WIDE),
             pltpu.VMEM((2, STEP, d), LOW),
             pltpu.VMEM((2, STEP, d), LOW),
-            pltpu.VMEM((2, 2, STEP, d), LOW),
-            pltpu.VMEM((2, 3, STEP, 128), WIDE),
+            pltpu.VMEM((2, STEP, d), LOW),
+            pltpu.VMEM((3, rows, 128), WIDE),
             pltpu.VMEM((2, B, d), LOW),
+            pltpu.VMEM(shapes[0], LOW),
+        ]
+        + [pltpu.VMEM((rows, shapes[0][1] // 3), LOW)] * 3
+        + [
+            pltpu.VMEM((512, rows), WIDE),
+            pltpu.VMEM((2, 512, 128), WIDE),
             pltpu.SemaphoreType.DMA((8, PIECES)),
             pltpu.SemaphoreType.DMA((8, PIECES)),
             pltpu.SemaphoreType.DMA((2,)),
             pltpu.SemaphoreType.DMA((2, 2)),
-            pltpu.SemaphoreType.DMA((3, 2)),
+            pltpu.SemaphoreType.DMA((2, 2)),
             pltpu.SemaphoreType.DMA((2,)),
+            pltpu.SemaphoreType.DMA((4,)),
+            pltpu.SemaphoreType.DMA((2, 2)),
+            pltpu.SemaphoreType.DMA((rows // STEP,)),
         ],
         compiler_params=pltpu.CompilerParams(
-            vmem_limit_bytes=VMEM_BYTES, collective_id=3, has_side_effects=True
+            vmem_limit_bytes=GATHER_VMEM, collective_id=3, has_side_effects=True
         ),
         cost_estimate=pl.CostEstimate(
             flops=100_000_000_000, bytes_accessed=80 << 20, transcendentals=0
         ),
         name="gather_weights",
-    )(order, seq_len, seq_device, vectors, frequency, blocks, tokens, cotangent)
-
-
-def turn(values, cos, sin, back=False):
-    lanes = lax.broadcasted_iota(jnp.int32, values.shape, 1)
-    lower, upper = pltpu.roll(values, 96, 1), pltpu.roll(values, 32, 1)
-    other = jnp.where(lanes < 32, -lower, upper)
-    return values * cos - other * sin if back else values * cos + other * sin
-
-
-def qkv_kernel(scale, h_ref, w_ref, bias_ref, table_ref, q_ref, k_ref, v_ref):
-    for j in range(w_ref.shape[1] // HD):
-        head, part = divmod(j, 3)
-        cols = slice(head * HD, head * HD + HD)
-        proj = dot(h_ref[...], w_ref[:, j * HD : (j + 1) * HD]) + bias_ref[:, j * HD : (j + 1) * HD]
-        if part == 2:
-            v_ref[:, cols] = proj.astype(LOW)
-            continue
-        front = turn(proj[:, :128], table_ref[0], table_ref[1])
-        turned = jnp.concatenate([front, proj[:, 128:]], axis=1).astype(LOW)
-        if part == 0:
-            q_ref[:, cols] = (turned.astype(WIDE) * scale).astype(LOW)
-        else:
-            k_ref[:, cols] = turned
-
-
-def project_qkv(h1, qkv_w, bias, table):
-    rows, d = h1.shape
-    cols = qkv_w.shape[1]
-    out_cols = cols // 3
-    tile = 512
-    row_spec = lambda width: pl.BlockSpec((tile, width), lambda i: (i, 0))
-    return pl.pallas_call(
-        functools.partial(qkv_kernel, 1.0 / math.sqrt(HD)),
-        grid=(rows // tile,),
-        in_specs=[
-            row_spec(d),
-            resident((d, cols)),
-            resident(bias.shape),
-            pl.BlockSpec((3, tile, 128), lambda i: (0, i, 0)),
-        ],
-        out_specs=[row_spec(out_cols)] * 3,
-        out_shape=[jax.ShapeDtypeStruct((rows, out_cols), LOW)] * 3,
-        compiler_params=pltpu.CompilerParams(vmem_limit_bytes=VMEM_BYTES),
-        name="project_qkv",
-    )(h1, qkv_w, bias, table)
-
-
-def attention_kernel(tile, table_ref, q_ref, k_ref, v_ref, ctx_ref, stats_ref, s_scr):
-    step = pl.program_id(0)
-    heads = q_ref.shape[1] // HD
-    lanes = lax.broadcasted_iota(jnp.int32, (tile, 128), 1)
-
-    def rows(c):
-        first = table_ref[0][:, 0:1].astype(jnp.int32)
-        stats = jnp.broadcast_to(first.astype(WIDE), (tile, 128))
-        for h in range(heads):
-            cols = slice(h * HD, (h + 1) * HD)
-            q = q_ref[:, cols]
-            top = jnp.full((tile, 1), masked_score, WIDE)
-            for j in range(c + 1):
-                keys = slice(j * tile, (j + 1) * tile)
-                s = dot_nt(q, k_ref[keys, cols])
-                col = lax.broadcasted_iota(jnp.int32, (tile, tile), 1) + j * tile
-                ok = col >= first
-                if j == c:
-                    row = lax.broadcasted_iota(jnp.int32, (tile, tile), 0) + c * tile
-                    ok = ok & (col <= row)
-                s = jnp.where(ok, s, masked_score)
-                s_scr[h, :, keys] = s
-                top = jnp.maximum(top, jnp.max(s, axis=1, keepdims=True))
-            total = jnp.zeros((tile, 1), WIDE)
-            ctx = jnp.zeros((tile, HD), WIDE)
-            for j in range(c + 1):
-                keys = slice(j * tile, (j + 1) * tile)
-                e = jnp.exp(s_scr[h, :, keys] - top)
-                total = total + jnp.sum(e, axis=1, keepdims=True)
-                ctx = ctx + dot(e.astype(LOW), v_ref[keys, cols])
-            ctx_ref[:, cols] = (ctx * (1.0 / total)).astype(LOW)
-            stats = jnp.where(lanes == h, top + jnp.log(total), stats)
-        stats_ref[...] = stats
-
-    for c in range(k_ref.shape[0] // tile):
-        pl.when(step == c)(functools.partial(rows, c))
-
-
-def attention_forward_rows(table, q, k, v):
-    rows, cols = q.shape
-    tile = 512
-    tile_spec = pl.BlockSpec((tile, cols), lambda i: (i, 0))
-    full_spec = resident((rows, cols))
-    flops = rows * rows * cols * 3
-    return pl.pallas_call(
-        functools.partial(attention_kernel, tile),
-        grid=(rows // tile,),
-        in_specs=[pl.BlockSpec((1, tile, 128), lambda i: (2, i, 0)), tile_spec, full_spec, full_spec],
-        out_specs=[tile_spec, pl.BlockSpec((tile, 128), lambda i: (i, 0))],
-        out_shape=[
-            jax.ShapeDtypeStruct((rows, cols), LOW),
-            jax.ShapeDtypeStruct((rows, 128), WIDE),
-        ],
-        scratch_shapes=[pltpu.VMEM((cols // HD, tile, rows), WIDE)],
-        compiler_params=pltpu.CompilerParams(vmem_limit_bytes=VMEM_BYTES),
-        cost_estimate=pl.CostEstimate(flops=flops, bytes_accessed=30 << 20, transcendentals=0),
-        name="attention_forward",
-    )(table, q, k, v)
+    )(order, seq_len, seq_device, vectors, frequency, bias, blocks, tokens, cotangent)
 
 
 class Line:
@@ -1470,14 +1521,17 @@
     hg_ref,
     x_ref,
     g_ref,
-    qkv_ref,
-    up_ref,
     vec_ref,
     cot_sums,
     qkv_sums,
     hidden_sums,
+    qkv_hbm,
+    up_hbm,
     sums_ref,
     out_ref,
+    qkv_ref,
+    up_ref,
+    load_sem,
     gc_scr,
     xhat_scr,
     own,
@@ -1495,8 +1549,22 @@
     d = x_ref.shape[1]
     width = 512
 
+    def load(n):
+        part_rows = pl.ds(n * width, width)
+        return (
+            pltpu.make_async_copy(
+                qkv_hbm.at[part_rows, :], qkv_ref.at[part_rows, :], load_sem.at[0, n]
+            ),
+            pltpu.make_async_copy(
+                up_hbm.at[part_rows, :], up_ref.at[part_rows, :], load_sem.at[1, n]
+            ),
+        )
+
     @pl.when(step == 0)
     def _():
+        for n in range(d // width):
+            for copy in load(n):
+                copy.start()
         spread.greet()
         own[...] = jnp.zeros_like(own)
         own[4:5, :] = cot_sums[0:1, :]
@@ -1513,6 +1581,12 @@
         slope = jnp.zeros((STEP, 1), WIDE)
         for n in range(d // width):
             cols = slice(n * width, (n + 1) * width)
+
+            @pl.when(step == 0)
+            def _():
+                for copy in load(n):
+                    copy.wait()
+
             e1 = dot_nt(qg_ref[...], qkv_ref[cols, :])
             e2 = dot_nt(hg_ref[...], up_ref[cols, :])
             xhat = xhat_scr[:, cols]
@@ -1565,14 +1639,16 @@
             row_block(hidden_grad.shape[1]),
             row_block(d),
             base_block(d, BACKWARD_LAG),
-            resident(qkv_w.shape),
-            resident(up_w.shape),
             resident(vectors.shape),
         ]
-        + [resident(part.shape) for part in sums],
+        + [resident(part.shape) for part in sums]
+        + [ANY] * 2,
         out_specs=[pl.BlockSpec(small, lambda i: (0, 0)), ANY],
         out_shape=[jax.ShapeDtypeStruct(small, WIDE), jax.ShapeDtypeStruct((rows, d), LOW)],
         scratch_shapes=[
+            pltpu.VMEM(qkv_w.shape, LOW),
+            pltpu.VMEM(up_w.shape, LOW),
+            pltpu.SemaphoreType.DMA((2, d // 512)),
             pltpu.VMEM((STEP, d), WIDE),
             pltpu.VMEM((STEP, d), WIDE),
             pltpu.VMEM(small, WIDE),
@@ -1589,7 +1665,7 @@
         ),
         name="backward_line",
     )(
-        qkv_grad, hidden_grad, tokens, cotangent, qkv_w, up_w, vectors, *sums
+        qkv_grad, hidden_grad, tokens, cotangent, vectors, *sums, qkv_w, up_w
     )
 
 
@@ -1721,11 +1797,30 @@
     head_cols = d // groups
     unit_cols = FF // groups
     shapes = ((d, qkv_cols), (head_cols + unit_cols, d), (d, unit_cols))
-    qkv_w, od_w, up_w, normed_one, normed_two, table, cot_sums = gather_weights(
-        weight_blocks[0], owner_map, seq_len, seq_device, tokens, cotangent, vectors, shapes
-    )
-    q, k, v = project_qkv(normed_one, qkv_w, unit_bias, table)
-    ctx, stats = attention_forward_rows(table, q, k, v)
+    (
+        qkv_w,
+        od_w,
+        up_w,
+        normed_one,
+        normed_two,
+        table,
+        q,
+        k,
+        v,
+        ctx,
+        stats,
+        cot_sums,
+    ) = gather_weights(
+        weight_blocks[0],
+        owner_map,
+        seq_len,
+        seq_device,
+        tokens,
+        cotangent,
+        vectors,
+        unit_bias,
+        shapes,
+    )
     block_out, hidden_grad, qkv_grad, weight_grads, hidden_sums, qkv_sums = forward_line(
         normed_one,
         normed_two,

time: 701 us -> 680 us (0.970)
  Pallas kernels: 677 us -> 656 us
    pallas_call x3 -> x1, Pallas kernels: 160 us -> 144 us  [gather_weights(): pl.pallas_call(gather_kernel, in_specs=[smem, smem, smem, vmem, vmem, vme...]
where the time goes in v5:
time: 680 us; the launch traced here: 671 us
  Pallas kernels  656 us (96%)
  between operations  14.5 us (2%)
    pallas_call x1, Pallas kernels, forward_line(): pl.pallas_call(forward_kernel, grid=(FORWARD_GRID,), in_specs=[row_block(...  236 us
    pallas_call x1, Pallas kernels, backward_line(): pl.pallas_call(backward_kernel, grid=(BACKWARD_GRID,), in_specs=[row_bloc...  223 us
    pallas_call x1, Pallas kernels, gather_weights(): pl.pallas_call(gather_kernel, in_specs=[smem, smem, smem, vmem, vmem, vme...  144 us
    pallas_call x1, Pallas kernels, shampoo(): pl.pallas_call(shampoo_kernel, grid=(count // group,), in_specs=[spec] *...  33.3 us
    pallas_call x1, Pallas kernels, unplace_blocks(): pl.pallas_call(unplace_kernel, grid_spec=pltpu.PrefetchScalarGridSpec(num...  19.5 us
  transfers between devices with their start and end apart: 1, of which 0 were waited for; matrix products, arithmetic and copies ran while one was open for 0% of the time, Pallas kernels for 33%

profile of v5, /device:TPU:0, one launch (start us, length us, event | category | flops | bytes accessed | tf_op | source)
XLA Modules:
  0.0 671.0 jit_solution(14821225370584301877)
XLA Ops:
  7.2 0.0 reduce-scatter.2.cloned.1.call-start
  7.2 0.6 maximum_bitcast_fusion.freq_ref
  7.8 143.8 %gather_weights.1 = (bf16[2048,1536]{1,0:T(8,128)(2,1)}, bf16[2560,2048]{1,0:T(8,128)(2,1)}, bf16[2048,2048]{1,0:T(8,128)(2,1)}, bf16[2048,2048]{1,0:T(8,128)(2,...) custom-call(s32[192]{0:T(256)} %order_ref.3, ...), custom_call_target="tpu_custom_call" | custom-call | flops 99999997952 | bytes 83886080 | tf_op jit(solution)/shard_map/gather_weights/pallas_call | solution.py:781
  151.6 235.9 %forward_line.1 = (bf16[2048,2048]{1,0:T(8,128)(2,1)}, bf16[2048,2048]{1,0:T(8,128)(2,1)}, bf16[2048,1536]{1,0:T(8,128)(2,1)}, bf16[192,256,256]{2,1,0:T(8,128)(...) custom-call(bf16[2048,2048]{1,0:T(8,128)(2,1)} %get-tuple-element.46.h_ref.h2_hbm, bf16[2048,2048]{1,0:T(8,128)(2,1)} %g_ref.3, ...), custom_call_target="tpu_custom_call" | custom-call | flops 199999995904 | bytes 83886080 | tf_op jit(solution)/shard_map/forward_line/pallas_call | solution.py:1382
  387.5 19.5 %unplace_blocks.1 = bf16[192,256,256]{2,1,0:T(8,128)(2,1)} custom-call(s32[192]{0:T(256)} %order_ref.3, bf16[192,256,256]{2,1,0:T(8,128)(2,1)} %get-tuple-element.56.blocks_ref), custom_call_target="tpu_custom_call" | custom-call | tf_op jit(solution)/shard_map/unplace_blocks/pallas_call | solution.py:389
  407.1 0.0 reduce-scatter.2.cloned.1.call-update
  407.1 223.3 %backward_line.1 = (f32[8,2048]{1,0:T(8,128)}, bf16[2048,2048]{1,0:T(8,128)(2,1)}) custom-call(bf16[2048,1536]{1,0:T(8,128)(2,1)} %get-tuple-element.59.qg_ref, bf16[2048,2048]{1,0:T(8,128)(2,1)} %get-tuple-element.60.hg_ref, bf16[2048,2048]{1,0:T(8,128)(2,1)} %x_ref.3, bf16[2048,2048]{1,0:T(8,128)(2,1)} %g_ref.3, f32[6,2048]{1,0:T(8,128)} %vec_ref.7, ...), custom_call_target="tpu_custom_call" | custom-call | flops 199999995904 | bytes 62914560 | tf_op jit(solution)/shard_map/backward_line/pallas_call | solution.py:1634
  630.4 0.0 reduce-scatter.2.cloned.1.call-done.g_ref
  630.4 33.3 %shampoo.1 = (f32[24,256,256]{2,1,0:T(8,128)}, f32[24,256,256]{2,1,0:T(8,128)}, f32[24,256,256]{2,1,0:T(8,128)}, f32[24,256,256]{2,1,0:T(8,128)}, f32[6,2048]{1,...) custom-call(bf16[24,256,256]{2,1,0:T(8,128)(2,1)} %reduce-scatter.2., ...), custom_call_target="tpu_custom_call" | custom-call | tf_op jit(solution)/shard_map/shampoo/pallas_call | solution.py:1760
  (2 shorter events, 0.0 us)
Async XLA Ops:
  7.2 623.2 %reduce-scatter.2.cloned.1.call-start = ((), (), s32[]{:S(2)}) async-start(), calls=%async_computation.1 | async-start | bytes 28311552 | tf_op jit(solution)/shard_map/reduce_scatter | solution.py:1839
Sparse Core Ops, SparseCore 0:
  407.2 160.9 reduce-scatter.1

commit v6 on v5

--- a/solution.py
+++ b/solution.py
@@ -1754,7 +1754,7 @@
 
 def shampoo(grads, weights, left_stat, right_stat, left_root, right_root, small, one, two):
     count = grads.shape[0]
-    group = 2
+    group = 4
     spec = pl.BlockSpec((group, B, B), lambda i: (i, 0, 0))
     results = [small[1]] * 3 + [small[3]] * 3
     return pl.pallas_call(

time: 680 us -> 678 us (level)
  no operation moved by 1% of the time
where the time goes in v6:
time: 678 us; the launch traced here: 668 us
  Pallas kernels  653 us (96%)
  between operations  14.5 us (2%)
    pallas_call x1, Pallas kernels, forward_line(): pl.pallas_call(forward_kernel, grid=(FORWARD_GRID,), in_specs=[row_block(...  236 us
    pallas_call x1, Pallas kernels, backward_line(): pl.pallas_call(backward_kernel, grid=(BACKWARD_GRID,), in_specs=[row_bloc...  223 us
    pallas_call x1, Pallas kernels, gather_weights(): pl.pallas_call(gather_kernel, in_specs=[smem, smem, smem, vmem, vmem, vme...  144 us
    pallas_call x1, Pallas kernels, shampoo(): pl.pallas_call(shampoo_kernel, grid=(count // group,), in_specs=[spec] *...  30.6 us
    pallas_call x1, Pallas kernels, unplace_blocks(): pl.pallas_call(unplace_kernel, grid_spec=pltpu.PrefetchScalarGridSpec(num...  19.5 us
  transfers between devices with their start and end apart: 1, of which 0 were waited for; matrix products, arithmetic and copies ran while one was open for 0% of the time, Pallas kernels for 33%

profile of v6, /device:TPU:0, one launch (start us, length us, event | category | flops | bytes accessed | tf_op | source)
XLA Modules:
  0.0 668.2 jit_solution(9615500885000313064)
XLA Ops:
  7.2 0.0 reduce-scatter.2.cloned.1.call-start
  7.2 0.6 maximum_bitcast_fusion.freq_ref
  7.8 143.8 %gather_weights.1 = (bf16[2048,1536]{1,0:T(8,128)(2,1)}, bf16[2560,2048]{1,0:T(8,128)(2,1)}, bf16[2048,2048]{1,0:T(8,128)(2,1)}, bf16[2048,2048]{1,0:T(8,128)(2,...) custom-call(s32[192]{0:T(256)} %order_ref.3, ...), custom_call_target="tpu_custom_call" | custom-call | flops 99999997952 | bytes 83886080 | tf_op jit(solution)/shard_map/gather_weights/pallas_call | solution.py:781
  151.6 235.9 %forward_line.1 = (bf16[2048,2048]{1,0:T(8,128)(2,1)}, bf16[2048,2048]{1,0:T(8,128)(2,1)}, bf16[2048,1536]{1,0:T(8,128)(2,1)}, bf16[192,256,256]{2,1,0:T(8,128)(...) custom-call(bf16[2048,2048]{1,0:T(8,128)(2,1)} %get-tuple-element.46.h_ref.h2_hbm, bf16[2048,2048]{1,0:T(8,128)(2,1)} %g_ref.3, ...), custom_call_target="tpu_custom_call" | custom-call | flops 199999995904 | bytes 83886080 | tf_op jit(solution)/shard_map/forward_line/pallas_call | solution.py:1382
  387.5 19.5 %unplace_blocks.1 = bf16[192,256,256]{2,1,0:T(8,128)(2,1)} custom-call(s32[192]{0:T(256)} %order_ref.3, bf16[192,256,256]{2,1,0:T(8,128)(2,1)} %get-tuple-element.56.blocks_ref), custom_call_target="tpu_custom_call" | custom-call | tf_op jit(solution)/shard_map/unplace_blocks/pallas_call | solution.py:389
  407.0 0.0 reduce-scatter.2.cloned.1.call-update
  407.1 223.3 %backward_line.1 = (f32[8,2048]{1,0:T(8,128)}, bf16[2048,2048]{1,0:T(8,128)(2,1)}) custom-call(bf16[2048,1536]{1,0:T(8,128)(2,1)} %get-tuple-element.59.qg_ref, bf16[2048,2048]{1,0:T(8,128)(2,1)} %get-tuple-element.60.hg_ref, bf16[2048,2048]{1,0:T(8,128)(2,1)} %x_ref.3, bf16[2048,2048]{1,0:T(8,128)(2,1)} %g_ref.3, f32[6,2048]{1,0:T(8,128)} %vec_ref.7, ...), custom_call_target="tpu_custom_call" | custom-call | flops 199999995904 | bytes 62914560 | tf_op jit(solution)/shard_map/backward_line/pallas_call | solution.py:1634
  630.4 0.0 reduce-scatter.2.cloned.1.call-done.g_ref
  630.4 30.6 %shampoo.1 = (f32[24,256,256]{2,1,0:T(8,128)}, f32[24,256,256]{2,1,0:T(8,128)}, f32[24,256,256]{2,1,0:T(8,128)}, f32[24,256,256]{2,1,0:T(8,128)}, f32[6,2048]{1,...) custom-call(bf16[24,256,256]{2,1,0:T(8,128)(2,1)} %reduce-scatter.2., ...), custom_call_target="tpu_custom_call" | custom-call | tf_op jit(solution)/shard_map/shampoo/pallas_call | solution.py:1760
  (2 shorter events, 0.0 us)
Async XLA Ops:
  7.2 623.2 %reduce-scatter.2.cloned.1.call-start = ((), (), s32[]{:S(2)}) async-start(), calls=%async_computation.1 | async-start | bytes 28311552 | tf_op jit(solution)/shard_map/reduce_scatter | solution.py:1839
Sparse Core Ops, SparseCore 0:
  407.2 160.9 reduce-scatter.1

commit v7 on v6

--- a/solution.py
+++ b/solution.py
@@ -1258,7 +1258,7 @@
         def _(i):
             store_hg(i).wait()
 
-    def head_grads(h, start, stop):
+    def head_grads(h, second):
         tile = 512
         count = rows // tile
 
@@ -1273,8 +1273,9 @@
             front = turn(values[:, :128], table_ref[0, tile_rows(i), :], table_ref[1, tile_rows(i), :], True)
             return jnp.concatenate([front, values[:, 128:]], axis=1)
 
-        @pl.loop(start, stop)
-        def _(j):
+        @pl.loop(0, 2)
+        def _(turn_index):
+            j = second + turn_index * (3 - 2 * second)
             keys = act_all[tile_rows(j), HD : 2 * HD]
             values = act_all[tile_rows(j), 2 * HD : 3 * HD]
             dk_scr[...] = jnp.zeros_like(dk_scr)
@@ -1300,7 +1301,7 @@
             put(j, 1, turned_back(j, dk_scr[...]))
             put(j, 2, dv_scr[...])
 
-        @pl.when(stop == count)
+        @pl.when(second == 1)
         def _():
             @pl.loop(0, count)
             def _(i):
@@ -1315,7 +1316,7 @@
     @pl.when((step >= 12) & (step < 16))
     def _():
         second = (step - 12) % 2
-        head_grads((step - 12) // 2, second, 1 + 3 * second)
+        head_grads((step - 12) // 2, second)
 
     @pl.when(step == 13)
     def _():

time: 678 us -> 678 us (level)
  no operation moved by 1% of the time
where the time goes in v7:
time: 678 us; the launch traced here: 669 us
  Pallas kernels  654 us (96%)
  between operations  14.5 us (2%)
    pallas_call x1, Pallas kernels, forward_line(): pl.pallas_call(forward_kernel, grid=(FORWARD_GRID,), in_specs=[row_block(...  236 us
    pallas_call x1, Pallas kernels, backward_line(): pl.pallas_call(backward_kernel, grid=(BACKWARD_GRID,), in_specs=[row_bloc...  224 us
    pallas_call x1, Pallas kernels, gather_weights(): pl.pallas_call(gather_kernel, in_specs=[smem, smem, smem, vmem, vmem, vme...  144 us
    pallas_call x1, Pallas kernels, shampoo(): pl.pallas_call(shampoo_kernel, grid=(count // group,), in_specs=[spec] *...  30.6 us
    pallas_call x1, Pallas kernels, unplace_blocks(): pl.pallas_call(unplace_kernel, grid_spec=pltpu.PrefetchScalarGridSpec(num...  19.6 us
  transfers between devices with their start and end apart: 1, of which 0 were waited for; matrix products, arithmetic and copies ran while one was open for 0% of the time, Pallas kernels for 33%

profile of v7, /device:TPU:0, one launch (start us, length us, event | category | flops | bytes accessed | tf_op | source)
XLA Modules:
  0.0 668.9 jit_solution(9785584848588220332)
XLA Ops:
  7.2 0.0 reduce-scatter.2.cloned.1.call-start
  7.2 0.6 maximum_bitcast_fusion.freq_ref
  7.8 143.8 %gather_weights.1 = (bf16[2048,1536]{1,0:T(8,128)(2,1)}, bf16[2560,2048]{1,0:T(8,128)(2,1)}, bf16[2048,2048]{1,0:T(8,128)(2,1)}, bf16[2048,2048]{1,0:T(8,128)(2,...) custom-call(s32[192]{0:T(256)} %order_ref.3, ...), custom_call_target="tpu_custom_call" | custom-call | flops 99999997952 | bytes 83886080 | tf_op jit(solution)/shard_map/gather_weights/pallas_call | solution.py:781
  151.6 235.9 %forward_line.1 = (bf16[2048,2048]{1,0:T(8,128)(2,1)}, bf16[2048,2048]{1,0:T(8,128)(2,1)}, bf16[2048,1536]{1,0:T(8,128)(2,1)}, bf16[192,256,256]{2,1,0:T(8,128)(...) custom-call(bf16[2048,2048]{1,0:T(8,128)(2,1)} %get-tuple-element.46.h_ref.h2_hbm, bf16[2048,2048]{1,0:T(8,128)(2,1)} %g_ref.3, ...), custom_call_target="tpu_custom_call" | custom-call | flops 199999995904 | bytes 83886080 | tf_op jit(solution)/shard_map/forward_line/pallas_call | solution.py:1383
  387.5 19.6 %unplace_blocks.1 = bf16[192,256,256]{2,1,0:T(8,128)(2,1)} custom-call(s32[192]{0:T(256)} %order_ref.3, bf16[192,256,256]{2,1,0:T(8,128)(2,1)} %get-tuple-element.56.blocks_ref), custom_call_target="tpu_custom_call" | custom-call | tf_op jit(solution)/shard_map/unplace_blocks/pallas_call | solution.py:389
  407.1 0.0 reduce-scatter.2.cloned.1.call-update
  407.1 224.0 %backward_line.1 = (f32[8,2048]{1,0:T(8,128)}, bf16[2048,2048]{1,0:T(8,128)(2,1)}) custom-call(bf16[2048,1536]{1,0:T(8,128)(2,1)} %get-tuple-element.59.qg_ref, bf16[2048,2048]{1,0:T(8,128)(2,1)} %get-tuple-element.60.hg_ref, bf16[2048,2048]{1,0:T(8,128)(2,1)} %x_ref.3, bf16[2048,2048]{1,0:T(8,128)(2,1)} %g_ref.3, f32[6,2048]{1,0:T(8,128)} %vec_ref.7, ...), custom_call_target="tpu_custom_call" | custom-call | flops 199999995904 | bytes 62914560 | tf_op jit(solution)/shard_map/backward_line/pallas_call | solution.py:1635
  631.1 0.0 reduce-scatter.2.cloned.1.call-done.g_ref
  631.1 30.6 %shampoo.1 = (f32[24,256,256]{2,1,0:T(8,128)}, f32[24,256,256]{2,1,0:T(8,128)}, f32[24,256,256]{2,1,0:T(8,128)}, f32[24,256,256]{2,1,0:T(8,128)}, f32[6,2048]{1,...) custom-call(bf16[24,256,256]{2,1,0:T(8,128)(2,1)} %reduce-scatter.2., ...), custom_call_target="tpu_custom_call" | custom-call | tf_op jit(solution)/shard_map/shampoo/pallas_call | solution.py:1761
  (2 shorter events, 0.0 us)
Async XLA Ops:
  7.2 623.9 %reduce-scatter.2.cloned.1.call-start = ((), (), s32[]{:S(2)}) async-start(), calls=%async_computation.1 | async-start | bytes 28311552 | tf_op jit(solution)/shard_map/reduce_scatter | solution.py:1840
Sparse Core Ops, SparseCore 0:
  407.2 161.8 reduce-scatter.1
